TPU v7x, 32 devices: a whole 2x2x4 slice. The times are simulated.
32 devices in a mesh: rows: 4 (over x, core), cols: 8 (over z, y).
Axes of the slice: x: 2, y: 2, z: 4, core: 2. Of those that a mesh axis runs over, the one named last changes fastest.
Arguments:
- expression: float32 [4096, 1024], P(('rows', 'cols')), may hold values from -10 to 10
- pivots: int32 [512], replicated, may hold values from 0 to 4095
- degrees: int32 [4096], replicated, may hold values from 256 to 8191
Outputs:
- correlation: float32 [4096, 4096], P('rows', 'cols')
All inputs are finite; a program needn't handle non-finite values.
Results may differ from a plain program's by a relative error of at most 0.00042.
Values may be sent and summed in bfloat16 or wider, within the bound.
No kernel may reach another device: no remote copies, remote signals or barrier semaphores. Data moves between devices by JAX's collectives and lax.ppermute only.
A program may use at most 64 MiB of HBM per device.

v0:
```python
import jax
import jax.numpy as jnp
from jax import lax
from jax.sharding import PartitionSpec as P

S = 1024


def standard(expression):
    centered = expression - jnp.mean(expression, axis=1, keepdims=True)
    spread = jnp.mean(centered * centered, axis=1, keepdims=True)
    return (centered * lax.rsqrt(spread + 1e-06)).astype(jnp.bfloat16)


def adjacency(left, right):
    corr = (
        lax.dot_general(left, right, (((1,), (1,)), ((), ())), preferred_element_type=jnp.float32)
        / S
    )
    return ((1.0 + corr) * 0.5) ** 6


def per_device(expression, pivots, degrees):
    n_rows = lax.axis_size("rows")
    n_cols = lax.axis_size("cols")
    row_index = lax.axis_index("rows")
    col_index = lax.axis_index("cols")
    local = expression.shape[0]
    zrows = standard(expression)
    mine = (row_index * n_cols + col_index) * local + jnp.arange(local, dtype=jnp.int32)
    onehot = (pivots[:, None] == mine[None, :]).astype(jnp.bfloat16)
    partial_piv = jnp.dot(onehot, zrows, preferred_element_type=jnp.float32)
    zpiv = lax.psum(partial_piv, ("rows", "cols")).astype(jnp.bfloat16)
    scale = degrees.astype(jnp.float32) * (1.0 / 1024.0)
    kcol = lax.dynamic_index_in_dim(
        scale.reshape(n_rows, n_cols, local), col_index, 1, False
    ).reshape(-1)
    row_total = local * n_cols
    zcol = lax.all_gather(zrows, "rows", axis=0, tiled=True)
    acol = adjacency(zcol, zpiv).astype(jnp.bfloat16)
    piece = lax.all_gather(zrows, "cols", axis=0, tiled=True)
    arow = adjacency(piece, zpiv).astype(jnp.bfloat16)
    width = piece.shape[0]
    kr = lax.dynamic_slice_in_dim(scale, row_index * row_total, width, 0)
    direct = adjacency(piece, zcol)
    shared = lax.dot_general(
        arow, acol, (((1,), (1,)), ((), ())), preferred_element_type=jnp.float32
    )
    denom = jnp.minimum(kr[:, None], kcol[None, :]) + 1.0 - direct
    return (shared + direct) / denom


def solution(mesh):
    in_specs = (P(("rows", "cols"), None), P(), P())
    out_specs = P("rows", "cols")
    return jax.shard_map(
        per_device, mesh=mesh, in_specs=in_specs, out_specs=out_specs, check_vma=False
    )
```

profile of v0, /device:TPU:0, one launch (start us, length us, event | category | flops | bytes accessed | tf_op | source)
XLA Modules:
  0.0 112.4 jit_solution(3831659431422845299)
XLA Ops:
  6.5 0.0 copy-start.1
  6.5 0.0 all-gather.5.cloned.1.call-start
  6.5 1.2 %reduce_sum.18 = f32[128]{0:T(128)S(1)} reduce(f32[128,1024]{1,0:T(8,128)} %param.3, f32[]{:T(128)} %constant.12.clone.1), dimensions={1}, to_apply=%region_0.0 | reduce | flops 130944 | bytes 524804 | tf_op jit(solution)/shard_map/reduce_sum | solution.py:10
  7.7 0.0 copy-start
  7.7 1.2 %multiply_reduce_fusion = f32[128]{0:T(128)S(1)} fusion(f32[128,1024]{1,0:T(8,128)} %param.3, f32[128]{0:T(128)S(1)} %broadcast_multiply_fusion), kind=kLoop, calls=%fused_computation.16 | loop fusion | flops 393088 | bytes 525312 | tf_op jit(solution)/shard_map/reduce_sum | solution.py:11
  9.0 1.9 %multiply_convert_fusion = bf16[128,1024]{1,0:T(8,128)(2,1)} fusion(f32[128,1024]{1,0:T(8,128)} %param.3, f32[128]{0:T(128)S(1)} %add_rsqrt_fusion, f32[128]{0:T(128)S(1)} %broadcast_multiply_fusion), kind=kLoop, calls=%fused_computation.15 | loop fusion | flops 393216 | bytes 787456 | tf_op jit(solution)/shard_map/convert_element_type | solution.py:12
  10.9 0.0 all-gather.5.cloned.1.call-update
  10.9 0.0 all-gather.3.cloned.1.call-start
  10.9 0.7 all-gather.3.cloned.1.call-update
  11.7 0.0 copy-done.1
  11.7 1.4 %fusion.11 = f32[512,1024]{1,0:T(8,128)S(1)} fusion(bf16[128,1024]{1,0:T(8,128)(2,1)} %multiply_convert_fusion, s32[128]{0:T(128)S(1)} %iota_add_fusion, s32[512]{0:T(512)S(1)} %copy-done.1), kind=kOutput, calls=%fused_computation.17 | convolution fusion | flops 134283264 | bytes 2361856 | tf_op jit(solution)/shard_map/dot_general | solution.py:32
  13.1 0.0 copy-done
  13.2 79.4 %all-reduce.1 = bf16[512,1024]{1,0:T(8,128)(2,1)S(1)} all-reduce(f32[512,1024]{1,0:T(8,128)S(1)} %fusion.11), channel_id=1, replica_groups=mesh['rows'=4,'cols'=8] {'rows','cols'}, use_global_device_ids=true, to_apply=%region_2.0 | all-reduce | flops 524288 | bytes 3145728 | tf_op jit(solution)/shard_map/psum | solution.py:33
  92.6 0.0 all-gather.5.cloned.1.call-done
  92.6 2.9 %fusion.4 = bf16[512,512]{1,0:T(8,128)(2,1)} fusion(bf16[512,1024]{1,0:T(8,128)(2,1)} %all-gather.5.cloned.1.call-done, bf16[512,1024]{1,0:T(8,128)(2,1)S(1)} %all-reduce.1), kind=kOutput, calls=%fused_computation.9 | convolution fusion | flops 538705920 | bytes 2621440 | tf_op jit(solution)/shard_map/dot_general | solution.py:17
  95.4 0.0 all-gather.3.cloned.1.call-done
  95.4 0.0 copy-start.2
  95.5 4.6 %fusion.19 = f32[1024,512]{1,0:T(8,128)} fusion(bf16[1024,1024]{1,0:T(8,128)(2,1)} %all-gather.3.cloned.1.call-done, bf16[512,1024]{1,0:T(8,128)(2,1)} %all-gather.5.cloned.1.call-done), kind=kOutput, calls=%fused_computation.30 | convolution fusion | flops 1073741824 | bytes 5242880 | tf_op jit(solution)/shard_map/dot_general | solution.py:17
  100.1 0.0 copy-done.2
  100.1 5.5 %subtract_divide_fusion = f32[1024,512]{1,0:T(8,128)} fusion(f32[1024,512]{1,0:T(8,128)} %fusion.19, bf16[512,512]{1,0:T(8,128)(2,1)} %fusion.4, bf16[1024,1024]{1,0:T(8,128)(2,1)S(1)} %copy-done.2, f32[512]{0:T(512)S(1)} %bitcast.11, f32[1024]{0:T(1024)S(1)} %dynamic_slice.7, bf16[512,1024]{1,0:T(8,128)(2,1)S(1)} %all-reduce.1), kind=kOutput, calls=%fused_computation.3 | convolution fusion | flops 1620049920 | bytes 7870464 | tf_op jit(solution)/shard_map/dot_general | solution.py:46
  (6 shorter events, 0.0 us)
Async XLA Ops:
  6.5 5.1 %copy-start.1 = (s32[512]{0:T(512)S(1)}, s32[512]{0:T(512)}, u32[]{:S(2)}) copy-start(s32[512]{0:T(512)} %param.4) | copy-start | bytes 6148
  6.5 86.0 %all-gather.5.cloned.1.call-start = ((), (), s32[]{:S(2)}) async-start(), calls=%async_computation.1 | async-start | bytes 1310720 | tf_op jit(solution)/shard_map/all_gather | solution.py:39
  7.7 5.4 %copy-start = (s32[4096]{0:T(1024)S(1)}, s32[4096]{0:T(1024)}, u32[]{:S(2)}) copy-start(s32[4096]{0:T(1024)} %param.5) | copy-start | bytes 49156
  10.9 84.6 %all-gather.3.cloned.1.call-start = ((), (), s32[]{:S(2)}) async-start(), calls=%async_computation | async-start | bytes 2359296 | tf_op jit(solution)/shard_map/all_gather | solution.py:41
  95.4 4.6 %copy-start.2 = (bf16[1024,1024]{1,0:T(8,128)(2,1)S(1)}, bf16[1024,1024]{1,0:T(8,128)(2,1)}, u32[]{:S(2)}) copy-start(bf16[1024,1024]{1,0:T(8,128)(2,1)} %all-gather.3.cloned.1.call-done) | copy-start | bytes 6291460
Sparse Core Ops, SparseCore 0:
  11.0 24.5 all-gather.4
  37.7 53.7 all-gather.2
where the time goes:
time: 113 us; the launch traced here: 112 us
  blocking collectives  79.4 us (70%)
  matrix products  14.4 us (13%)
  between operations  13.5 us (12%)
  other arithmetic  4.31 us (4%)
    psum x1, blocking collectives, per_device(): zpiv = lax.psum(partial_piv, ('rows', 'cols')).astype(jnp.bfloat16)  79.4 us
    dot_general x2, matrix products, adjacency(): lax.dot_general(left, right, (((1,), (1,)), ((), ())), preferred_element_...  7.46 us
    dot_general x1, matrix products, per_device(): lax.dot_general(arow, acol, (((1,), (1,)), ((), ())), preferred_element_t...  5.53 us
  transfers between devices with their start and end apart: 2, of which 0 were waited for; matrix products, arithmetic and copies ran while one was open for 4% of the time, Pallas kernels for 0%

commit v1 on v0

v1 whole, which is shorter than its diff:
```python
import functools

import jax
import jax.numpy as jnp
from jax import lax
from jax.experimental import pallas as pl
from jax.experimental.pallas import tpu as pltpu
from jax.sharding import PartitionSpec as P

VMEM = pl.BlockSpec(memory_space=pltpu.VMEM)
SMEM = pl.BlockSpec(memory_space=pltpu.SMEM)
ANY = pl.BlockSpec(memory_space=pl.ANY)
LIMIT = 48 * 1024 * 1024


def params():
    return pltpu.CompilerParams(vmem_limit_bytes=LIMIT)


def dot_t(left, right):
    return lax.dot_general(
        left, right, (((1,), (1,)), ((), ())), preferred_element_type=jnp.float32
    )


def power6(product, samples):
    half = (1.0 + product * (1.0 / samples)) * 0.5
    square = half * half
    return square * square * square


def standard_kernel(x_ref, z_ref, za_ref, zb_ref):
    x = x_ref[...]
    centered = x - jnp.mean(x, axis=1, keepdims=True)
    spread = jnp.mean(centered * centered, axis=1, keepdims=True)
    z = (centered * lax.rsqrt(spread + 1e-06)).astype(jnp.bfloat16)
    z_ref[...] = z
    wa = za_ref.shape[1]
    za_ref[...] = z[:, :wa]
    zb_ref[...] = z[:, wa:]


def select_kernel(n, hot_ref, *refs):
    shards, (mine_ref, theirs_ref) = refs[:n], refs[n:]
    half = mine_ref.shape[0]
    genes = jnp.concatenate([s[...] for s in shards], axis=0)
    for out, at in ((mine_ref, 0), (theirs_ref, half)):
        out[...] = jnp.dot(
            hot_ref[at : at + half, :], genes, preferred_element_type=jnp.float32
        ).astype(jnp.bfloat16)


def final_kernel(n, m, cols_ref, kr_ref, kc_ref, *refs):
    refs = list(refs)
    take = lambda count: [refs.pop(0) for _ in range(count)]
    za, zb, pieces, pa, pb = take(n), take(n), take(m), take(2), take(2)
    out_ref, zr, zc, zp, stage, sems = refs
    local, samples = pieces[0].shape
    wa = za[0].shape[1]
    half = pa[0].shape[0]
    for j in range(n):
        at = pl.ds(pl.multiple_of(cols_ref[j] * local, local), local)
        zr[at, :wa] = za[j][...]
        zr[at, wa:] = zb[j][...]
    for i in range(m):
        at = pl.ds(pl.multiple_of(cols_ref[n + i] * local, local), local)
        zc[at, :] = pieces[i][...]
    for i in range(2):
        zp[i * half : (i + 1) * half, :wa] = pa[i][...]
        zp[i * half : (i + 1) * half, wa:] = pb[i][...]
    acol = power6(dot_t(zc[...], zp[...]), samples).astype(jnp.bfloat16)
    block = 2 * local
    copies = []
    for b in range(n * local // block):
        rows = slice(b * block, (b + 1) * block)
        arow = power6(dot_t(zr[rows, :], zp[...]), samples).astype(jnp.bfloat16)
        direct = power6(dot_t(zr[rows, :], zc[...]), samples)
        shared = dot_t(arow, acol)
        denom = jnp.minimum(kr_ref[rows, :], kc_ref[...]) + 1.0 - direct
        stage[rows, :] = (shared + direct) / denom
        copy = pltpu.make_async_copy(
            stage.at[rows, :], out_ref.at[rows, :], sems.at[b]
        )
        copy.start()
        copies.append(copy)
    for copy in copies:
        copy.wait()


def per_device(expression, pivots, degrees):
    n_rows = lax.axis_size("rows")
    n = lax.axis_size("cols")
    r = lax.axis_index("rows")
    c = lax.axis_index("cols")
    local, samples = expression.shape
    wa = samples // 2
    wb = samples - wa
    bf16 = jnp.bfloat16

    z, za, zb = pl.pallas_call(
        standard_kernel,
        out_shape=[
            jax.ShapeDtypeStruct((local, samples), bf16),
            jax.ShapeDtypeStruct((local, wa), bf16),
            jax.ShapeDtypeStruct((local, wb), bf16),
        ],
        in_specs=[VMEM],
        out_specs=[VMEM] * 3,
        compiler_params=params(),
        name="standardize",
    )(expression)

    order = list(range(0, n, 2)) + list(range(n - 1, 0, -2))
    forward = [(order[k], order[(k + 1) % n]) for k in range(n)]
    backward = [(b, a) for a, b in forward]
    flip = lambda v, mask: lax.ppermute(
        v, "rows", [(i, i ^ mask) for i in range(n_rows)]
    )

    offsets = [0]
    for s in range(1, n // 2 + 1):
        offsets += [-s, s] if s < n // 2 else [s]
    fa, ba, fb, bb = za, za, zb, zb
    list_a, list_b = [za], [zb]
    pieces, masks = [z], [0]
    for s in range(1, n // 2 + 1):
        last = s == n // 2
        fa = lax.ppermute(fa, "cols", forward)
        list_a.append(fa)
        if not last:
            ba = lax.ppermute(ba, "cols", backward)
            list_a.append(ba)
            fb = lax.ppermute(fb, "cols", forward)
            list_b.append(fb)
        bb = lax.ppermute(bb, "cols", backward)
        list_b.append(bb)
        if s == 1:
            mask = n_rows // 2
            while mask:
                pieces += [flip(p, mask) for p in pieces]
                masks += [q ^ mask for q in masks]
                mask //= 2

    place = jnp.where(c % 2 == 0, c // 2, n - 1 - c // 2)
    spots = (place + jnp.array(offsets, jnp.int32)) % n
    columns = jnp.where(spots < n // 2, 2 * spots, 2 * (n - 1 - spots) + 1)
    ids = ((r * n + columns)[:, None] * local + jnp.arange(local, dtype=jnp.int32)).reshape(-1)
    half = pivots.shape[0] // 2
    side = r % 2
    split = pivots.reshape(2, half)
    ordered = jnp.concatenate(
        [
            lax.dynamic_index_in_dim(split, side, 0, False),
            lax.dynamic_index_in_dim(split, 1 - side, 0, False),
        ]
    )
    hot = (ordered[:, None] == ids[None, :]).astype(bf16)

    def pivot_rows(shards):
        width = shards[0].shape[1]
        mine, theirs = pl.pallas_call(
            functools.partial(select_kernel, n),
            out_shape=[jax.ShapeDtypeStruct((half, width), bf16)] * 2,
            in_specs=[VMEM] * (n + 1),
            out_specs=[VMEM] * 2,
            compiler_params=params(),
            name="select",
        )(hot, *shards)
        total = mine + flip(theirs, 1)
        mask = 2
        while mask < n_rows:
            total = total + flip(total, mask)
            mask *= 2
        return total, flip(total, 1)

    pa = pivot_rows(list_a)
    pb = pivot_rows(list_b)

    scale = degrees.astype(jnp.float32) * (1.0 / 1024.0)
    kc = lax.dynamic_index_in_dim(scale.reshape(n_rows, n, local), c, 1, False).reshape(1, -1)
    height = n * local
    kr = lax.dynamic_slice_in_dim(scale, r * height, height, 0).reshape(-1, 1)
    where = jnp.concatenate([columns, jnp.array(masks, jnp.int32) ^ r])
    width = n_rows * local
    return pl.pallas_call(
        functools.partial(final_kernel, n, n_rows),
        out_shape=jax.ShapeDtypeStruct((height, width), jnp.float32),
        in_specs=[SMEM] + [VMEM] * (2 + 2 * n + n_rows + 4),
        out_specs=ANY,
        scratch_shapes=[
            pltpu.VMEM((height, samples), bf16),
            pltpu.VMEM((width, samples), bf16),
            pltpu.VMEM((2 * half, samples), bf16),
            pltpu.VMEM((height, width), jnp.float32),
            pltpu.SemaphoreType.DMA((n // 2,)),
        ],
        compiler_params=params(),
        name="final",
    )(where, kr, kc, *list_a, *list_b, *pieces, *pa, *pb)


def solution(mesh):
    in_specs = (P(("rows", "cols"), None), P(), P())
    out_specs = P("rows", "cols")
    return jax.shard_map(
        per_device, mesh=mesh, in_specs=in_specs, out_specs=out_specs, check_vma=False
    )
```

time: 113 us -> 57.8 us (0.51)
  blocking collectives: 79.4 us -> 0 us
  waiting for transfers between devices: 0.73 us -> 26.9 us
  starting transfers between devices: 0.04 us -> 19.4 us
  matrix products: 14.4 us -> 0 us
  between operations: 13.5 us -> 0.19 us
  Pallas kernels: 0 us -> 7.74 us
  other arithmetic: 4.31 us -> 1.33 us
  local copies, waits for them, and re-layouts: 0.03 us -> 1.99 us
    psum x1 -> x0, blocking collectives: 79.4 us -> none  [per_device(): zpiv = lax.psum(partial_piv, ('rows', 'cols')).astype(jnp.bfloat16)]
    ppermute x0 -> x23, waiting for transfers between devices: none -> 26.9 us  [the longest x9 16.7 us: per_device(): lax.ppermute(v, 'rows', [(i, i ^ mask) for i in range(n_rows)])]
    ppermute x0 -> x23, starting transfers between devices: none -> 19.4 us  [the longest x4 6.56 us: per_device(): bb = lax.ppermute(bb, 'cols', backward)]
    dot_general x4 -> x0, matrix products: 14.4 us -> none  [the longest x2 7.46 us: adjacency(): lax.dot_general(left, right, (((1,), (1,)), ((), ())), preferred_element_...]
    pallas_call x0 -> x4, Pallas kernels: none -> 7.74 us  [the longest x1 6.09 us: per_device(): pl.pallas_call(functools.partial(final_kernel, n, n_rows), out_shape=jax....]
    reduce_sum x2 -> x0, other arithmetic: 2.41 us -> none  [the longest x1 1.24 us: standard(): spread = jnp.mean(centered * centered, axis=1, keepdims=True)]
    convert_element_type x1, other arithmetic: 1.88 us -> 0.23 us  [per_device(): hot = (ordered[:, None] == ids[None, :]).astype(bf16)]
  transfers between devices with their start and end apart: 2 -> 23, of which waited for: 0 -> 11; matrix products, arithmetic and copies ran while one was open for 4% -> 4% of each run, Pallas kernels for 0% -> 2%
where the time goes in v1:
time: 57.8 us; the launch traced here: 57.5 us
  waiting for transfers between devices  26.9 us (47%)
  starting transfers between devices  19.4 us (34%)
  Pallas kernels  7.74 us (13%)
  local copies, waits for them, and re-layouts  1.99 us (3%)
  other arithmetic  1.33 us (2%)
    ppermute x9, waiting for transfers between devices, per_device(): lax.ppermute(v, 'rows', [(i, i ^ mask) for i in range(n_rows)])  16.7 us
    ppermute x4, starting transfers between devices, per_device(): bb = lax.ppermute(bb, 'cols', backward)  6.56 us
    pallas_call x1, Pallas kernels, per_device(): pl.pallas_call(functools.partial(final_kernel, n, n_rows), out_shape=jax....  6.09 us
    ppermute x3, starting transfers between devices, per_device(): ba = lax.ppermute(ba, 'cols', backward)  5.8 us
    ppermute x4, waiting for transfers between devices, per_device(): fa = lax.ppermute(fa, 'cols', forward)  4.98 us
    ppermute x9, starting transfers between devices, per_device(): lax.ppermute(v, 'rows', [(i, i ^ mask) for i in range(n_rows)])  4.51 us
    ppermute x4, waiting for transfers between devices, per_device(): bb = lax.ppermute(bb, 'cols', backward)  2.45 us
    ppermute x3, waiting for transfers between devices, per_device(): ba = lax.ppermute(ba, 'cols', backward)  1.6 us
  transfers between devices with their start and end apart: 23, of which 11 were waited for; matrix products, arithmetic and copies ran while one was open for 4% of the time, Pallas kernels for 2%

profile of v1, /device:TPU:0, one launch (start us, length us, event | category | flops | bytes accessed | tf_op | source)
XLA Modules:
  0.0 57.5 jit_solution(12124131844858900028)
XLA Ops:
  0.0 1.0 %copy-done = f32[128,1024]{1,0:T(8,128)S(1)} copy-done((f32[128,1024]{1,0:T(8,128)S(1)}, f32[128,1024]{1,0:T(8,128)}, u32[]{:S(2)}) %copy-start) | copy-done | bytes 524312
  1.0 0.2 standardize.1
  1.3 3.0 %collective-permute-start.1 = (bf16[128,512]{1,0:T(8,128)(2,1)S(1)}, bf16[128,512]{1,0:T(8,128)(2,1)S(1)}, u32[]{:S(2)}, u32[]{:S(2)}) collective-permute-start(bf16[128,512]{1,0:T(8,128)(2,1)S(1)} %get-tuple-element.12.refs_0_), channel_id=1, source_target_pairs={{2,0},{4,2},{6,4},{7,6},{5,7},{3,5},{1,3},{0,1},{10,8},{12,10},{14... | collective-permute-start | bytes 393224 | tf_op jit(solution)/shard_map/ppermute | solution.py:131
  4.3 0.1 collective-permute-start
  4.4 1.9 %collective-permute-start.8 = (bf16[128,512]{1,0:T(8,128)(2,1)S(1)}, bf16[128,512]{1,0:T(8,128)(2,1)S(1)}, u32[]{:S(2)}, u32[]{:S(2)}) collective-permute-start(bf16[128,512]{1,0:T(8,128)(2,1)S(1)} %get-tuple-element.13.refs_0_.refs_8_), channel_id=1, source_target_pairs={{2,0},{4,2},{6,4},{7,6},{5,7},{3,5},{1,3},{0,1},{10,8},{12,10},{14... | collective-permute-start | bytes 393224 | tf_op jit(solution)/shard_map/ppermute | solution.py:135
  6.3 0.1 collective-permute-start.7
  6.5 0.7 %reshape.33 = s32[2,256]{1,0:T(2,128)S(1)} reshape(s32[512]{0:T(512)} %param.6) | data formatting | bytes 4096 | tf_op jit(solution)/shard_map/reshape | solution.py:150
  7.1 0.7 %add_multiply_fusion = (s32[8]{0:T(128)S(1)}, s32[8]{0:T(128)S(1)}) fusion(s32[]{:T(128)S(6)} %mul.27, s32[8]{0:T(128)} %constant.84.clone, s32[]{:T(128)S(6)} %select_n.45), kind=kLoop, calls=%fused_computation.13 | loop fusion | flops 160 | bytes 104 | tf_op jit(solution)/shard_map/mul | solution.py:147
  7.8 2.8 %collective-permute-done.refs_1_ = bf16[128,512]{1,0:T(8,128)(2,1)S(1)} collective-permute-done((bf16[128,512]{1,0:T(8,128)(2,1)S(1)}, bf16[128,512]{1,0:T(8,128)(2,1)S(1)}, u32[]{:S(2)}, u32[]{:S(2)}) %collective-permute-start) | collective-permute-done | bytes 131104 | tf_op jit(solution)/shard_map/ppermute | solution.py:128
  10.6 0.2 collective-permute-start.2
  10.8 0.0 collective-permute-done.8.refs_2_.refs_10_
  10.8 1.8 %collective-permute-start.10 = (bf16[128,512]{1,0:T(8,128)(2,1)S(1)}, bf16[128,512]{1,0:T(8,128)(2,1)S(1)}, u32[]{:S(2)}, u32[]{:S(2)}) collective-permute-start(bf16[128,512]{1,0:T(8,128)(2,1)S(1)} %collective-permute-done.8.refs_2_.refs_10_), channel_id=1, source_target_pairs={{2,0},{4,2},{6,4},{7,6},{5,7},{3,5},{1,3},{0,1},{10,8},{12,10},{14... | collective-permute-start | bytes 393224 | tf_op jit(solution)/shard_map/ppermute | solution.py:135
  12.7 0.1 add_bitcast_fusion
  12.7 0.0 collective-permute-done.1.refs_2_
  12.7 1.6 %collective-permute-start.3 = (bf16[128,512]{1,0:T(8,128)(2,1)S(1)}, bf16[128,512]{1,0:T(8,128)(2,1)S(1)}, u32[]{:S(2)}, u32[]{:S(2)}) collective-permute-start(bf16[128,512]{1,0:T(8,128)(2,1)S(1)} %collective-permute-done.1.refs_2_), channel_id=1, source_target_pairs={{2,0},{4,2},{6,4},{7,6},{5,7},{3,5},{1,3},{0,1},{10,8},{12,10},{14... | collective-permute-start | bytes 393224 | tf_op jit(solution)/shard_map/ppermute | solution.py:131
  14.3 0.0 collective-permute-done.7.refs_1_.refs_9_
  14.3 0.5 collective-permute-start.9
  14.8 1.4 %collective-permute-done.2.refs_3_ = bf16[128,512]{1,0:T(8,128)(2,1)S(1)} collective-permute-done((bf16[128,512]{1,0:T(8,128)(2,1)S(1)}, bf16[128,512]{1,0:T(8,128)(2,1)S(1)}, u32[]{:S(2)}, u32[]{:S(2)}) %collective-permute-start.2) | collective-permute-done | bytes 131104 | tf_op jit(solution)/shard_map/ppermute | solution.py:128
  16.2 0.4 collective-permute-start.4
  16.6 0.5 collective-permute-done.10.refs_4_.refs_12_
  17.1 1.2 %collective-permute-start.12 = (bf16[128,512]{1,0:T(8,128)(2,1)S(1)}, bf16[128,512]{1,0:T(8,128)(2,1)S(1)}, u32[]{:S(2)}, u32[]{:S(2)}) collective-permute-start(bf16[128,512]{1,0:T(8,128)(2,1)S(1)} %collective-permute-done.10.refs_4_.refs_12_), channel_id=1, source_target_pairs={{2,0},{4,2},{6,4},{7,6},{5,7},{3,5},{1,3},{0,1},{10,8},{12,10},{14... | collective-permute-start | bytes 393224 | tf_op jit(solution)/shard_map/ppermute | solution.py:135
  18.3 1.6 %collective-permute-done.3.refs_4_ = bf16[128,512]{1,0:T(8,128)(2,1)S(1)} collective-permute-done((bf16[128,512]{1,0:T(8,128)(2,1)S(1)}, bf16[128,512]{1,0:T(8,128)(2,1)S(1)}, u32[]{:S(2)}, u32[]{:S(2)}) %collective-permute-start.3) | collective-permute-done | bytes 131104 | tf_op jit(solution)/shard_map/ppermute | solution.py:131
  19.9 1.2 %collective-permute-start.5 = (bf16[128,512]{1,0:T(8,128)(2,1)S(1)}, bf16[128,512]{1,0:T(8,128)(2,1)S(1)}, u32[]{:S(2)}, u32[]{:S(2)}) collective-permute-start(bf16[128,512]{1,0:T(8,128)(2,1)S(1)} %collective-permute-done.3.refs_4_), channel_id=1, source_target_pairs={{2,0},{4,2},{6,4},{7,6},{5,7},{3,5},{1,3},{0,1},{10,8},{12,10},{14... | collective-permute-start | bytes 393224 | tf_op jit(solution)/shard_map/ppermute | solution.py:131
  21.1 0.0 collective-permute-done.9.refs_3_.refs_11_
  21.1 0.8 %collective-permute-start.11 = (bf16[128,512]{1,0:T(8,128)(2,1)S(1)}, bf16[128,512]{1,0:T(8,128)(2,1)S(1)}, u32[]{:S(2)}, u32[]{:S(2)}) collective-permute-start(bf16[128,512]{1,0:T(8,128)(2,1)S(1)} %collective-permute-done.9.refs_3_.refs_11_), channel_id=1, source_target_pairs={{0,2},{2,4},{4,6},{6,7},{7,5},{5,3},{3,1},{1,0},{8,10},{10,12},{12... | collective-permute-start | bytes 393224 | tf_op jit(solution)/shard_map/ppermute | solution.py:133
  21.9 0.7 %collective-permute-done.4.refs_5_ = bf16[128,512]{1,0:T(8,128)(2,1)S(1)} collective-permute-done((bf16[128,512]{1,0:T(8,128)(2,1)S(1)}, bf16[128,512]{1,0:T(8,128)(2,1)S(1)}, u32[]{:S(2)}, u32[]{:S(2)}) %collective-permute-start.4) | collective-permute-done | bytes 131104 | tf_op jit(solution)/shard_map/ppermute | solution.py:128
  22.6 0.4 collective-permute-start.6
  23.1 0.0 collective-permute-done.12.refs_6_.refs_14_
  23.1 1.6 %collective-permute-start.13 = (bf16[128,512]{1,0:T(8,128)(2,1)S(1)}, bf16[128,512]{1,0:T(8,128)(2,1)S(1)}, u32[]{:S(2)}, u32[]{:S(2)}) collective-permute-start(bf16[128,512]{1,0:T(8,128)(2,1)S(1)} %collective-permute-done.12.refs_6_.refs_14_), channel_id=1, source_target_pairs={{2,0},{4,2},{6,4},{7,6},{5,7},{3,5},{1,3},{0,1},{10,8},{12,10},{14... | collective-permute-start | bytes 393224 | tf_op jit(solution)/shard_map/ppermute | solution.py:135
  24.7 0.2 compare_convert_fusion.hot_ref
  24.9 1.1 %collective-permute-done.11.refs_5_.refs_13_ = bf16[128,512]{1,0:T(8,128)(2,1)S(1)} collective-permute-done((bf16[128,512]{1,0:T(8,128)(2,1)S(1)}, bf16[128,512]{1,0:T(8,128)(2,1)S(1)}, u32[]{:S(2)}, u32[]{:S(2)}) %collective-permute-start.11) | collective-permute-done | bytes 131104 | tf_op jit(solution)/shard_map/ppermute | solution.py:133
  26.1 2.0 %collective-permute-done.13.refs_7_.refs_15_ = bf16[128,512]{1,0:T(8,128)(2,1)S(1)} collective-permute-done((bf16[128,512]{1,0:T(8,128)(2,1)S(1)}, bf16[128,512]{1,0:T(8,128)(2,1)S(1)}, u32[]{:S(2)}, u32[]{:S(2)}) %collective-permute-start.13) | collective-permute-done | bytes 131104 | tf_op jit(solution)/shard_map/ppermute | solution.py:135
  28.0 0.7 %select.13 = (bf16[256,512]{1,0:T(8,128)(2,1)S(1)}, bf16[256,512]{1,0:T(8,128)(2,1)S(1)}) custom-call(bf16[512,1024]{1,0:T(8,128)(2,1)S(1)} %compare_convert_fusion.hot_ref, bf16[128,512]{1,0:T(8,128)(2,1)S(1)} %get-tuple-element.13.refs_0_.refs_8_, bf16[128,512]{1,0:T(8,128)(2,1)S(1)} %collective-permute-done.7.refs_1_.refs_9_, ...), custom_call_target="tpu_custom_call" | custom-call | tf_op jit(solution)/shard_map/select/pallas_call | solution.py:161
  28.7 0.0 copy-start.1
  28.7 0.1 collective-permute-start.20
  28.8 0.0 collective-permute-done.5.refs_6_
  28.8 0.0 collective-permute-done.6.refs_7_
  28.8 0.7 %select.12 = (bf16[256,512]{1,0:T(8,128)(2,1)S(1)}, bf16[256,512]{1,0:T(8,128)(2,1)S(1)}) custom-call(bf16[512,1024]{1,0:T(8,128)(2,1)S(1)} %compare_convert_fusion.hot_ref, bf16[128,512]{1,0:T(8,128)(2,1)S(1)} %get-tuple-element.12.refs_0_, bf16[128,512]{1,0:T(8,128)(2,1)S(1)} %collective-permute-done.refs_1_, ...), custom_call_target="tpu_custom_call" | custom-call | tf_op jit(solution)/shard_map/select/pallas_call | solution.py:161
  29.6 0.0 copy-start.2
  29.6 0.5 collective-permute-start.17
  30.1 1.6 %collective-permute-start.14 = (bf16[128,1024]{1,0:T(8,128)(2,1)S(1)}, bf16[128,1024]{1,0:T(8,128)(2,1)}, u32[]{:S(2)}, u32[]{:S(2)}) collective-permute-start(bf16[128,1024]{1,0:T(8,128)(2,1)S(1)} %get-tuple-element.14.refs_16_), channel_id=1, source_target_pairs={{0,16},{8,24},{16,0},{24,8},{1,17},{9,25},{17,1},{25,9},{2,18},{10... | collective-permute-start | bytes 786440 | tf_op jit(solution)/shard_map/ppermute | solution.py:116
  31.7 0.0 collective-permute-done.20
  31.7 0.1 add.94
  31.8 0.5 collective-permute-start.21
  32.3 0.0 collective-permute-done.17
  32.3 0.1 add.92
  32.4 1.7 %collective-permute-start.18 = (bf16[256,512]{1,0:T(8,128)(2,1)S(1)}, bf16[256,512]{1,0:T(8,128)(2,1)S(1)}, u32[]{:S(2)}, u32[]{:S(2)}) collective-permute-start(bf16[256,512]{1,0:T(8,128)(2,1)S(1)} %add.92), channel_id=1, source_target_pairs={{0,16},{8,24},{16,0},{24,8},{1,17},{9,25},{17,1},{25,9},{2,18},{10... | collective-permute-start | bytes 786440 | tf_op jit(solution)/shard_map/ppermute | solution.py:116
  34.0 0.0 collective-permute-start.15
  34.0 0.0 copy-done.1
  34.0 5.4 %collective-permute-done.14.refs_17_ = bf16[128,1024]{1,0:T(8,128)(2,1)} collective-permute-done((bf16[128,1024]{1,0:T(8,128)(2,1)S(1)}, bf16[128,1024]{1,0:T(8,128)(2,1)}, u32[]{:S(2)}, u32[]{:S(2)}) %collective-permute-start.14) | collective-permute-done | bytes 262176 | tf_op jit(solution)/shard_map/ppermute | solution.py:116
  39.4 0.0 collective-permute-start.16
  39.4 5.5 %collective-permute-done.21 = bf16[256,512]{1,0:T(8,128)(2,1)S(1)} collective-permute-done((bf16[256,512]{1,0:T(8,128)(2,1)S(1)}, bf16[256,512]{1,0:T(8,128)(2,1)S(1)}, u32[]{:S(2)}, u32[]{:S(2)}) %collective-permute-start.21) | collective-permute-done | bytes 262176 | tf_op jit(solution)/shard_map/ppermute | solution.py:116
  44.9 0.1 add.95.refs_22_
  45.0 0.1 collective-permute-start.22
  45.0 4.6 %collective-permute-done.18 = bf16[256,512]{1,0:T(8,128)(2,1)S(1)} collective-permute-done((bf16[256,512]{1,0:T(8,128)(2,1)S(1)}, bf16[256,512]{1,0:T(8,128)(2,1)S(1)}, u32[]{:S(2)}, u32[]{:S(2)}) %collective-permute-start.18) | collective-permute-done | bytes 262176 | tf_op jit(solution)/shard_map/ppermute | solution.py:116
  49.6 0.1 add.93.refs_20_
  49.7 0.1 collective-permute-start.19
  49.8 0.2 copy.6.kr_ref
  50.1 0.1 pad_add_fusion.1.cols_ref
  50.1 0.0 collective-permute-done.15.refs_18_
  50.2 0.0 collective-permute-done.16.refs_19_
  50.2 0.0 collective-permute-done.22.refs_23_
  50.2 1.3 %collective-permute-done.19.refs_21_ = bf16[256,512]{1,0:T(8,128)(2,1)} collective-permute-done((bf16[256,512]{1,0:T(8,128)(2,1)S(1)}, bf16[256,512]{1,0:T(8,128)(2,1)}, u32[]{:S(2)}, u32[]{:S(2)}) %collective-permute-start.19) | collective-permute-done | bytes 262176 | tf_op jit(solution)/shard_map/ppermute | solution.py:116
  51.4 6.1 %final.1 = f32[1024,512]{1,0:T(8,128)} custom-call(s32[12]{0:T(128)S(1)} %pad_add_fusion.1.cols_ref, f32[1024,1]{1,0:T(8,128)S(1)} %copy.6.kr_ref, f32[1,512]{1,0:T(1,128)S(1)} %dynamic-slice_bitcast_fusion.kc_ref, bf16[128,512]{1,0:T(8,128)(2,1)S(1)} %get-tuple-element.12.refs_0_, bf16[128,512]{1,0:T(8,128)(2,1)S(1)} %collective-permute-done.refs_1_, ...), custom_call_target="tpu_custom_call" | custom-call | tf_op jit(solution)/shard_map/final/pallas_call | solution.py:185
  (8 shorter events, 0.0 us)
Async XLA Ops:
  0.0 1.0 %copy-start = (f32[128,1024]{1,0:T(8,128)S(1)}, f32[128,1024]{1,0:T(8,128)}, u32[]{:S(2)}) copy-start(f32[128,1024]{1,0:T(8,128)} %x_ref.1) | copy-start | bytes 1572868
  1.3 11.4 %collective-permute-start.1 = (bf16[128,512]{1,0:T(8,128)(2,1)S(1)}, bf16[128,512]{1,0:T(8,128)(2,1)S(1)}, u32[]{:S(2)}, u32[]{:S(2)}) collective-permute-start(bf16[128,512]{1,0:T(8,128)(2,1)S(1)} %get-tuple-element.12.refs_0_), channel_id=1, source_target_pairs={{2,0},{4,2},{6,4},{7,6},{5,7},{3,5},{1,3},{0,1},{10,8},{12,10},{14... | collective-permute-start | bytes 393224 | tf_op jit(solution)/shard_map/ppermute | solution.py:131
  4.3 6.3 %collective-permute-start = (bf16[128,512]{1,0:T(8,128)(2,1)S(1)}, bf16[128,512]{1,0:T(8,128)(2,1)S(1)}, u32[]{:S(2)}, u32[]{:S(2)}) collective-permute-start(bf16[128,512]{1,0:T(8,128)(2,1)S(1)} %get-tuple-element.12.refs_0_), channel_id=1, source_target_pairs={{0,2},{2,4},{4,6},{6,7},{7,5},{5,3},{3,1},{1,0},{8,10},{10,12},{12... | collective-permute-start | bytes 393224 | tf_op jit(solution)/shard_map/ppermute | solution.py:128
  4.4 6.4 %collective-permute-start.8 = (bf16[128,512]{1,0:T(8,128)(2,1)S(1)}, bf16[128,512]{1,0:T(8,128)(2,1)S(1)}, u32[]{:S(2)}, u32[]{:S(2)}) collective-permute-start(bf16[128,512]{1,0:T(8,128)(2,1)S(1)} %get-tuple-element.13.refs_0_.refs_8_), channel_id=1, source_target_pairs={{2,0},{4,2},{6,4},{7,6},{5,7},{3,5},{1,3},{0,1},{10,8},{12,10},{14... | collective-permute-start | bytes 393224 | tf_op jit(solution)/shard_map/ppermute | solution.py:135
  6.3 8.0 %collective-permute-start.7 = (bf16[128,512]{1,0:T(8,128)(2,1)S(1)}, bf16[128,512]{1,0:T(8,128)(2,1)S(1)}, u32[]{:S(2)}, u32[]{:S(2)}) collective-permute-start(bf16[128,512]{1,0:T(8,128)(2,1)S(1)} %get-tuple-element.13.refs_0_.refs_8_), channel_id=1, source_target_pairs={{0,2},{2,4},{4,6},{6,7},{7,5},{5,3},{3,1},{1,0},{8,10},{10,12},{12... | collective-permute-start | bytes 393224 | tf_op jit(solution)/shard_map/ppermute | solution.py:133
  10.6 5.6 %collective-permute-start.2 = (bf16[128,512]{1,0:T(8,128)(2,1)S(1)}, bf16[128,512]{1,0:T(8,128)(2,1)S(1)}, u32[]{:S(2)}, u32[]{:S(2)}) collective-permute-start(bf16[128,512]{1,0:T(8,128)(2,1)S(1)} %collective-permute-done.refs_1_), channel_id=1, source_target_pairs={{0,2},{2,4},{4,6},{6,7},{7,5},{5,3},{3,1},{1,0},{8,10},{10,12},{12... | collective-permute-start | bytes 393224 | tf_op jit(solution)/shard_map/ppermute | solution.py:128
  10.8 6.3 %collective-permute-start.10 = (bf16[128,512]{1,0:T(8,128)(2,1)S(1)}, bf16[128,512]{1,0:T(8,128)(2,1)S(1)}, u32[]{:S(2)}, u32[]{:S(2)}) collective-permute-start(bf16[128,512]{1,0:T(8,128)(2,1)S(1)} %collective-permute-done.8.refs_2_.refs_10_), channel_id=1, source_target_pairs={{2,0},{4,2},{6,4},{7,6},{5,7},{3,5},{1,3},{0,1},{10,8},{12,10},{14... | collective-permute-start | bytes 393224 | tf_op jit(solution)/shard_map/ppermute | solution.py:135
  12.7 7.2 %collective-permute-start.3 = (bf16[128,512]{1,0:T(8,128)(2,1)S(1)}, bf16[128,512]{1,0:T(8,128)(2,1)S(1)}, u32[]{:S(2)}, u32[]{:S(2)}) collective-permute-start(bf16[128,512]{1,0:T(8,128)(2,1)S(1)} %collective-permute-done.1.refs_2_), channel_id=1, source_target_pairs={{2,0},{4,2},{6,4},{7,6},{5,7},{3,5},{1,3},{0,1},{10,8},{12,10},{14... | collective-permute-start | bytes 393224 | tf_op jit(solution)/shard_map/ppermute | solution.py:131
  14.3 6.8 %collective-permute-start.9 = (bf16[128,512]{1,0:T(8,128)(2,1)S(1)}, bf16[128,512]{1,0:T(8,128)(2,1)S(1)}, u32[]{:S(2)}, u32[]{:S(2)}) collective-permute-start(bf16[128,512]{1,0:T(8,128)(2,1)S(1)} %collective-permute-done.7.refs_1_.refs_9_), channel_id=1, source_target_pairs={{0,2},{2,4},{4,6},{6,7},{7,5},{5,3},{3,1},{1,0},{8,10},{10,12},{12... | collective-permute-start | bytes 393224 | tf_op jit(solution)/shard_map/ppermute | solution.py:133
  16.2 6.4 %collective-permute-start.4 = (bf16[128,512]{1,0:T(8,128)(2,1)S(1)}, bf16[128,512]{1,0:T(8,128)(2,1)S(1)}, u32[]{:S(2)}, u32[]{:S(2)}) collective-permute-start(bf16[128,512]{1,0:T(8,128)(2,1)S(1)} %collective-permute-done.2.refs_3_), channel_id=1, source_target_pairs={{0,2},{2,4},{4,6},{6,7},{7,5},{5,3},{3,1},{1,0},{8,10},{10,12},{12... | collective-permute-start | bytes 393224 | tf_op jit(solution)/shard_map/ppermute | solution.py:128
  17.1 6.0 %collective-permute-start.12 = (bf16[128,512]{1,0:T(8,128)(2,1)S(1)}, bf16[128,512]{1,0:T(8,128)(2,1)S(1)}, u32[]{:S(2)}, u32[]{:S(2)}) collective-permute-start(bf16[128,512]{1,0:T(8,128)(2,1)S(1)} %collective-permute-done.10.refs_4_.refs_12_), channel_id=1, source_target_pairs={{2,0},{4,2},{6,4},{7,6},{5,7},{3,5},{1,3},{0,1},{10,8},{12,10},{14... | collective-permute-start | bytes 393224 | tf_op jit(solution)/shard_map/ppermute | solution.py:135
  19.9 8.9 %collective-permute-start.5 = (bf16[128,512]{1,0:T(8,128)(2,1)S(1)}, bf16[128,512]{1,0:T(8,128)(2,1)S(1)}, u32[]{:S(2)}, u32[]{:S(2)}) collective-permute-start(bf16[128,512]{1,0:T(8,128)(2,1)S(1)} %collective-permute-done.3.refs_4_), channel_id=1, source_target_pairs={{2,0},{4,2},{6,4},{7,6},{5,7},{3,5},{1,3},{0,1},{10,8},{12,10},{14... | collective-permute-start | bytes 393224 | tf_op jit(solution)/shard_map/ppermute | solution.py:131
  21.1 5.0 %collective-permute-start.11 = (bf16[128,512]{1,0:T(8,128)(2,1)S(1)}, bf16[128,512]{1,0:T(8,128)(2,1)S(1)}, u32[]{:S(2)}, u32[]{:S(2)}) collective-permute-start(bf16[128,512]{1,0:T(8,128)(2,1)S(1)} %collective-permute-done.9.refs_3_.refs_11_), channel_id=1, source_target_pairs={{0,2},{2,4},{4,6},{6,7},{7,5},{5,3},{3,1},{1,0},{8,10},{10,12},{12... | collective-permute-start | bytes 393224 | tf_op jit(solution)/shard_map/ppermute | solution.py:133
  22.6 6.2 %collective-permute-start.6 = (bf16[128,512]{1,0:T(8,128)(2,1)S(1)}, bf16[128,512]{1,0:T(8,128)(2,1)S(1)}, u32[]{:S(2)}, u32[]{:S(2)}) collective-permute-start(bf16[128,512]{1,0:T(8,128)(2,1)S(1)} %collective-permute-done.4.refs_5_), channel_id=1, source_target_pairs={{0,2},{2,4},{4,6},{6,7},{7,5},{5,3},{3,1},{1,0},{8,10},{10,12},{12... | collective-permute-start | bytes 393224 | tf_op jit(solution)/shard_map/ppermute | solution.py:128
  23.1 5.0 %collective-permute-start.13 = (bf16[128,512]{1,0:T(8,128)(2,1)S(1)}, bf16[128,512]{1,0:T(8,128)(2,1)S(1)}, u32[]{:S(2)}, u32[]{:S(2)}) collective-permute-start(bf16[128,512]{1,0:T(8,128)(2,1)S(1)} %collective-permute-done.12.refs_6_.refs_14_), channel_id=1, source_target_pairs={{2,0},{4,2},{6,4},{7,6},{5,7},{3,5},{1,3},{0,1},{10,8},{12,10},{14... | collective-permute-start | bytes 393224 | tf_op jit(solution)/shard_map/ppermute | solution.py:135
  28.7 5.3 %copy-start.1 = (s32[4096]{0:T(1024)S(1)}, s32[4096]{0:T(1024)}, u32[]{:S(2)}) copy-start(s32[4096]{0:T(1024)} %param.7) | copy-start | bytes 49156
  28.7 3.0 %collective-permute-start.20 = (bf16[256,512]{1,0:T(8,128)(2,1)S(1)}, bf16[256,512]{1,0:T(8,128)(2,1)S(1)}, u32[]{:S(2)}, u32[]{:S(2)}) collective-permute-start(bf16[256,512]{1,0:T(8,128)(2,1)S(1)} %get-tuple-element.18), channel_id=1, source_target_pairs={{0,8},{8,0},{16,24},{24,16},{1,9},{9,1},{17,25},{25,17},{2,10},{10... | collective-permute-start | bytes 786440 | tf_op jit(solution)/shard_map/ppermute | solution.py:116
  29.6 20.2 %copy-start.2 = (s32[4]{0:T(128)S(1)}, s32[4]{0:T(128)}, u32[]{:S(2)}) copy-start(s32[4]{0:T(128)} %constant.85.clone) | copy-start | bytes 52
  29.6 2.7 %collective-permute-start.17 = (bf16[256,512]{1,0:T(8,128)(2,1)S(1)}, bf16[256,512]{1,0:T(8,128)(2,1)S(1)}, u32[]{:S(2)}, u32[]{:S(2)}) collective-permute-start(bf16[256,512]{1,0:T(8,128)(2,1)S(1)} %get-tuple-element.16), channel_id=1, source_target_pairs={{0,8},{8,0},{16,24},{24,16},{1,9},{9,1},{17,25},{25,17},{2,10},{10... | collective-permute-start | bytes 786440 | tf_op jit(solution)/shard_map/ppermute | solution.py:116
  30.1 9.3 %collective-permute-start.14 = (bf16[128,1024]{1,0:T(8,128)(2,1)S(1)}, bf16[128,1024]{1,0:T(8,128)(2,1)}, u32[]{:S(2)}, u32[]{:S(2)}) collective-permute-start(bf16[128,1024]{1,0:T(8,128)(2,1)S(1)} %get-tuple-element.14.refs_16_), channel_id=1, source_target_pairs={{0,16},{8,24},{16,0},{24,8},{1,17},{9,25},{17,1},{25,9},{2,18},{10... | collective-permute-start | bytes 786440 | tf_op jit(solution)/shard_map/ppermute | solution.py:116
  31.8 13.1 %collective-permute-start.21 = (bf16[256,512]{1,0:T(8,128)(2,1)S(1)}, bf16[256,512]{1,0:T(8,128)(2,1)S(1)}, u32[]{:S(2)}, u32[]{:S(2)}) collective-permute-start(bf16[256,512]{1,0:T(8,128)(2,1)S(1)} %add.94), channel_id=1, source_target_pairs={{0,16},{8,24},{16,0},{24,8},{1,17},{9,25},{17,1},{25,9},{2,18},{10... | collective-permute-start | bytes 786440 | tf_op jit(solution)/shard_map/ppermute | solution.py:116
  32.4 17.3 %collective-permute-start.18 = (bf16[256,512]{1,0:T(8,128)(2,1)S(1)}, bf16[256,512]{1,0:T(8,128)(2,1)S(1)}, u32[]{:S(2)}, u32[]{:S(2)}) collective-permute-start(bf16[256,512]{1,0:T(8,128)(2,1)S(1)} %add.92), channel_id=1, source_target_pairs={{0,16},{8,24},{16,0},{24,8},{1,17},{9,25},{17,1},{25,9},{2,18},{10... | collective-permute-start | bytes 786440 | tf_op jit(solution)/shard_map/ppermute | solution.py:116
  34.0 16.1 %collective-permute-start.15 = (bf16[128,1024]{1,0:T(8,128)(2,1)S(1)}, bf16[128,1024]{1,0:T(8,128)(2,1)}, u32[]{:S(2)}, u32[]{:S(2)}) collective-permute-start(bf16[128,1024]{1,0:T(8,128)(2,1)S(1)} %get-tuple-element.14.refs_16_), channel_id=1, source_target_pairs={{0,8},{8,0},{16,24},{24,16},{1,9},{9,1},{17,25},{25,17},{2,10},{10... | collective-permute-start | bytes 786440 | tf_op jit(solution)/shard_map/ppermute | solution.py:116
  39.4 10.8 %collective-permute-start.16 = (bf16[128,1024]{1,0:T(8,128)(2,1)}, bf16[128,1024]{1,0:T(8,128)(2,1)}, u32[]{:S(2)}, u32[]{:S(2)}) collective-permute-start(bf16[128,1024]{1,0:T(8,128)(2,1)} %collective-permute-done.14.refs_17_), channel_id=1, source_target_pairs={{0,8},{8,0},{16,24},{24,16},{1,9},{9,1},{17,25},{25,17},{2,10},{10... | collective-permute-start | bytes 786440 | tf_op jit(solution)/shard_map/ppermute | solution.py:116
  45.0 5.2 %collective-permute-start.22 = (bf16[256,512]{1,0:T(8,128)(2,1)S(1)}, bf16[256,512]{1,0:T(8,128)(2,1)}, u32[]{:S(2)}, u32[]{:S(2)}) collective-permute-start(bf16[256,512]{1,0:T(8,128)(2,1)S(1)} %add.95.refs_22_), channel_id=1, source_target_pairs={{0,8},{8,0},{16,24},{24,16},{1,9},{9,1},{17,25},{25,17},{2,10},{10... | collective-permute-start | bytes 786440 | tf_op jit(solution)/shard_map/ppermute | solution.py:116
  49.7 1.7 %collective-permute-start.19 = (bf16[256,512]{1,0:T(8,128)(2,1)S(1)}, bf16[256,512]{1,0:T(8,128)(2,1)}, u32[]{:S(2)}, u32[]{:S(2)}) collective-permute-start(bf16[256,512]{1,0:T(8,128)(2,1)S(1)} %add.93.refs_20_), channel_id=1, source_target_pairs={{0,8},{8,0},{16,24},{24,16},{1,9},{9,1},{17,25},{25,17},{2,10},{10... | collective-permute-start | bytes 786440 | tf_op jit(solution)/shard_map/ppermute | solution.py:116

commit v2 on v1

--- a/solution.py
+++ b/solution.py
@@ -10,11 +10,14 @@
 VMEM = pl.BlockSpec(memory_space=pltpu.VMEM)
 SMEM = pl.BlockSpec(memory_space=pltpu.SMEM)
 ANY = pl.BlockSpec(memory_space=pl.ANY)
-LIMIT = 48 * 1024 * 1024
-
-
-def params():
-    return pltpu.CompilerParams(vmem_limit_bytes=LIMIT)
+MIB = 1024 * 1024
+
+
+def params(mib):
+    return pltpu.CompilerParams(vmem_limit_bytes=mib * MIB)
+
+
+CHEAP = pl.CostEstimate(flops=1, bytes_accessed=1, transcendentals=0)
 
 
 def dot_t(left, right):
@@ -50,14 +53,13 @@
         ).astype(jnp.bfloat16)
 
 
-def final_kernel(n, m, cols_ref, kr_ref, kc_ref, *refs):
+def direct_kernel(n, m, cols_ref, kr_ref, kc_ref, *refs):
     refs = list(refs)
     take = lambda count: [refs.pop(0) for _ in range(count)]
-    za, zb, pieces, pa, pb = take(n), take(n), take(m), take(2), take(2)
-    out_ref, zr, zc, zp, stage, sems = refs
+    za, zb, pieces = take(n), take(n), take(m)
+    zr, zc, inverse, share = refs
     local, samples = pieces[0].shape
     wa = za[0].shape[1]
-    half = pa[0].shape[0]
     for j in range(n):
         at = pl.ds(pl.multiple_of(cols_ref[j] * local, local), local)
         zr[at, :wa] = za[j][...]
@@ -65,19 +67,35 @@
     for i in range(m):
         at = pl.ds(pl.multiple_of(cols_ref[n + i] * local, local), local)
         zc[at, :] = pieces[i][...]
-    for i in range(2):
-        zp[i * half : (i + 1) * half, :wa] = pa[i][...]
-        zp[i * half : (i + 1) * half, wa:] = pb[i][...]
-    acol = power6(dot_t(zc[...], zp[...]), samples).astype(jnp.bfloat16)
     block = 2 * local
-    copies = []
     for b in range(n * local // block):
         rows = slice(b * block, (b + 1) * block)
-        arow = power6(dot_t(zr[rows, :], zp[...]), samples).astype(jnp.bfloat16)
         direct = power6(dot_t(zr[rows, :], zc[...]), samples)
-        shared = dot_t(arow, acol)
-        denom = jnp.minimum(kr_ref[rows, :], kc_ref[...]) + 1.0 - direct
-        stage[rows, :] = (shared + direct) / denom
+        inv = 1.0 / (jnp.minimum(kr_ref[rows, :], kc_ref[...]) + 1.0 - direct)
+        inverse[rows, :] = inv
+        share[rows, :] = direct * inv
+
+
+def partial_kernel(zr, zc, near, far, row_part, col_part):
+    wa = near.shape[1]
+    zp = jnp.concatenate([near[...], far[...]], axis=0)
+    row_part[...] = dot_t(zr[:, :wa], zp)
+    col_part[...] = dot_t(zc[:, :wa], zp)
+
+
+def final_kernel(zr, zc, near, far, row_part, col_part, inverse, share, out_ref, stage, sems):
+    height, samples = zr.shape
+    wa = samples - near.shape[1]
+    zp = jnp.concatenate([near[...], far[...]], axis=0)
+    acol = power6(col_part[...] + dot_t(zc[:, wa:], zp), samples).astype(jnp.bfloat16)
+    count = sems.shape[0]
+    block = height // count
+    copies = []
+    for b in range(count):
+        rows = slice(b * block, (b + 1) * block)
+        product = row_part[rows, :] + dot_t(zr[rows, wa:], zp)
+        arow = power6(product, samples).astype(jnp.bfloat16)
+        stage[rows, :] = dot_t(arow, acol) * inverse[rows, :] + share[rows, :]
         copy = pltpu.make_async_copy(
             stage.at[rows, :], out_ref.at[rows, :], sems.at[b]
         )
@@ -85,6 +103,22 @@
         copies.append(copy)
     for copy in copies:
         copy.wait()
+
+
+def add_kernel(left, right, out):
+    out[...] = left[...] + right[...]
+
+
+def add(left, right):
+    return pl.pallas_call(
+        add_kernel,
+        out_shape=jax.ShapeDtypeStruct(left.shape, left.dtype),
+        in_specs=[VMEM] * 2,
+        out_specs=VMEM,
+        compiler_params=params(4),
+        cost_estimate=CHEAP,
+        name="add",
+    )(left, right)
 
 
 def per_device(expression, pivots, degrees):
@@ -106,7 +140,7 @@
         ],
         in_specs=[VMEM],
         out_specs=[VMEM] * 3,
-        compiler_params=params(),
+        compiler_params=params(8),
         name="standardize",
     )(expression)
 
@@ -122,9 +156,12 @@
         offsets += [-s, s] if s < n // 2 else [s]
     fa, ba, fb, bb = za, za, zb, zb
     list_a, list_b = [za], [zb]
-    pieces, masks = [z], [0]
+    top = n_rows // 2
+    across = flip(z, top)
     for s in range(1, n // 2 + 1):
         last = s == n // 2
+        if s == n // 2 - 1:
+            fa, across = lax.optimization_barrier((fa, across))
         fa = lax.ppermute(fa, "cols", forward)
         list_a.append(fa)
         if not last:
@@ -134,12 +171,6 @@
             list_b.append(fb)
         bb = lax.ppermute(bb, "cols", backward)
         list_b.append(bb)
-        if s == 1:
-            mask = n_rows // 2
-            while mask:
-                pieces += [flip(p, mask) for p in pieces]
-                masks += [q ^ mask for q in masks]
-                mask //= 2
 
     place = jnp.where(c % 2 == 0, c // 2, n - 1 - c // 2)
     spots = (place + jnp.array(offsets, jnp.int32)) % n
@@ -156,25 +187,38 @@
     )
     hot = (ordered[:, None] == ids[None, :]).astype(bf16)
 
-    def pivot_rows(shards):
+    def pivot_sums(shards):
         width = shards[0].shape[1]
         mine, theirs = pl.pallas_call(
             functools.partial(select_kernel, n),
             out_shape=[jax.ShapeDtypeStruct((half, width), bf16)] * 2,
             in_specs=[VMEM] * (n + 1),
             out_specs=[VMEM] * 2,
-            compiler_params=params(),
+            compiler_params=params(8),
+            cost_estimate=CHEAP,
             name="select",
         )(hot, *shards)
-        total = mine + flip(theirs, 1)
-        mask = 2
+        return add(mine, flip(theirs, 1))
+
+    def spread(total, got):
+        total = add(total, got)
+        mask = 4
         while mask < n_rows:
-            total = total + flip(total, mask)
+            total = add(total, flip(total, mask))
             mask *= 2
         return total, flip(total, 1)
 
-    pa = pivot_rows(list_a)
-    pb = pivot_rows(list_b)
+    sum_a = pivot_sums(list_a)
+    got_a = flip(sum_a, 2)
+    sum_b = pivot_sums(list_b)
+    sum_b, z, across = lax.optimization_barrier((sum_b, z, across))
+    got_b = flip(sum_b, 2)
+    pieces, masks = [z, across], [0, top]
+    mask = top // 2
+    while mask:
+        pieces += [flip(p, mask) for p in pieces]
+        masks += [q ^ mask for q in masks]
+        mask //= 2
 
     scale = degrees.astype(jnp.float32) * (1.0 / 1024.0)
     kc = lax.dynamic_index_in_dim(scale.reshape(n_rows, n, local), c, 1, False).reshape(1, -1)
@@ -182,21 +226,44 @@
     kr = lax.dynamic_slice_in_dim(scale, r * height, height, 0).reshape(-1, 1)
     where = jnp.concatenate([columns, jnp.array(masks, jnp.int32) ^ r])
     width = n_rows * local
+    f32 = jnp.float32
+    shape = jax.ShapeDtypeStruct
+    zr, zc, inverse, share = pl.pallas_call(
+        functools.partial(direct_kernel, n, n_rows),
+        out_shape=[
+            shape((height, samples), bf16),
+            shape((width, samples), bf16),
+            shape((height, width), f32),
+            shape((height, width), f32),
+        ],
+        in_specs=[SMEM] + [VMEM] * (2 + 2 * n + n_rows),
+        out_specs=[VMEM] * 4,
+        compiler_params=params(8),
+        cost_estimate=CHEAP,
+        name="direct",
+    )(where, kr, kc, *list_a, *list_b, *pieces)
+    got_a, got_b, zr, zc, inverse, share = lax.optimization_barrier((got_a, got_b, zr, zc, inverse, share))
+    pa = spread(sum_a, got_a)
+    row_part, col_part = pl.pallas_call(
+        partial_kernel,
+        out_shape=[shape((height, 2 * half), f32), shape((width, 2 * half), f32)],
+        in_specs=[VMEM] * 4,
+        out_specs=[VMEM] * 2,
+        compiler_params=params(8),
+        cost_estimate=CHEAP,
+        name="partial",
+    )(zr, zc, *pa)
+    pb = spread(sum_b, got_b)
     return pl.pallas_call(
-        functools.partial(final_kernel, n, n_rows),
-        out_shape=jax.ShapeDtypeStruct((height, width), jnp.float32),
-        in_specs=[SMEM] + [VMEM] * (2 + 2 * n + n_rows + 4),
+        final_kernel,
+        out_shape=shape((height, width), f32),
+        in_specs=[VMEM] * 8,
         out_specs=ANY,
-        scratch_shapes=[
-            pltpu.VMEM((height, samples), bf16),
-            pltpu.VMEM((width, samples), bf16),
-            pltpu.VMEM((2 * half, samples), bf16),
-            pltpu.VMEM((height, width), jnp.float32),
-            pltpu.SemaphoreType.DMA((n // 2,)),
-        ],
-        compiler_params=params(),
+        scratch_shapes=[pltpu.VMEM((height, width), f32), pltpu.SemaphoreType.DMA((n // 2,))],
+        compiler_params=params(16),
+        cost_estimate=CHEAP,
         name="final",
-    )(where, kr, kc, *list_a, *list_b, *pieces, *pa, *pb)
+    )(zr, zc, *pb, row_part, col_part, inverse, share)
 
 
 def solution(mesh):

time: 57.8 us -> 51.3 us (0.89)
  waiting for transfers between devices: 26.9 us -> 16.1 us
  Pallas kernels: 7.74 us -> 10.8 us
  starting transfers between devices: 19.4 us -> 20.9 us
    ppermute x9, waiting for transfers between devices: 16.7 us -> 8.44 us  [per_device(): lax.ppermute(v, 'rows', [(i, i ^ mask) for i in range(n_rows)])]
    pallas_call x3 -> x9, Pallas kernels: 7.5 us -> 10.5 us  [the longest x1 3.05 us: per_device(): pl.pallas_call(final_kernel, out_shape=shape((height, width), f32), in_sp...]
    ppermute x4, waiting for transfers between devices: 4.98 us -> 2.59 us  [per_device(): fa = lax.ppermute(fa, 'cols', forward)]
    ppermute x4, starting transfers between devices: 1.11 us -> 2.7 us  [per_device(): fa = lax.ppermute(fa, 'cols', forward)]
    ppermute x4, starting transfers between devices: 6.56 us -> 5.48 us  [per_device(): bb = lax.ppermute(bb, 'cols', backward)]
    ppermute x9, starting transfers between devices: 4.51 us -> 5.57 us  [per_device(): lax.ppermute(v, 'rows', [(i, i ^ mask) for i in range(n_rows)])]
  transfers between devices with their start and end apart: 23 -> 23, of which waited for: 11 -> 12; matrix products, arithmetic and copies ran while one was open for 4% -> 4% of each run, Pallas kernels for 2% -> 13%
where the time goes in v2:
time: 51.3 us; the launch traced here: 51 us
  starting transfers between devices  20.9 us (41%)
  waiting for transfers between devices  16.1 us (31%)
  Pallas kernels  10.8 us (21%)
  local copies, waits for them, and re-layouts  1.99 us (4%)
  other arithmetic  1.07 us (2%)
    ppermute x9, waiting for transfers between devices, per_device(): lax.ppermute(v, 'rows', [(i, i ^ mask) for i in range(n_rows)])  8.44 us
    ppermute x3, starting transfers between devices, per_device(): ba = lax.ppermute(ba, 'cols', backward)  5.7 us
    ppermute x9, starting transfers between devices, per_device(): lax.ppermute(v, 'rows', [(i, i ^ mask) for i in range(n_rows)])  5.57 us
    ppermute x4, starting transfers between devices, per_device(): bb = lax.ppermute(bb, 'cols', backward)  5.48 us
    pallas_call x1, Pallas kernels, per_device(): pl.pallas_call(final_kernel, out_shape=shape((height, width), f32), in_sp...  3.05 us
    pallas_call x1, Pallas kernels, per_device(): pl.pallas_call(functools.partial(direct_kernel, n, n_rows), out_shape=[sh...  3.04 us
    ppermute x4, starting transfers between devices, per_device(): fa = lax.ppermute(fa, 'cols', forward)  2.7 us
    ppermute x4, waiting for transfers between devices, per_device(): fa = lax.ppermute(fa, 'cols', forward)  2.59 us
  transfers between devices with their start and end apart: 23, of which 12 were waited for; matrix products, arithmetic and copies ran while one was open for 4% of the time, Pallas kernels for 13%

profile of v2, /device:TPU:0, one launch (start us, length us, event | category | flops | bytes accessed | tf_op | source)
XLA Modules:
  0.0 51.0 jit_solution(1768806274358140747)
XLA Ops:
  0.0 1.0 %copy-done = f32[128,1024]{1,0:T(8,128)S(1)} copy-done((f32[128,1024]{1,0:T(8,128)S(1)}, f32[128,1024]{1,0:T(8,128)}, u32[]{:S(2)}) %copy-start) | copy-done | bytes 524312
  1.0 0.2 standardize.1
  1.3 3.0 %collective-permute-start.1 = (bf16[128,512]{1,0:T(8,128)(2,1)S(1)}, bf16[128,512]{1,0:T(8,128)(2,1)S(1)}, u32[]{:S(2)}, u32[]{:S(2)}) collective-permute-start(bf16[128,512]{1,0:T(8,128)(2,1)S(1)} %get-tuple-element.29.refs_0_), channel_id=1, source_target_pairs={{2,0},{4,2},{6,4},{7,6},{5,7},{3,5},{1,3},{0,1},{10,8},{12,10},{14... | collective-permute-start | bytes 393224 | tf_op jit(solution)/shard_map/ppermute | solution.py:168
  4.3 0.1 collective-permute-start
  4.4 1.9 %collective-permute-start.11 = (bf16[128,512]{1,0:T(8,128)(2,1)S(1)}, bf16[128,512]{1,0:T(8,128)(2,1)S(1)}, u32[]{:S(2)}, u32[]{:S(2)}) collective-permute-start(bf16[128,512]{1,0:T(8,128)(2,1)S(1)} %get-tuple-element.34.refs_0_.refs_8_), channel_id=1, source_target_pairs={{2,0},{4,2},{6,4},{7,6},{5,7},{3,5},{1,3},{0,1},{10,8},{12,10},{14... | collective-permute-start | bytes 393224 | tf_op jit(solution)/shard_map/ppermute | solution.py:172
  6.3 0.1 collective-permute-start.10
  6.5 1.9 %collective-permute-start.4 = (bf16[128,1024]{1,0:T(8,128)(2,1)S(1)}, bf16[128,1024]{1,0:T(8,128)(2,1)}, u32[]{:S(2)}, u32[]{:S(2)}) collective-permute-start(bf16[128,1024]{1,0:T(8,128)(2,1)S(1)} %get-tuple-element.39.refs_16_), channel_id=1, source_target_pairs={{0,16},{8,24},{16,0},{24,8},{1,17},{9,25},{17,1},{25,9},{2,18},{10... | collective-permute-start | bytes 786440 | tf_op jit(solution)/shard_map/ppermute | solution.py:150
  8.3 0.7 %add_multiply_fusion = (s32[8]{0:T(128)S(1)}, s32[8]{0:T(128)S(1)}) fusion(s32[]{:T(128)S(6)} %mul.22, s32[8]{0:T(128)} %constant.84.clone, s32[]{:T(128)S(6)} %select_n.48), kind=kLoop, calls=%fused_computation.13 | loop fusion | flops 160 | bytes 104 | tf_op jit(solution)/shard_map/mul | solution.py:178
  9.0 0.7 %reshape.30 = s32[2,256]{1,0:T(2,128)S(1)} reshape(s32[512]{0:T(512)} %param.6) | data formatting | bytes 4096 | tf_op jit(solution)/shard_map/reshape | solution.py:181
  9.7 0.9 %collective-permute-done.refs_1_ = bf16[128,512]{1,0:T(8,128)(2,1)S(1)} collective-permute-done((bf16[128,512]{1,0:T(8,128)(2,1)S(1)}, bf16[128,512]{1,0:T(8,128)(2,1)S(1)}, u32[]{:S(2)}, u32[]{:S(2)}) %collective-permute-start) | collective-permute-done | bytes 131104 | tf_op jit(solution)/shard_map/ppermute | solution.py:165
  10.6 0.7 %collective-permute-start.2 = (bf16[128,512]{1,0:T(8,128)(2,1)S(1)}, bf16[128,512]{1,0:T(8,128)(2,1)S(1)}, u32[]{:S(2)}, u32[]{:S(2)}) collective-permute-start(bf16[128,512]{1,0:T(8,128)(2,1)S(1)} %collective-permute-done.refs_1_), channel_id=1, source_target_pairs={{0,2},{2,4},{4,6},{6,7},{7,5},{5,3},{3,1},{1,0},{8,10},{10,12},{12... | collective-permute-start | bytes 393224 | tf_op jit(solution)/shard_map/ppermute | solution.py:165
  11.3 0.0 collective-permute-done.11.refs_2_.refs_10_
  11.3 1.4 %collective-permute-start.13 = (bf16[128,512]{1,0:T(8,128)(2,1)S(1)}, bf16[128,512]{1,0:T(8,128)(2,1)S(1)}, u32[]{:S(2)}, u32[]{:S(2)}) collective-permute-start(bf16[128,512]{1,0:T(8,128)(2,1)S(1)} %collective-permute-done.11.refs_2_.refs_10_), channel_id=1, source_target_pairs={{2,0},{4,2},{6,4},{7,6},{5,7},{3,5},{1,3},{0,1},{10,8},{12,10},{14... | collective-permute-start | bytes 393224 | tf_op jit(solution)/shard_map/ppermute | solution.py:172
  12.7 0.1 add_bitcast_fusion
  12.7 0.0 collective-permute-done.1.refs_2_
  12.7 1.6 %collective-permute-start.3 = (bf16[128,512]{1,0:T(8,128)(2,1)S(1)}, bf16[128,512]{1,0:T(8,128)(2,1)S(1)}, u32[]{:S(2)}, u32[]{:S(2)}) collective-permute-start(bf16[128,512]{1,0:T(8,128)(2,1)S(1)} %collective-permute-done.1.refs_2_), channel_id=1, source_target_pairs={{2,0},{4,2},{6,4},{7,6},{5,7},{3,5},{1,3},{0,1},{10,8},{12,10},{14... | collective-permute-start | bytes 393224 | tf_op jit(solution)/shard_map/ppermute | solution.py:168
  14.3 0.0 collective-permute-done.10.refs_1_.refs_9_
  14.3 0.5 collective-permute-start.12
  14.8 1.4 %collective-permute-done.2.refs_3_ = bf16[128,512]{1,0:T(8,128)(2,1)S(1)} collective-permute-done((bf16[128,512]{1,0:T(8,128)(2,1)S(1)}, bf16[128,512]{1,0:T(8,128)(2,1)S(1)}, u32[]{:S(2)}, u32[]{:S(2)}) %collective-permute-start.2) | collective-permute-done | bytes 131104 | tf_op jit(solution)/shard_map/ppermute | solution.py:165
  16.2 0.0 collective-permute-done.4.refs_17_
  16.2 0.9 %collective-permute-start.5 = (bf16[128,512]{1,0:T(8,128)(2,1)S(1)}, bf16[128,512]{1,0:T(8,128)(2,1)S(1)}, u32[]{:S(2)}, u32[]{:S(2)}) collective-permute-start(bf16[128,512]{1,0:T(8,128)(2,1)S(1)} %collective-permute-done.2.refs_3_), channel_id=1, source_target_pairs={{0,2},{2,4},{4,6},{6,7},{7,5},{5,3},{3,1},{1,0},{8,10},{10,12},{12... | collective-permute-start | bytes 393224 | tf_op jit(solution)/shard_map/ppermute | solution.py:165
  17.1 0.0 collective-permute-done.13.refs_4_.refs_12_
  17.1 1.1 %collective-permute-start.15 = (bf16[128,512]{1,0:T(8,128)(2,1)S(1)}, bf16[128,512]{1,0:T(8,128)(2,1)S(1)}, u32[]{:S(2)}, u32[]{:S(2)}) collective-permute-start(bf16[128,512]{1,0:T(8,128)(2,1)S(1)} %collective-permute-done.13.refs_4_.refs_12_), channel_id=1, source_target_pairs={{2,0},{4,2},{6,4},{7,6},{5,7},{3,5},{1,3},{0,1},{10,8},{12,10},{14... | collective-permute-start | bytes 393224 | tf_op jit(solution)/shard_map/ppermute | solution.py:172
  18.3 1.5 %collective-permute-done.3.refs_4_ = bf16[128,512]{1,0:T(8,128)(2,1)S(1)} collective-permute-done((bf16[128,512]{1,0:T(8,128)(2,1)S(1)}, bf16[128,512]{1,0:T(8,128)(2,1)S(1)}, u32[]{:S(2)}, u32[]{:S(2)}) %collective-permute-start.3) | collective-permute-done | bytes 131104 | tf_op jit(solution)/shard_map/ppermute | solution.py:168
  19.8 1.1 %collective-permute-start.6 = (bf16[128,512]{1,0:T(8,128)(2,1)S(1)}, bf16[128,512]{1,0:T(8,128)(2,1)S(1)}, u32[]{:S(2)}, u32[]{:S(2)}) collective-permute-start(bf16[128,512]{1,0:T(8,128)(2,1)S(1)} %collective-permute-done.3.refs_4_), channel_id=1, source_target_pairs={{2,0},{4,2},{6,4},{7,6},{5,7},{3,5},{1,3},{0,1},{10,8},{12,10},{14... | collective-permute-start | bytes 393224 | tf_op jit(solution)/shard_map/ppermute | solution.py:168
  20.9 0.0 collective-permute-done.12.refs_3_.refs_11_
  20.9 0.9 %collective-permute-start.14 = (bf16[128,512]{1,0:T(8,128)(2,1)S(1)}, bf16[128,512]{1,0:T(8,128)(2,1)S(1)}, u32[]{:S(2)}, u32[]{:S(2)}) collective-permute-start(bf16[128,512]{1,0:T(8,128)(2,1)S(1)} %collective-permute-done.12.refs_3_.refs_11_), channel_id=1, source_target_pairs={{0,2},{2,4},{4,6},{6,7},{7,5},{5,3},{3,1},{1,0},{8,10},{10,12},{12... | collective-permute-start | bytes 393224 | tf_op jit(solution)/shard_map/ppermute | solution.py:170
  21.8 0.8 %collective-permute-done.15.refs_6_.refs_14_ = bf16[128,512]{1,0:T(8,128)(2,1)S(1)} collective-permute-done((bf16[128,512]{1,0:T(8,128)(2,1)S(1)}, bf16[128,512]{1,0:T(8,128)(2,1)S(1)}, u32[]{:S(2)}, u32[]{:S(2)}) %collective-permute-start.15) | collective-permute-done | bytes 131104 | tf_op jit(solution)/shard_map/ppermute | solution.py:172
  22.7 1.1 %collective-permute-start.16 = (bf16[128,512]{1,0:T(8,128)(2,1)S(1)}, bf16[128,512]{1,0:T(8,128)(2,1)S(1)}, u32[]{:S(2)}, u32[]{:S(2)}) collective-permute-start(bf16[128,512]{1,0:T(8,128)(2,1)S(1)} %collective-permute-done.15.refs_6_.refs_14_), channel_id=1, source_target_pairs={{2,0},{4,2},{6,4},{7,6},{5,7},{3,5},{1,3},{0,1},{10,8},{12,10},{14... | collective-permute-start | bytes 393224 | tf_op jit(solution)/shard_map/ppermute | solution.py:172
  23.8 0.0 collective-permute-done.5.refs_5_
  23.8 1.0 %collective-permute-start.7 = (bf16[128,512]{1,0:T(8,128)(2,1)S(1)}, bf16[128,512]{1,0:T(8,128)(2,1)S(1)}, u32[]{:S(2)}, u32[]{:S(2)}) collective-permute-start(bf16[128,512]{1,0:T(8,128)(2,1)S(1)} %collective-permute-done.5.refs_5_), channel_id=1, source_target_pairs={{0,2},{2,4},{4,6},{6,7},{7,5},{5,3},{3,1},{1,0},{8,10},{10,12},{12... | collective-permute-start | bytes 393224 | tf_op jit(solution)/shard_map/ppermute | solution.py:165
  24.8 0.2 compare_convert_fusion.hot_ref
  25.0 0.0 copy-start.1
  25.0 1.2 %collective-permute-done.14.refs_5_.refs_13_ = bf16[128,512]{1,0:T(8,128)(2,1)S(1)} collective-permute-done((bf16[128,512]{1,0:T(8,128)(2,1)S(1)}, bf16[128,512]{1,0:T(8,128)(2,1)S(1)}, u32[]{:S(2)}, u32[]{:S(2)}) %collective-permute-start.14) | collective-permute-done | bytes 131104 | tf_op jit(solution)/shard_map/ppermute | solution.py:170
  26.2 1.5 %collective-permute-done.16.refs_7_.refs_15_ = bf16[128,512]{1,0:T(8,128)(2,1)S(1)} collective-permute-done((bf16[128,512]{1,0:T(8,128)(2,1)S(1)}, bf16[128,512]{1,0:T(8,128)(2,1)S(1)}, u32[]{:S(2)}, u32[]{:S(2)}) %collective-permute-start.16) | collective-permute-done | bytes 131104 | tf_op jit(solution)/shard_map/ppermute | solution.py:172
  27.7 0.7 %select.13 = (bf16[256,512]{1,0:T(8,128)(2,1)S(1)}, bf16[256,512]{1,0:T(8,128)(2,1)S(1)}) custom-call(bf16[512,1024]{1,0:T(8,128)(2,1)S(1)} %compare_convert_fusion.hot_ref, bf16[128,512]{1,0:T(8,128)(2,1)S(1)} %get-tuple-element.34.refs_0_.refs_8_, bf16[128,512]{1,0:T(8,128)(2,1)S(1)} %collective-permute-done.10.refs_1_.refs_9_, ...), custom_call_target="tpu_custom_call" | custom-call | flops 1 | bytes 1 | tf_op jit(solution)/shard_map/select/pallas_call | solution.py:192
  28.4 0.0 copy-start.2
  28.4 0.1 collective-permute-start.17
  28.5 0.0 collective-permute-done.6.refs_6_
  28.5 0.2 collective-permute-done.7.refs_7_
  28.7 0.7 %select.12 = (bf16[256,512]{1,0:T(8,128)(2,1)S(1)}, bf16[256,512]{1,0:T(8,128)(2,1)S(1)}) custom-call(bf16[512,1024]{1,0:T(8,128)(2,1)S(1)} %compare_convert_fusion.hot_ref, bf16[128,512]{1,0:T(8,128)(2,1)S(1)} %get-tuple-element.29.refs_0_, bf16[128,512]{1,0:T(8,128)(2,1)S(1)} %collective-permute-done.refs_1_, ...), custom_call_target="tpu_custom_call" | custom-call | flops 1 | bytes 1 | tf_op jit(solution)/shard_map/select/pallas_call | solution.py:192
  29.5 0.3 collective-permute-start.8
  29.8 0.2 collective-permute-done.17.right
  30.1 1.2 %collective-permute-start.18 = (bf16[256,512]{1,0:T(8,128)(2,1)S(1)}, bf16[256,512]{1,0:T(8,128)(2,1)}, u32[]{:S(2)}, u32[]{:S(2)}) collective-permute-start(bf16[256,512]{1,0:T(8,128)(2,1)S(1)} %add.113.left), channel_id=1, source_target_pairs={{0,16},{8,24},{16,0},{24,8},{1,17},{9,25},{17,1},{25,9},{2,18},{10... | collective-permute-start | bytes 786440 | tf_op jit(solution)/shard_map/ppermute | solution.py:150
  31.3 0.1 collective-permute-start.19
  31.4 0.4 collective-permute-start.20
  31.8 0.0 collective-permute-done.8.right
  31.8 0.9 %collective-permute-start.9 = (bf16[256,512]{1,0:T(8,128)(2,1)S(1)}, bf16[256,512]{1,0:T(8,128)(2,1)}, u32[]{:S(2)}, u32[]{:S(2)}) collective-permute-start(bf16[256,512]{1,0:T(8,128)(2,1)S(1)} %add.112.left), channel_id=1, source_target_pairs={{0,16},{8,24},{16,0},{24,8},{1,17},{9,25},{17,1},{25,9},{2,18},{10... | collective-permute-start | bytes 786440 | tf_op jit(solution)/shard_map/ppermute | solution.py:150
  32.8 0.0 copy-done.2
  32.8 0.2 copy.6.kr_ref
  33.0 0.1 pad_add_fusion.1.cols_ref
  33.1 0.0 collective-permute-done.19.refs_18_
  33.1 0.4 collective-permute-done.20.refs_19_
  33.5 3.0 %direct.1 = (bf16[1024,1024]{1,0:T(8,128)(2,1)S(1)}, bf16[512,1024]{1,0:T(8,128)(2,1)S(1)}, f32[1024,512]{1,0:T(8,128)S(1)}, f32[1024,512]{1,0:T(8,128)S(1)}) custom-call(s32[12]{0:T(128)S(1)} %pad_add_fusion.1.cols_ref, f32[1024,1]{1,0:T(8,128)S(1)} %copy.6.kr_ref, f32[1,512]{1,0:T(1,128)S(1)} %dynamic-slice_bitcast_fusion.kc_ref, ...), custom_call_target="tpu_custom_call" | custom-call | flops 1 | bytes 1 | tf_op jit(solution)/shard_map/direct/pallas_call | solution.py:231
  36.6 2.8 %collective-permute-done.18.right = bf16[256,512]{1,0:T(8,128)(2,1)} collective-permute-done((bf16[256,512]{1,0:T(8,128)(2,1)S(1)}, bf16[256,512]{1,0:T(8,128)(2,1)}, u32[]{:S(2)}, u32[]{:S(2)}) %collective-permute-start.18) | collective-permute-done | bytes 262176 | tf_op jit(solution)/shard_map/ppermute | solution.py:150
  39.4 4.8 %collective-permute-done.9.right = bf16[256,512]{1,0:T(8,128)(2,1)} collective-permute-done((bf16[256,512]{1,0:T(8,128)(2,1)S(1)}, bf16[256,512]{1,0:T(8,128)(2,1)}, u32[]{:S(2)}, u32[]{:S(2)}) %collective-permute-start.9) | collective-permute-done | bytes 262176 | tf_op jit(solution)/shard_map/ppermute | solution.py:150
  44.2 1.0 %add.115.near = bf16[256,512]{1,0:T(8,128)(2,1)S(1)} custom-call(bf16[256,512]{1,0:T(8,128)(2,1)S(1)} %add.112.left, bf16[256,512]{1,0:T(8,128)(2,1)} %collective-permute-done.9.right), custom_call_target="tpu_custom_call" | custom-call | flops 1 | bytes 1 | tf_op jit(solution)/shard_map/add/pallas_call | solution.py:113
  45.2 0.1 collective-permute-start.22
  45.3 1.0 %add.114.near = bf16[256,512]{1,0:T(8,128)(2,1)S(1)} custom-call(bf16[256,512]{1,0:T(8,128)(2,1)S(1)} %add.113.left, bf16[256,512]{1,0:T(8,128)(2,1)} %collective-permute-done.18.right), custom_call_target="tpu_custom_call" | custom-call | flops 1 | bytes 1 | tf_op jit(solution)/shard_map/add/pallas_call | solution.py:113
  46.2 0.6 %collective-permute-start.21 = (bf16[256,512]{1,0:T(8,128)(2,1)S(1)}, bf16[256,512]{1,0:T(8,128)(2,1)S(1)}, u32[]{:S(2)}, u32[]{:S(2)}) collective-permute-start(bf16[256,512]{1,0:T(8,128)(2,1)S(1)} %add.114.near), channel_id=1, source_target_pairs={{0,8},{8,0},{16,24},{24,16},{1,9},{9,1},{17,25},{25,17},{2,10},{10... | collective-permute-start | bytes 786440 | tf_op jit(solution)/shard_map/ppermute | solution.py:150
  46.8 0.0 collective-permute-done.22.far
  46.8 1.0 %partial.1 = (f32[1024,512]{1,0:T(8,128)S(1)}, f32[512,512]{1,0:T(8,128)S(1)}) custom-call(bf16[1024,1024]{1,0:T(8,128)(2,1)S(1)} %get-tuple-element.45.zr, bf16[512,1024]{1,0:T(8,128)(2,1)S(1)} %get-tuple-element.46.zc, bf16[256,512]{1,0:T(8,128)(2,1)S(1)} %add.115.near, bf16[256,512]{1,0:T(8,128)(2,1)S(1)} %collective-permute-done.22.far), custom_call_target="tpu_custom_call" | custom-call | flops 1 | bytes 1 | tf_op jit(solution)/shard_map/partial/pallas_call | solution.py:247
  47.8 0.1 collective-permute-done.21.far
  48.0 3.0 %final.1 = f32[1024,512]{1,0:T(8,128)} custom-call(bf16[1024,1024]{1,0:T(8,128)(2,1)S(1)} %get-tuple-element.45.zr, bf16[512,1024]{1,0:T(8,128)(2,1)S(1)} %get-tuple-element.46.zc, bf16[256,512]{1,0:T(8,128)(2,1)S(1)} %add.114.near, bf16[256,512]{1,0:T(8,128)(2,1)S(1)} %collective-permute-done.21.far, f32[1024,512]{1,0:T(8,128)S(1)} %get-tuple-element.49.row_part, ...), custom_call_target="tpu_custom_call" | custom-call | flops 1 | bytes 1 | tf_op jit(solution)/shard_map/final/pallas_call | solution.py:257
  (10 shorter events, 0.1 us)
Async XLA Ops:
  0.0 1.0 %copy-start = (f32[128,1024]{1,0:T(8,128)S(1)}, f32[128,1024]{1,0:T(8,128)}, u32[]{:S(2)}) copy-start(f32[128,1024]{1,0:T(8,128)} %x_ref.1) | copy-start | bytes 1572868
  1.3 11.4 %collective-permute-start.1 = (bf16[128,512]{1,0:T(8,128)(2,1)S(1)}, bf16[128,512]{1,0:T(8,128)(2,1)S(1)}, u32[]{:S(2)}, u32[]{:S(2)}) collective-permute-start(bf16[128,512]{1,0:T(8,128)(2,1)S(1)} %get-tuple-element.29.refs_0_), channel_id=1, source_target_pairs={{2,0},{4,2},{6,4},{7,6},{5,7},{3,5},{1,3},{0,1},{10,8},{12,10},{14... | collective-permute-start | bytes 393224 | tf_op jit(solution)/shard_map/ppermute | solution.py:168
  4.3 6.3 %collective-permute-start = (bf16[128,512]{1,0:T(8,128)(2,1)S(1)}, bf16[128,512]{1,0:T(8,128)(2,1)S(1)}, u32[]{:S(2)}, u32[]{:S(2)}) collective-permute-start(bf16[128,512]{1,0:T(8,128)(2,1)S(1)} %get-tuple-element.29.refs_0_), channel_id=1, source_target_pairs={{0,2},{2,4},{4,6},{6,7},{7,5},{5,3},{3,1},{1,0},{8,10},{10,12},{12... | collective-permute-start | bytes 393224 | tf_op jit(solution)/shard_map/ppermute | solution.py:165
  4.4 6.9 %collective-permute-start.11 = (bf16[128,512]{1,0:T(8,128)(2,1)S(1)}, bf16[128,512]{1,0:T(8,128)(2,1)S(1)}, u32[]{:S(2)}, u32[]{:S(2)}) collective-permute-start(bf16[128,512]{1,0:T(8,128)(2,1)S(1)} %get-tuple-element.34.refs_0_.refs_8_), channel_id=1, source_target_pairs={{2,0},{4,2},{6,4},{7,6},{5,7},{3,5},{1,3},{0,1},{10,8},{12,10},{14... | collective-permute-start | bytes 393224 | tf_op jit(solution)/shard_map/ppermute | solution.py:172
  6.3 8.0 %collective-permute-start.10 = (bf16[128,512]{1,0:T(8,128)(2,1)S(1)}, bf16[128,512]{1,0:T(8,128)(2,1)S(1)}, u32[]{:S(2)}, u32[]{:S(2)}) collective-permute-start(bf16[128,512]{1,0:T(8,128)(2,1)S(1)} %get-tuple-element.34.refs_0_.refs_8_), channel_id=1, source_target_pairs={{0,2},{2,4},{4,6},{6,7},{7,5},{5,3},{3,1},{1,0},{8,10},{10,12},{12... | collective-permute-start | bytes 393224 | tf_op jit(solution)/shard_map/ppermute | solution.py:170
  6.5 9.8 %collective-permute-start.4 = (bf16[128,1024]{1,0:T(8,128)(2,1)S(1)}, bf16[128,1024]{1,0:T(8,128)(2,1)}, u32[]{:S(2)}, u32[]{:S(2)}) collective-permute-start(bf16[128,1024]{1,0:T(8,128)(2,1)S(1)} %get-tuple-element.39.refs_16_), channel_id=1, source_target_pairs={{0,16},{8,24},{16,0},{24,8},{1,17},{9,25},{17,1},{25,9},{2,18},{10... | collective-permute-start | bytes 786440 | tf_op jit(solution)/shard_map/ppermute | solution.py:150
  10.6 5.6 %collective-permute-start.2 = (bf16[128,512]{1,0:T(8,128)(2,1)S(1)}, bf16[128,512]{1,0:T(8,128)(2,1)S(1)}, u32[]{:S(2)}, u32[]{:S(2)}) collective-permute-start(bf16[128,512]{1,0:T(8,128)(2,1)S(1)} %collective-permute-done.refs_1_), channel_id=1, source_target_pairs={{0,2},{2,4},{4,6},{6,7},{7,5},{5,3},{3,1},{1,0},{8,10},{10,12},{12... | collective-permute-start | bytes 393224 | tf_op jit(solution)/shard_map/ppermute | solution.py:165
  11.3 5.8 %collective-permute-start.13 = (bf16[128,512]{1,0:T(8,128)(2,1)S(1)}, bf16[128,512]{1,0:T(8,128)(2,1)S(1)}, u32[]{:S(2)}, u32[]{:S(2)}) collective-permute-start(bf16[128,512]{1,0:T(8,128)(2,1)S(1)} %collective-permute-done.11.refs_2_.refs_10_), channel_id=1, source_target_pairs={{2,0},{4,2},{6,4},{7,6},{5,7},{3,5},{1,3},{0,1},{10,8},{12,10},{14... | collective-permute-start | bytes 393224 | tf_op jit(solution)/shard_map/ppermute | solution.py:172
  12.7 7.1 %collective-permute-start.3 = (bf16[128,512]{1,0:T(8,128)(2,1)S(1)}, bf16[128,512]{1,0:T(8,128)(2,1)S(1)}, u32[]{:S(2)}, u32[]{:S(2)}) collective-permute-start(bf16[128,512]{1,0:T(8,128)(2,1)S(1)} %collective-permute-done.1.refs_2_), channel_id=1, source_target_pairs={{2,0},{4,2},{6,4},{7,6},{5,7},{3,5},{1,3},{0,1},{10,8},{12,10},{14... | collective-permute-start | bytes 393224 | tf_op jit(solution)/shard_map/ppermute | solution.py:168
  14.3 6.6 %collective-permute-start.12 = (bf16[128,512]{1,0:T(8,128)(2,1)S(1)}, bf16[128,512]{1,0:T(8,128)(2,1)S(1)}, u32[]{:S(2)}, u32[]{:S(2)}) collective-permute-start(bf16[128,512]{1,0:T(8,128)(2,1)S(1)} %collective-permute-done.10.refs_1_.refs_9_), channel_id=1, source_target_pairs={{0,2},{2,4},{4,6},{6,7},{7,5},{5,3},{3,1},{1,0},{8,10},{10,12},{12... | collective-permute-start | bytes 393224 | tf_op jit(solution)/shard_map/ppermute | solution.py:170
  16.2 7.6 %collective-permute-start.5 = (bf16[128,512]{1,0:T(8,128)(2,1)S(1)}, bf16[128,512]{1,0:T(8,128)(2,1)S(1)}, u32[]{:S(2)}, u32[]{:S(2)}) collective-permute-start(bf16[128,512]{1,0:T(8,128)(2,1)S(1)} %collective-permute-done.2.refs_3_), channel_id=1, source_target_pairs={{0,2},{2,4},{4,6},{6,7},{7,5},{5,3},{3,1},{1,0},{8,10},{10,12},{12... | collective-permute-start | bytes 393224 | tf_op jit(solution)/shard_map/ppermute | solution.py:165
  17.1 5.5 %collective-permute-start.15 = (bf16[128,512]{1,0:T(8,128)(2,1)S(1)}, bf16[128,512]{1,0:T(8,128)(2,1)S(1)}, u32[]{:S(2)}, u32[]{:S(2)}) collective-permute-start(bf16[128,512]{1,0:T(8,128)(2,1)S(1)} %collective-permute-done.13.refs_4_.refs_12_), channel_id=1, source_target_pairs={{2,0},{4,2},{6,4},{7,6},{5,7},{3,5},{1,3},{0,1},{10,8},{12,10},{14... | collective-permute-start | bytes 393224 | tf_op jit(solution)/shard_map/ppermute | solution.py:172
  19.8 8.7 %collective-permute-start.6 = (bf16[128,512]{1,0:T(8,128)(2,1)S(1)}, bf16[128,512]{1,0:T(8,128)(2,1)S(1)}, u32[]{:S(2)}, u32[]{:S(2)}) collective-permute-start(bf16[128,512]{1,0:T(8,128)(2,1)S(1)} %collective-permute-done.3.refs_4_), channel_id=1, source_target_pairs={{2,0},{4,2},{6,4},{7,6},{5,7},{3,5},{1,3},{0,1},{10,8},{12,10},{14... | collective-permute-start | bytes 393224 | tf_op jit(solution)/shard_map/ppermute | solution.py:168
  20.9 5.3 %collective-permute-start.14 = (bf16[128,512]{1,0:T(8,128)(2,1)S(1)}, bf16[128,512]{1,0:T(8,128)(2,1)S(1)}, u32[]{:S(2)}, u32[]{:S(2)}) collective-permute-start(bf16[128,512]{1,0:T(8,128)(2,1)S(1)} %collective-permute-done.12.refs_3_.refs_11_), channel_id=1, source_target_pairs={{0,2},{2,4},{4,6},{6,7},{7,5},{5,3},{3,1},{1,0},{8,10},{10,12},{12... | collective-permute-start | bytes 393224 | tf_op jit(solution)/shard_map/ppermute | solution.py:170
  22.7 5.0 %collective-permute-start.16 = (bf16[128,512]{1,0:T(8,128)(2,1)S(1)}, bf16[128,512]{1,0:T(8,128)(2,1)S(1)}, u32[]{:S(2)}, u32[]{:S(2)}) collective-permute-start(bf16[128,512]{1,0:T(8,128)(2,1)S(1)} %collective-permute-done.15.refs_6_.refs_14_), channel_id=1, source_target_pairs={{2,0},{4,2},{6,4},{7,6},{5,7},{3,5},{1,3},{0,1},{10,8},{12,10},{14... | collective-permute-start | bytes 393224 | tf_op jit(solution)/shard_map/ppermute | solution.py:172
  23.8 5.0 %collective-permute-start.7 = (bf16[128,512]{1,0:T(8,128)(2,1)S(1)}, bf16[128,512]{1,0:T(8,128)(2,1)S(1)}, u32[]{:S(2)}, u32[]{:S(2)}) collective-permute-start(bf16[128,512]{1,0:T(8,128)(2,1)S(1)} %collective-permute-done.5.refs_5_), channel_id=1, source_target_pairs={{0,2},{2,4},{4,6},{6,7},{7,5},{5,3},{3,1},{1,0},{8,10},{10,12},{12... | collective-permute-start | bytes 393224 | tf_op jit(solution)/shard_map/ppermute | solution.py:165
  25.0 4.8 %copy-start.1 = (s32[4096]{0:T(1024)S(1)}, s32[4096]{0:T(1024)}, u32[]{:S(2)}) copy-start(s32[4096]{0:T(1024)} %param.7) | copy-start | bytes 49156
  28.4 4.4 %copy-start.2 = (s32[4]{0:T(128)S(1)}, s32[4]{0:T(128)}, u32[]{:S(2)}) copy-start(s32[4]{0:T(128)} %constant.85.clone) | copy-start | bytes 52
  28.4 1.6 %collective-permute-start.17 = (bf16[256,512]{1,0:T(8,128)(2,1)S(1)}, bf16[256,512]{1,0:T(8,128)(2,1)S(1)}, u32[]{:S(2)}, u32[]{:S(2)}) collective-permute-start(bf16[256,512]{1,0:T(8,128)(2,1)S(1)} %get-tuple-element.36), channel_id=1, source_target_pairs={{0,8},{8,0},{16,24},{24,16},{1,9},{9,1},{17,25},{25,17},{2,10},{10... | collective-permute-start | bytes 786440 | tf_op jit(solution)/shard_map/ppermute | solution.py:150
  29.5 2.3 %collective-permute-start.8 = (bf16[256,512]{1,0:T(8,128)(2,1)S(1)}, bf16[256,512]{1,0:T(8,128)(2,1)S(1)}, u32[]{:S(2)}, u32[]{:S(2)}) collective-permute-start(bf16[256,512]{1,0:T(8,128)(2,1)S(1)} %get-tuple-element.33), channel_id=1, source_target_pairs={{0,8},{8,0},{16,24},{24,16},{1,9},{9,1},{17,25},{25,17},{2,10},{10... | collective-permute-start | bytes 786440 | tf_op jit(solution)/shard_map/ppermute | solution.py:150
  30.1 9.3 %collective-permute-start.18 = (bf16[256,512]{1,0:T(8,128)(2,1)S(1)}, bf16[256,512]{1,0:T(8,128)(2,1)}, u32[]{:S(2)}, u32[]{:S(2)}) collective-permute-start(bf16[256,512]{1,0:T(8,128)(2,1)S(1)} %add.113.left), channel_id=1, source_target_pairs={{0,16},{8,24},{16,0},{24,8},{1,17},{9,25},{17,1},{25,9},{2,18},{10... | collective-permute-start | bytes 786440 | tf_op jit(solution)/shard_map/ppermute | solution.py:150
  31.3 1.8 %collective-permute-start.19 = (bf16[128,1024]{1,0:T(8,128)(2,1)S(1)}, bf16[128,1024]{1,0:T(8,128)(2,1)}, u32[]{:S(2)}, u32[]{:S(2)}) collective-permute-start(bf16[128,1024]{1,0:T(8,128)(2,1)S(1)} %get-tuple-element.39.refs_16_), channel_id=1, source_target_pairs={{0,8},{8,0},{16,24},{24,16},{1,9},{9,1},{17,25},{25,17},{2,10},{10... | collective-permute-start | bytes 786440 | tf_op jit(solution)/shard_map/ppermute | solution.py:150
  31.4 2.2 %collective-permute-start.20 = (bf16[128,1024]{1,0:T(8,128)(2,1)}, bf16[128,1024]{1,0:T(8,128)(2,1)}, u32[]{:S(2)}, u32[]{:S(2)}) collective-permute-start(bf16[128,1024]{1,0:T(8,128)(2,1)} %collective-permute-done.4.refs_17_), channel_id=1, source_target_pairs={{0,8},{8,0},{16,24},{24,16},{1,9},{9,1},{17,25},{25,17},{2,10},{10... | collective-permute-start | bytes 786440 | tf_op jit(solution)/shard_map/ppermute | solution.py:150
  31.8 12.4 %collective-permute-start.9 = (bf16[256,512]{1,0:T(8,128)(2,1)S(1)}, bf16[256,512]{1,0:T(8,128)(2,1)}, u32[]{:S(2)}, u32[]{:S(2)}) collective-permute-start(bf16[256,512]{1,0:T(8,128)(2,1)S(1)} %add.112.left), channel_id=1, source_target_pairs={{0,16},{8,24},{16,0},{24,8},{1,17},{9,25},{17,1},{25,9},{2,18},{10... | collective-permute-start | bytes 786440 | tf_op jit(solution)/shard_map/ppermute | solution.py:150
  45.2 1.6 %collective-permute-start.22 = (bf16[256,512]{1,0:T(8,128)(2,1)S(1)}, bf16[256,512]{1,0:T(8,128)(2,1)S(1)}, u32[]{:S(2)}, u32[]{:S(2)}) collective-permute-start(bf16[256,512]{1,0:T(8,128)(2,1)S(1)} %add.115.near), channel_id=1, source_target_pairs={{0,8},{8,0},{16,24},{24,16},{1,9},{9,1},{17,25},{25,17},{2,10},{10... | collective-permute-start | bytes 786440 | tf_op jit(solution)/shard_map/ppermute | solution.py:150
  46.2 1.7 %collective-permute-start.21 = (bf16[256,512]{1,0:T(8,128)(2,1)S(1)}, bf16[256,512]{1,0:T(8,128)(2,1)S(1)}, u32[]{:S(2)}, u32[]{:S(2)}) collective-permute-start(bf16[256,512]{1,0:T(8,128)(2,1)S(1)} %add.114.near), channel_id=1, source_target_pairs={{0,8},{8,0},{16,24},{24,16},{1,9},{9,1},{17,25},{25,17},{2,10},{10... | collective-permute-start | bytes 786440 | tf_op jit(solution)/shard_map/ppermute | solution.py:150

commit v3 on v2

--- a/solution.py
+++ b/solution.py
@@ -18,6 +18,10 @@
 
 
 CHEAP = pl.CostEstimate(flops=1, bytes_accessed=1, transcendentals=0)
+
+
+def OUT(size, dtype):
+    return pltpu.VMEM(size, dtype)
 
 
 def dot_t(left, right):
@@ -112,13 +116,39 @@
 def add(left, right):
     return pl.pallas_call(
         add_kernel,
-        out_shape=jax.ShapeDtypeStruct(left.shape, left.dtype),
+        out_shape=OUT(left.shape, left.dtype),
         in_specs=[VMEM] * 2,
         out_specs=VMEM,
         compiler_params=params(4),
         cost_estimate=CHEAP,
         name="add",
     )(left, right)
+
+
+def sum_part_kernel(side_ref, left, right, both, part):
+    total = left[...] + right[...]
+    both[...] = total
+    rows = part.shape[0]
+
+    @pl.when(side_ref[0] == 0)
+    def _():
+        part[...] = total[:rows, :]
+
+    @pl.when(side_ref[0] != 0)
+    def _():
+        part[...] = total[rows:, :]
+
+
+def merge_kernel(side_ref, sum_a, got_a, sum_b, mine, mate, out_a, out_b):
+    out_a[...] = sum_a[...] + got_a[...]
+    rows = mine.shape[0]
+    for side in range(2):
+        first, second = (mine, mate) if side == 0 else (mate, mine)
+
+        @pl.when(side_ref[0] == side)
+        def _():
+            out_b[:rows, :] = sum_b[:rows, :] + first[...]
+            out_b[rows:, :] = sum_b[rows:, :] + second[...]
 
 
 def per_device(expression, pivots, degrees):
@@ -198,21 +228,25 @@
             cost_estimate=CHEAP,
             name="select",
         )(hot, *shards)
-        return add(mine, flip(theirs, 1))
-
-    def spread(total, got):
-        total = add(total, got)
-        mask = 4
-        while mask < n_rows:
-            total = add(total, flip(total, mask))
-            mask *= 2
-        return total, flip(total, 1)
-
-    sum_a = pivot_sums(list_a)
-    got_a = flip(sum_a, 2)
-    sum_b = pivot_sums(list_b)
-    sum_b, z, across = lax.optimization_barrier((sum_b, z, across))
-    got_b = flip(sum_b, 2)
+        return mine, flip(theirs, 1)
+
+    parity = (c % 2).astype(jnp.int32).reshape(1)
+    beside = [(k, k ^ 1) for k in range(n)]
+    mine, theirs = pivot_sums(list_b)
+    sum_b, part = pl.pallas_call(
+        sum_part_kernel,
+        out_shape=[OUT(mine.shape, bf16), OUT((half // 2, mine.shape[1]), bf16)],
+        in_specs=[SMEM, VMEM, VMEM],
+        out_specs=[VMEM] * 2,
+        compiler_params=params(4),
+        cost_estimate=CHEAP,
+        name="sum",
+    )(parity, mine, theirs)
+    got_b = flip(part, top)
+    sum_a = add(*pivot_sums(list_a))
+    sum_a, z, across = lax.optimization_barrier((sum_a, z, across))
+    got_a = flip(sum_a, top)
+    mate_b = lax.ppermute(got_b, "cols", beside)
     pieces, masks = [z, across], [0, top]
     mask = top // 2
     while mask:
@@ -242,8 +276,19 @@
         cost_estimate=CHEAP,
         name="direct",
     )(where, kr, kc, *list_a, *list_b, *pieces)
-    got_a, got_b, zr, zc, inverse, share = lax.optimization_barrier((got_a, got_b, zr, zc, inverse, share))
-    pa = spread(sum_a, got_a)
+    got_a, got_b, zr, zc, inverse, share, mate_b = lax.optimization_barrier(
+        (got_a, got_b, zr, zc, inverse, share, mate_b)
+    )
+    total_a, total_b = pl.pallas_call(
+        merge_kernel,
+        out_shape=[OUT(sum_a.shape, bf16), OUT(sum_b.shape, bf16)],
+        in_specs=[SMEM] + [VMEM] * 5,
+        out_specs=[VMEM] * 2,
+        compiler_params=params(4),
+        cost_estimate=CHEAP,
+        name="merge",
+    )(parity, sum_a, got_a, sum_b, got_b, mate_b)
+    pa, pb = (total_a, flip(total_a, 1)), (total_b, flip(total_b, 1))
     row_part, col_part = pl.pallas_call(
         partial_kernel,
         out_shape=[shape((height, 2 * half), f32), shape((width, 2 * half), f32)],
@@ -253,7 +298,6 @@
         cost_estimate=CHEAP,
         name="partial",
     )(zr, zc, *pa)
-    pb = spread(sum_b, got_b)
     return pl.pallas_call(
         final_kernel,
         out_shape=shape((height, width), f32),

time: 51.3 us -> 49.3 us (0.961)
  waiting for transfers between devices: 16.1 us -> 12.5 us
  starting transfers between devices: 20.9 us -> 22.1 us
  Pallas kernels: 10.8 us -> 9.79 us
  local copies, waits for them, and re-layouts: 1.99 us -> 2.77 us
  other arithmetic: 1.07 us -> 1.67 us
    ppermute x9, waiting for transfers between devices: 8.44 us -> 4.7 us  [per_device(): lax.ppermute(v, 'rows', [(i, i ^ mask) for i in range(n_rows)])]
    ppermute x0 -> x1, starting transfers between devices: none -> 1.32 us  [per_device(): mate_b = lax.ppermute(got_b, 'cols', beside)]
    pallas_call x4 -> x3, Pallas kernels: 2.03 us -> 1.11 us  [the longest x1 1.05 us: per_device(): pl.pallas_call(merge_kernel, out_shape=[OUT(sum_a.shape, bf16), OUT(sum_b...]
    reshape x1, local copies, waits for them, and re-layouts: 0.01 us -> 0.77 us  [per_device(): lax.dynamic_index_in_dim(scale.reshape(n_rows, n, local), c, 1, False)]
    reshape x1, other arithmetic: 0.01 us -> 0.6 us  [per_device(): scale.reshape(n_rows, n, local)]
    unnamed x6 -> x10, local copies, waits for them, and re-layouts: 1.05 us -> 1.07 us
  transfers between devices with their start and end apart: 23 -> 24, of which waited for: 12 -> 9; matrix products, arithmetic and copies ran while one was open for 4% -> 7% of each run, Pallas kernels for 13% -> 11%
where the time goes in v3:
time: 49.3 us; the launch traced here: 49.1 us
  starting transfers between devices  22.1 us (45%)
  waiting for transfers between devices  12.5 us (25%)
  Pallas kernels  9.79 us (20%)
  local copies, waits for them, and re-layouts  2.77 us (6%)
  other arithmetic  1.67 us (3%)
    ppermute x3, starting transfers between devices, per_device(): ba = lax.ppermute(ba, 'cols', backward)  5.7 us
    ppermute x9, starting transfers between devices, per_device(): lax.ppermute(v, 'rows', [(i, i ^ mask) for i in range(n_rows)])  5.51 us
    ppermute x4, starting transfers between devices, per_device(): bb = lax.ppermute(bb, 'cols', backward)  5.43 us
    ppermute x9, waiting for transfers between devices, per_device(): lax.ppermute(v, 'rows', [(i, i ^ mask) for i in range(n_rows)])  4.7 us
    pallas_call x1, Pallas kernels, per_device(): pl.pallas_call(final_kernel, out_shape=shape((height, width), f32), in_sp...  3.05 us
    pallas_call x1, Pallas kernels, per_device(): pl.pallas_call(functools.partial(direct_kernel, n, n_rows), out_shape=[sh...  2.98 us
    ppermute x4, starting transfers between devices, per_device(): fa = lax.ppermute(fa, 'cols', forward)  2.68 us
    ppermute x4, waiting for transfers between devices, per_device(): fa = lax.ppermute(fa, 'cols', forward)  2.61 us
  transfers between devices with their start and end apart: 24, of which 9 were waited for; matrix products, arithmetic and copies ran while one was open for 7% of the time, Pallas kernels for 11%

profile of v3, /device:TPU:0, one launch (start us, length us, event | category | flops | bytes accessed | tf_op | source)
XLA Modules:
  0.0 49.1 jit_solution(11341207306553614166)
XLA Ops:
  0.0 1.0 %copy-done = f32[128,1024]{1,0:T(8,128)S(1)} copy-done((f32[128,1024]{1,0:T(8,128)S(1)}, f32[128,1024]{1,0:T(8,128)}, u32[]{:S(2)}) %copy-start) | copy-done | bytes 524312
  1.0 0.2 standardize.1
  1.3 3.0 %collective-permute-start.1 = (bf16[128,512]{1,0:T(8,128)(2,1)S(1)}, bf16[128,512]{1,0:T(8,128)(2,1)S(1)}, u32[]{:S(2)}, u32[]{:S(2)}) collective-permute-start(bf16[128,512]{1,0:T(8,128)(2,1)S(1)} %get-tuple-element.34.refs_0_), channel_id=1, source_target_pairs={{2,0},{4,2},{6,4},{7,6},{5,7},{3,5},{1,3},{0,1},{10,8},{12,10},{14... | collective-permute-start | bytes 393224 | tf_op jit(solution)/shard_map/ppermute | solution.py:198
  4.3 0.1 collective-permute-start
  4.4 1.9 %collective-permute-start.11 = (bf16[128,512]{1,0:T(8,128)(2,1)S(1)}, bf16[128,512]{1,0:T(8,128)(2,1)S(1)}, u32[]{:S(2)}, u32[]{:S(2)}) collective-permute-start(bf16[128,512]{1,0:T(8,128)(2,1)S(1)} %get-tuple-element.41.refs_0_.refs_8_), channel_id=1, source_target_pairs={{2,0},{4,2},{6,4},{7,6},{5,7},{3,5},{1,3},{0,1},{10,8},{12,10},{14... | collective-permute-start | bytes 393224 | tf_op jit(solution)/shard_map/ppermute | solution.py:202
  6.3 0.1 collective-permute-start.10
  6.5 1.9 %collective-permute-start.4 = (bf16[128,1024]{1,0:T(8,128)(2,1)S(1)}, bf16[128,1024]{1,0:T(8,128)(2,1)S(1)}, u32[]{:S(2)}, u32[]{:S(2)}) collective-permute-start(bf16[128,1024]{1,0:T(8,128)(2,1)S(1)} %get-tuple-element.45.refs_16_), channel_id=1, source_target_pairs={{0,16},{8,24},{16,0},{24,8},{1,17},{9,25},{17,1},{25,9},{2,18},{10... | collective-permute-start | bytes 786440 | tf_op jit(solution)/shard_map/ppermute | solution.py:180
  8.3 0.7 %add_multiply_fusion = (s32[8]{0:T(128)S(1)}, s32[8]{0:T(128)S(1)}) fusion(s32[]{:T(128)S(6)} %mul.22, s32[8]{0:T(128)} %constant.86.clone, s32[]{:T(128)S(6)} %select_n.50), kind=kLoop, calls=%fused_computation.13 | loop fusion | flops 160 | bytes 104 | tf_op jit(solution)/shard_map/mul | solution.py:208
  9.0 0.7 %reshape.33 = s32[2,256]{1,0:T(2,128)S(1)} reshape(s32[512]{0:T(512)} %param.6) | data formatting | bytes 4096 | tf_op jit(solution)/shard_map/reshape | solution.py:211
  9.7 0.9 %collective-permute-done.refs_1_ = bf16[128,512]{1,0:T(8,128)(2,1)S(1)} collective-permute-done((bf16[128,512]{1,0:T(8,128)(2,1)S(1)}, bf16[128,512]{1,0:T(8,128)(2,1)S(1)}, u32[]{:S(2)}, u32[]{:S(2)}) %collective-permute-start) | collective-permute-done | bytes 131104 | tf_op jit(solution)/shard_map/ppermute | solution.py:195
  10.6 0.7 %collective-permute-start.2 = (bf16[128,512]{1,0:T(8,128)(2,1)S(1)}, bf16[128,512]{1,0:T(8,128)(2,1)S(1)}, u32[]{:S(2)}, u32[]{:S(2)}) collective-permute-start(bf16[128,512]{1,0:T(8,128)(2,1)S(1)} %collective-permute-done.refs_1_), channel_id=1, source_target_pairs={{0,2},{2,4},{4,6},{6,7},{7,5},{5,3},{3,1},{1,0},{8,10},{10,12},{12... | collective-permute-start | bytes 393224 | tf_op jit(solution)/shard_map/ppermute | solution.py:195
  11.3 0.0 collective-permute-done.11.refs_2_.refs_10_
  11.3 1.4 %collective-permute-start.13 = (bf16[128,512]{1,0:T(8,128)(2,1)S(1)}, bf16[128,512]{1,0:T(8,128)(2,1)S(1)}, u32[]{:S(2)}, u32[]{:S(2)}) collective-permute-start(bf16[128,512]{1,0:T(8,128)(2,1)S(1)} %collective-permute-done.11.refs_2_.refs_10_), channel_id=1, source_target_pairs={{2,0},{4,2},{6,4},{7,6},{5,7},{3,5},{1,3},{0,1},{10,8},{12,10},{14... | collective-permute-start | bytes 393224 | tf_op jit(solution)/shard_map/ppermute | solution.py:202
  12.7 0.1 add_bitcast_fusion
  12.7 0.0 collective-permute-done.1.refs_2_
  12.7 1.6 %collective-permute-start.3 = (bf16[128,512]{1,0:T(8,128)(2,1)S(1)}, bf16[128,512]{1,0:T(8,128)(2,1)S(1)}, u32[]{:S(2)}, u32[]{:S(2)}) collective-permute-start(bf16[128,512]{1,0:T(8,128)(2,1)S(1)} %collective-permute-done.1.refs_2_), channel_id=1, source_target_pairs={{2,0},{4,2},{6,4},{7,6},{5,7},{3,5},{1,3},{0,1},{10,8},{12,10},{14... | collective-permute-start | bytes 393224 | tf_op jit(solution)/shard_map/ppermute | solution.py:198
  14.3 0.0 collective-permute-done.10.refs_1_.refs_9_
  14.3 0.5 collective-permute-start.12
  14.8 1.4 %collective-permute-done.2.refs_3_ = bf16[128,512]{1,0:T(8,128)(2,1)S(1)} collective-permute-done((bf16[128,512]{1,0:T(8,128)(2,1)S(1)}, bf16[128,512]{1,0:T(8,128)(2,1)S(1)}, u32[]{:S(2)}, u32[]{:S(2)}) %collective-permute-start.2) | collective-permute-done | bytes 131104 | tf_op jit(solution)/shard_map/ppermute | solution.py:195
  16.2 0.0 collective-permute-done.4.refs_17_
  16.2 0.9 %collective-permute-start.5 = (bf16[128,512]{1,0:T(8,128)(2,1)S(1)}, bf16[128,512]{1,0:T(8,128)(2,1)S(1)}, u32[]{:S(2)}, u32[]{:S(2)}) collective-permute-start(bf16[128,512]{1,0:T(8,128)(2,1)S(1)} %collective-permute-done.2.refs_3_), channel_id=1, source_target_pairs={{0,2},{2,4},{4,6},{6,7},{7,5},{5,3},{3,1},{1,0},{8,10},{10,12},{12... | collective-permute-start | bytes 393224 | tf_op jit(solution)/shard_map/ppermute | solution.py:195
  17.1 0.0 collective-permute-done.13.refs_4_.refs_12_
  17.1 1.1 %collective-permute-start.15 = (bf16[128,512]{1,0:T(8,128)(2,1)S(1)}, bf16[128,512]{1,0:T(8,128)(2,1)S(1)}, u32[]{:S(2)}, u32[]{:S(2)}) collective-permute-start(bf16[128,512]{1,0:T(8,128)(2,1)S(1)} %collective-permute-done.13.refs_4_.refs_12_), channel_id=1, source_target_pairs={{2,0},{4,2},{6,4},{7,6},{5,7},{3,5},{1,3},{0,1},{10,8},{12,10},{14... | collective-permute-start | bytes 393224 | tf_op jit(solution)/shard_map/ppermute | solution.py:202
  18.3 1.6 %collective-permute-done.3.refs_4_ = bf16[128,512]{1,0:T(8,128)(2,1)S(1)} collective-permute-done((bf16[128,512]{1,0:T(8,128)(2,1)S(1)}, bf16[128,512]{1,0:T(8,128)(2,1)S(1)}, u32[]{:S(2)}, u32[]{:S(2)}) %collective-permute-start.3) | collective-permute-done | bytes 131104 | tf_op jit(solution)/shard_map/ppermute | solution.py:198
  19.9 1.1 %collective-permute-start.6 = (bf16[128,512]{1,0:T(8,128)(2,1)S(1)}, bf16[128,512]{1,0:T(8,128)(2,1)S(1)}, u32[]{:S(2)}, u32[]{:S(2)}) collective-permute-start(bf16[128,512]{1,0:T(8,128)(2,1)S(1)} %collective-permute-done.3.refs_4_), channel_id=1, source_target_pairs={{2,0},{4,2},{6,4},{7,6},{5,7},{3,5},{1,3},{0,1},{10,8},{12,10},{14... | collective-permute-start | bytes 393224 | tf_op jit(solution)/shard_map/ppermute | solution.py:198
  21.0 0.0 collective-permute-done.12.refs_3_.refs_11_
  21.0 0.9 %collective-permute-start.14 = (bf16[128,512]{1,0:T(8,128)(2,1)S(1)}, bf16[128,512]{1,0:T(8,128)(2,1)S(1)}, u32[]{:S(2)}, u32[]{:S(2)}) collective-permute-start(bf16[128,512]{1,0:T(8,128)(2,1)S(1)} %collective-permute-done.12.refs_3_.refs_11_), channel_id=1, source_target_pairs={{0,2},{2,4},{4,6},{6,7},{7,5},{5,3},{3,1},{1,0},{8,10},{10,12},{12... | collective-permute-start | bytes 393224 | tf_op jit(solution)/shard_map/ppermute | solution.py:200
  21.9 0.9 %collective-permute-done.15.refs_6_.refs_14_ = bf16[128,512]{1,0:T(8,128)(2,1)S(1)} collective-permute-done((bf16[128,512]{1,0:T(8,128)(2,1)S(1)}, bf16[128,512]{1,0:T(8,128)(2,1)S(1)}, u32[]{:S(2)}, u32[]{:S(2)}) %collective-permute-start.15) | collective-permute-done | bytes 131104 | tf_op jit(solution)/shard_map/ppermute | solution.py:202
  22.8 1.1 %collective-permute-start.16 = (bf16[128,512]{1,0:T(8,128)(2,1)S(1)}, bf16[128,512]{1,0:T(8,128)(2,1)S(1)}, u32[]{:S(2)}, u32[]{:S(2)}) collective-permute-start(bf16[128,512]{1,0:T(8,128)(2,1)S(1)} %collective-permute-done.15.refs_6_.refs_14_), channel_id=1, source_target_pairs={{2,0},{4,2},{6,4},{7,6},{5,7},{3,5},{1,3},{0,1},{10,8},{12,10},{14... | collective-permute-start | bytes 393224 | tf_op jit(solution)/shard_map/ppermute | solution.py:202
  23.8 0.0 collective-permute-done.5.refs_5_
  23.8 1.0 %collective-permute-start.7 = (bf16[128,512]{1,0:T(8,128)(2,1)S(1)}, bf16[128,512]{1,0:T(8,128)(2,1)S(1)}, u32[]{:S(2)}, u32[]{:S(2)}) collective-permute-start(bf16[128,512]{1,0:T(8,128)(2,1)S(1)} %collective-permute-done.5.refs_5_), channel_id=1, source_target_pairs={{0,2},{2,4},{4,6},{6,7},{7,5},{5,3},{3,1},{1,0},{8,10},{10,12},{12... | collective-permute-start | bytes 393224 | tf_op jit(solution)/shard_map/ppermute | solution.py:195
  24.8 0.2 compare_convert_fusion.hot_ref
  25.0 0.0 copy-start.3
  25.1 1.0 %collective-permute-done.14.refs_5_.refs_13_ = bf16[128,512]{1,0:T(8,128)(2,1)S(1)} collective-permute-done((bf16[128,512]{1,0:T(8,128)(2,1)S(1)}, bf16[128,512]{1,0:T(8,128)(2,1)S(1)}, u32[]{:S(2)}, u32[]{:S(2)}) %collective-permute-start.14) | collective-permute-done | bytes 131104 | tf_op jit(solution)/shard_map/ppermute | solution.py:200
  26.1 1.6 %collective-permute-done.16.refs_7_.refs_15_ = bf16[128,512]{1,0:T(8,128)(2,1)S(1)} collective-permute-done((bf16[128,512]{1,0:T(8,128)(2,1)S(1)}, bf16[128,512]{1,0:T(8,128)(2,1)S(1)}, u32[]{:S(2)}, u32[]{:S(2)}) %collective-permute-start.16) | collective-permute-done | bytes 131104 | tf_op jit(solution)/shard_map/ppermute | solution.py:202
  27.7 0.7 %select.13 = (bf16[256,512]{1,0:T(8,128)(2,1)S(1)}, bf16[256,512]{1,0:T(8,128)(2,1)S(1)}) custom-call(bf16[512,1024]{1,0:T(8,128)(2,1)S(1)} %compare_convert_fusion.hot_ref, bf16[128,512]{1,0:T(8,128)(2,1)S(1)} %get-tuple-element.41.refs_0_.refs_8_, bf16[128,512]{1,0:T(8,128)(2,1)S(1)} %collective-permute-done.10.refs_1_.refs_9_, ...), custom_call_target="tpu_custom_call" | custom-call | flops 1 | bytes 1 | tf_op jit(solution)/shard_map/select/pallas_call | solution.py:222
  28.5 0.0 copy-start.4
  28.5 0.1 collective-permute-start.17
  28.5 0.0 collective-permute-done.6.refs_6_
  28.6 0.3 collective-permute-done.7.refs_7_
  28.8 0.7 %select.12 = (bf16[256,512]{1,0:T(8,128)(2,1)S(1)}, bf16[256,512]{1,0:T(8,128)(2,1)S(1)}) custom-call(bf16[512,1024]{1,0:T(8,128)(2,1)S(1)} %compare_convert_fusion.hot_ref, bf16[128,512]{1,0:T(8,128)(2,1)S(1)} %get-tuple-element.34.refs_0_, bf16[128,512]{1,0:T(8,128)(2,1)S(1)} %collective-permute-done.refs_1_, ...), custom_call_target="tpu_custom_call" | custom-call | flops 1 | bytes 1 | tf_op jit(solution)/shard_map/select/pallas_call | solution.py:222
  29.5 0.3 collective-permute-start.8
  29.8 0.6 %fusion.1 = (f32[4,8,128]{2,1,0:T(8,128)}, f32[4096]{0:T(1024)S(1)}) fusion(s32[4096]{0:T(1024)S(1)} %copy-done.3), kind=kLoop, calls=%fused_computation.15 | loop fusion | flops 8192 | bytes 49152 | tf_op jit(solution)/shard_map/reshape | solution.py:258
  30.4 0.0 collective-permute-done.17.right
  30.5 0.0 copy-start.1
  30.5 1.3 %collective-permute-start.18 = (bf16[128,512]{1,0:T(8,128)(2,1)S(1)}, bf16[128,512]{1,0:T(8,128)(2,1)S(1)}, u32[]{:S(2)}, u32[]{:S(2)}) collective-permute-start(bf16[128,512]{1,0:T(8,128)(2,1)S(1)} %get-tuple-element.44), channel_id=1, source_target_pairs={{0,16},{8,24},{16,0},{24,8},{1,17},{9,25},{17,1},{25,9},{2,18},{10... | collective-permute-start | bytes 393224 | tf_op jit(solution)/shard_map/ppermute | solution.py:180
  31.9 0.8 %collective-permute-start.9 = (bf16[256,512]{1,0:T(8,128)(2,1)S(1)}, bf16[256,512]{1,0:T(8,128)(2,1)}, u32[]{:S(2)}, u32[]{:S(2)}) collective-permute-start(bf16[256,512]{1,0:T(8,128)(2,1)S(1)} %add.110.sum_a), channel_id=1, source_target_pairs={{0,16},{8,24},{16,0},{24,8},{1,17},{9,25},{17,1},{25,9},{2,18},{10... | collective-permute-start | bytes 786440 | tf_op jit(solution)/shard_map/ppermute | solution.py:180
  32.7 0.0 collective-permute-start.19
  32.7 0.5 %collective-permute-start.20 = (bf16[128,1024]{1,0:T(8,128)(2,1)S(1)}, bf16[128,1024]{1,0:T(8,128)(2,1)}, u32[]{:S(2)}, u32[]{:S(2)}) collective-permute-start(bf16[128,1024]{1,0:T(8,128)(2,1)S(1)} %collective-permute-done.4.refs_17_), channel_id=1, source_target_pairs={{0,8},{8,0},{16,24},{24,16},{1,9},{9,1},{17,25},{25,17},{2,10},{10... | collective-permute-start | bytes 786440 | tf_op jit(solution)/shard_map/ppermute | solution.py:180
  33.2 3.7 %collective-permute-done.18.mine = bf16[128,512]{1,0:T(8,128)(2,1)S(1)} collective-permute-done((bf16[128,512]{1,0:T(8,128)(2,1)S(1)}, bf16[128,512]{1,0:T(8,128)(2,1)S(1)}, u32[]{:S(2)}, u32[]{:S(2)}) %collective-permute-start.18) | collective-permute-done | bytes 131104 | tf_op jit(solution)/shard_map/ppermute | solution.py:180
  36.9 1.3 %collective-permute-start.21 = (bf16[128,512]{1,0:T(8,128)(2,1)S(1)}, bf16[128,512]{1,0:T(8,128)(2,1)}, u32[]{:S(2)}, u32[]{:S(2)}) collective-permute-start(bf16[128,512]{1,0:T(8,128)(2,1)S(1)} %collective-permute-done.18.mine), channel_id=1, source_target_pairs={{0,1},{1,0},{2,3},{3,2},{4,5},{5,4},{6,7},{7,6},{8,9},{9,8},{10,11... | collective-permute-start | bytes 393224 | tf_op jit(solution)/shard_map/ppermute | solution.py:249
  38.2 0.1 pad_add_fusion.1.cols_ref
  38.3 0.2 copy.6.kr_ref
  38.5 0.0 copy-start.2
  38.5 0.8 %dynamic-slice_bitcast_fusion.kc_ref = f32[1,512]{1,0:T(1,128)S(1)} fusion(f32[4,8,128]{2,1,0:T(8,128)} %get-tuple-element.65, s32[]{:T(128)S(6)} %select_n.54), kind=kLoop, calls=%fused_computation.6 | loop fusion | bytes 4100 | tf_op jit(solution)/shard_map/reshape | solution.py:258
  39.3 0.0 collective-permute-done.19.refs_18_
  39.3 3.0 %direct.1 = (bf16[1024,1024]{1,0:T(8,128)(2,1)S(1)}, bf16[512,1024]{1,0:T(8,128)(2,1)S(1)}, f32[1024,512]{1,0:T(8,128)S(1)}, f32[1024,512]{1,0:T(8,128)S(1)}) custom-call(s32[12]{0:T(128)S(1)} %pad_add_fusion.1.cols_ref, f32[1024,1]{1,0:T(8,128)S(1)} %copy.6.kr_ref, f32[1,512]{1,0:T(1,128)S(1)} %dynamic-slice_bitcast_fusion.kc_ref, ...), custom_call_target="tpu_custom_call" | custom-call | flops 1 | bytes 1 | tf_op jit(solution)/shard_map/direct/pallas_call | solution.py:265
  42.3 0.0 collective-permute-done.21.mate
  42.3 1.0 %merge.1 = (bf16[256,512]{1,0:T(8,128)(2,1)S(1)}, bf16[256,512]{1,0:T(8,128)(2,1)S(1)}) custom-call(s32[1]{0:T(128)} %bitcast.3.side_ref, bf16[256,512]{1,0:T(8,128)(2,1)S(1)} %add.110.sum_a, bf16[256,512]{1,0:T(8,128)(2,1)} %collective-permute-done.9.got_a, bf16[256,512]{1,0:T(8,128)(2,1)S(1)} %copy-done.2, ...), custom_call_target="tpu_custom_call" | custom-call | flops 1 | bytes 1 | tf_op jit(solution)/shard_map/merge/pallas_call | solution.py:282
  43.4 0.1 collective-permute-start.23
  43.5 0.5 %collective-permute-start.22 = (bf16[256,512]{1,0:T(8,128)(2,1)S(1)}, bf16[256,512]{1,0:T(8,128)(2,1)S(1)}, u32[]{:S(2)}, u32[]{:S(2)}) collective-permute-start(bf16[256,512]{1,0:T(8,128)(2,1)S(1)} %get-tuple-element.57.near), channel_id=1, source_target_pairs={{0,8},{8,0},{16,24},{24,16},{1,9},{9,1},{17,25},{25,17},{2,10},{10... | collective-permute-start | bytes 786440 | tf_op jit(solution)/shard_map/ppermute | solution.py:180
  44.0 1.0 %collective-permute-done.23.far = bf16[256,512]{1,0:T(8,128)(2,1)S(1)} collective-permute-done((bf16[256,512]{1,0:T(8,128)(2,1)S(1)}, bf16[256,512]{1,0:T(8,128)(2,1)S(1)}, u32[]{:S(2)}, u32[]{:S(2)}) %collective-permute-start.23) | collective-permute-done | bytes 262176 | tf_op jit(solution)/shard_map/ppermute | solution.py:180
  45.0 1.0 %partial.1 = (f32[1024,512]{1,0:T(8,128)S(1)}, f32[512,512]{1,0:T(8,128)S(1)}) custom-call(bf16[1024,1024]{1,0:T(8,128)(2,1)S(1)} %get-tuple-element.51.zr, bf16[512,1024]{1,0:T(8,128)(2,1)S(1)} %get-tuple-element.52.zc, bf16[256,512]{1,0:T(8,128)(2,1)S(1)} %get-tuple-element.58.near, bf16[256,512]{1,0:T(8,128)(2,1)S(1)} %collective-permute-done.23.far), custom_call_target="tpu_custom_call" | custom-call | flops 1 | bytes 1 | tf_op jit(solution)/shard_map/partial/pallas_call | solution.py:292
  46.0 3.1 %final.1 = f32[1024,512]{1,0:T(8,128)} custom-call(bf16[1024,1024]{1,0:T(8,128)(2,1)S(1)} %get-tuple-element.51.zr, bf16[512,1024]{1,0:T(8,128)(2,1)S(1)} %get-tuple-element.52.zc, bf16[256,512]{1,0:T(8,128)(2,1)S(1)} %get-tuple-element.57.near, bf16[256,512]{1,0:T(8,128)(2,1)S(1)} %collective-permute-done.22.far, ...), custom_call_target="tpu_custom_call" | custom-call | flops 1 | bytes 1 | tf_op jit(solution)/shard_map/final/pallas_call | solution.py:301
  (15 shorter events, 0.1 us)
Async XLA Ops:
  0.0 1.0 %copy-start = (f32[128,1024]{1,0:T(8,128)S(1)}, f32[128,1024]{1,0:T(8,128)}, u32[]{:S(2)}) copy-start(f32[128,1024]{1,0:T(8,128)} %x_ref.1) | copy-start | bytes 1572868
  1.3 11.4 %collective-permute-start.1 = (bf16[128,512]{1,0:T(8,128)(2,1)S(1)}, bf16[128,512]{1,0:T(8,128)(2,1)S(1)}, u32[]{:S(2)}, u32[]{:S(2)}) collective-permute-start(bf16[128,512]{1,0:T(8,128)(2,1)S(1)} %get-tuple-element.34.refs_0_), channel_id=1, source_target_pairs={{2,0},{4,2},{6,4},{7,6},{5,7},{3,5},{1,3},{0,1},{10,8},{12,10},{14... | collective-permute-start | bytes 393224 | tf_op jit(solution)/shard_map/ppermute | solution.py:198
  4.3 6.3 %collective-permute-start = (bf16[128,512]{1,0:T(8,128)(2,1)S(1)}, bf16[128,512]{1,0:T(8,128)(2,1)S(1)}, u32[]{:S(2)}, u32[]{:S(2)}) collective-permute-start(bf16[128,512]{1,0:T(8,128)(2,1)S(1)} %get-tuple-element.34.refs_0_), channel_id=1, source_target_pairs={{0,2},{2,4},{4,6},{6,7},{7,5},{5,3},{3,1},{1,0},{8,10},{10,12},{12... | collective-permute-start | bytes 393224 | tf_op jit(solution)/shard_map/ppermute | solution.py:195
  4.4 6.9 %collective-permute-start.11 = (bf16[128,512]{1,0:T(8,128)(2,1)S(1)}, bf16[128,512]{1,0:T(8,128)(2,1)S(1)}, u32[]{:S(2)}, u32[]{:S(2)}) collective-permute-start(bf16[128,512]{1,0:T(8,128)(2,1)S(1)} %get-tuple-element.41.refs_0_.refs_8_), channel_id=1, source_target_pairs={{2,0},{4,2},{6,4},{7,6},{5,7},{3,5},{1,3},{0,1},{10,8},{12,10},{14... | collective-permute-start | bytes 393224 | tf_op jit(solution)/shard_map/ppermute | solution.py:202
  6.3 8.0 %collective-permute-start.10 = (bf16[128,512]{1,0:T(8,128)(2,1)S(1)}, bf16[128,512]{1,0:T(8,128)(2,1)S(1)}, u32[]{:S(2)}, u32[]{:S(2)}) collective-permute-start(bf16[128,512]{1,0:T(8,128)(2,1)S(1)} %get-tuple-element.41.refs_0_.refs_8_), channel_id=1, source_target_pairs={{0,2},{2,4},{4,6},{6,7},{7,5},{5,3},{3,1},{1,0},{8,10},{10,12},{12... | collective-permute-start | bytes 393224 | tf_op jit(solution)/shard_map/ppermute | solution.py:200
  6.5 9.8 %collective-permute-start.4 = (bf16[128,1024]{1,0:T(8,128)(2,1)S(1)}, bf16[128,1024]{1,0:T(8,128)(2,1)S(1)}, u32[]{:S(2)}, u32[]{:S(2)}) collective-permute-start(bf16[128,1024]{1,0:T(8,128)(2,1)S(1)} %get-tuple-element.45.refs_16_), channel_id=1, source_target_pairs={{0,16},{8,24},{16,0},{24,8},{1,17},{9,25},{17,1},{25,9},{2,18},{10... | collective-permute-start | bytes 786440 | tf_op jit(solution)/shard_map/ppermute | solution.py:180
  10.6 5.6 %collective-permute-start.2 = (bf16[128,512]{1,0:T(8,128)(2,1)S(1)}, bf16[128,512]{1,0:T(8,128)(2,1)S(1)}, u32[]{:S(2)}, u32[]{:S(2)}) collective-permute-start(bf16[128,512]{1,0:T(8,128)(2,1)S(1)} %collective-permute-done.refs_1_), channel_id=1, source_target_pairs={{0,2},{2,4},{4,6},{6,7},{7,5},{5,3},{3,1},{1,0},{8,10},{10,12},{12... | collective-permute-start | bytes 393224 | tf_op jit(solution)/shard_map/ppermute | solution.py:195
  11.3 5.8 %collective-permute-start.13 = (bf16[128,512]{1,0:T(8,128)(2,1)S(1)}, bf16[128,512]{1,0:T(8,128)(2,1)S(1)}, u32[]{:S(2)}, u32[]{:S(2)}) collective-permute-start(bf16[128,512]{1,0:T(8,128)(2,1)S(1)} %collective-permute-done.11.refs_2_.refs_10_), channel_id=1, source_target_pairs={{2,0},{4,2},{6,4},{7,6},{5,7},{3,5},{1,3},{0,1},{10,8},{12,10},{14... | collective-permute-start | bytes 393224 | tf_op jit(solution)/shard_map/ppermute | solution.py:202
  12.7 7.2 %collective-permute-start.3 = (bf16[128,512]{1,0:T(8,128)(2,1)S(1)}, bf16[128,512]{1,0:T(8,128)(2,1)S(1)}, u32[]{:S(2)}, u32[]{:S(2)}) collective-permute-start(bf16[128,512]{1,0:T(8,128)(2,1)S(1)} %collective-permute-done.1.refs_2_), channel_id=1, source_target_pairs={{2,0},{4,2},{6,4},{7,6},{5,7},{3,5},{1,3},{0,1},{10,8},{12,10},{14... | collective-permute-start | bytes 393224 | tf_op jit(solution)/shard_map/ppermute | solution.py:198
  14.3 6.7 %collective-permute-start.12 = (bf16[128,512]{1,0:T(8,128)(2,1)S(1)}, bf16[128,512]{1,0:T(8,128)(2,1)S(1)}, u32[]{:S(2)}, u32[]{:S(2)}) collective-permute-start(bf16[128,512]{1,0:T(8,128)(2,1)S(1)} %collective-permute-done.10.refs_1_.refs_9_), channel_id=1, source_target_pairs={{0,2},{2,4},{4,6},{6,7},{7,5},{5,3},{3,1},{1,0},{8,10},{10,12},{12... | collective-permute-start | bytes 393224 | tf_op jit(solution)/shard_map/ppermute | solution.py:200
  16.2 7.6 %collective-permute-start.5 = (bf16[128,512]{1,0:T(8,128)(2,1)S(1)}, bf16[128,512]{1,0:T(8,128)(2,1)S(1)}, u32[]{:S(2)}, u32[]{:S(2)}) collective-permute-start(bf16[128,512]{1,0:T(8,128)(2,1)S(1)} %collective-permute-done.2.refs_3_), channel_id=1, source_target_pairs={{0,2},{2,4},{4,6},{6,7},{7,5},{5,3},{3,1},{1,0},{8,10},{10,12},{12... | collective-permute-start | bytes 393224 | tf_op jit(solution)/shard_map/ppermute | solution.py:195
  17.1 5.6 %collective-permute-start.15 = (bf16[128,512]{1,0:T(8,128)(2,1)S(1)}, bf16[128,512]{1,0:T(8,128)(2,1)S(1)}, u32[]{:S(2)}, u32[]{:S(2)}) collective-permute-start(bf16[128,512]{1,0:T(8,128)(2,1)S(1)} %collective-permute-done.13.refs_4_.refs_12_), channel_id=1, source_target_pairs={{2,0},{4,2},{6,4},{7,6},{5,7},{3,5},{1,3},{0,1},{10,8},{12,10},{14... | collective-permute-start | bytes 393224 | tf_op jit(solution)/shard_map/ppermute | solution.py:202
  19.9 8.7 %collective-permute-start.6 = (bf16[128,512]{1,0:T(8,128)(2,1)S(1)}, bf16[128,512]{1,0:T(8,128)(2,1)S(1)}, u32[]{:S(2)}, u32[]{:S(2)}) collective-permute-start(bf16[128,512]{1,0:T(8,128)(2,1)S(1)} %collective-permute-done.3.refs_4_), channel_id=1, source_target_pairs={{2,0},{4,2},{6,4},{7,6},{5,7},{3,5},{1,3},{0,1},{10,8},{12,10},{14... | collective-permute-start | bytes 393224 | tf_op jit(solution)/shard_map/ppermute | solution.py:198
  21.0 5.1 %collective-permute-start.14 = (bf16[128,512]{1,0:T(8,128)(2,1)S(1)}, bf16[128,512]{1,0:T(8,128)(2,1)S(1)}, u32[]{:S(2)}, u32[]{:S(2)}) collective-permute-start(bf16[128,512]{1,0:T(8,128)(2,1)S(1)} %collective-permute-done.12.refs_3_.refs_11_), channel_id=1, source_target_pairs={{0,2},{2,4},{4,6},{6,7},{7,5},{5,3},{3,1},{1,0},{8,10},{10,12},{12... | collective-permute-start | bytes 393224 | tf_op jit(solution)/shard_map/ppermute | solution.py:200
  22.8 5.0 %collective-permute-start.16 = (bf16[128,512]{1,0:T(8,128)(2,1)S(1)}, bf16[128,512]{1,0:T(8,128)(2,1)S(1)}, u32[]{:S(2)}, u32[]{:S(2)}) collective-permute-start(bf16[128,512]{1,0:T(8,128)(2,1)S(1)} %collective-permute-done.15.refs_6_.refs_14_), channel_id=1, source_target_pairs={{2,0},{4,2},{6,4},{7,6},{5,7},{3,5},{1,3},{0,1},{10,8},{12,10},{14... | collective-permute-start | bytes 393224 | tf_op jit(solution)/shard_map/ppermute | solution.py:202
  23.8 5.0 %collective-permute-start.7 = (bf16[128,512]{1,0:T(8,128)(2,1)S(1)}, bf16[128,512]{1,0:T(8,128)(2,1)S(1)}, u32[]{:S(2)}, u32[]{:S(2)}) collective-permute-start(bf16[128,512]{1,0:T(8,128)(2,1)S(1)} %collective-permute-done.5.refs_5_), channel_id=1, source_target_pairs={{0,2},{2,4},{4,6},{6,7},{7,5},{5,3},{3,1},{1,0},{8,10},{10,12},{12... | collective-permute-start | bytes 393224 | tf_op jit(solution)/shard_map/ppermute | solution.py:195
  25.0 4.8 %copy-start.3 = (s32[4096]{0:T(1024)S(1)}, s32[4096]{0:T(1024)}, u32[]{:S(2)}) copy-start(s32[4096]{0:T(1024)} %param.7) | copy-start | bytes 49156
  28.5 4.8 %copy-start.4 = (s32[4]{0:T(128)S(1)}, s32[4]{0:T(128)}, u32[]{:S(2)}) copy-start(s32[4]{0:T(128)} %constant.87.clone) | copy-start | bytes 52
  28.5 2.0 %collective-permute-start.17 = (bf16[256,512]{1,0:T(8,128)(2,1)S(1)}, bf16[256,512]{1,0:T(8,128)(2,1)S(1)}, u32[]{:S(2)}, u32[]{:S(2)}) collective-permute-start(bf16[256,512]{1,0:T(8,128)(2,1)S(1)} %get-tuple-element.43), channel_id=1, source_target_pairs={{0,8},{8,0},{16,24},{24,16},{1,9},{9,1},{17,25},{25,17},{2,10},{10... | collective-permute-start | bytes 786440 | tf_op jit(solution)/shard_map/ppermute | solution.py:180
  29.5 2.3 %collective-permute-start.8 = (bf16[256,512]{1,0:T(8,128)(2,1)S(1)}, bf16[256,512]{1,0:T(8,128)(2,1)S(1)}, u32[]{:S(2)}, u32[]{:S(2)}) collective-permute-start(bf16[256,512]{1,0:T(8,128)(2,1)S(1)} %get-tuple-element.38), channel_id=1, source_target_pairs={{0,8},{8,0},{16,24},{24,16},{1,9},{9,1},{17,25},{25,17},{2,10},{10... | collective-permute-start | bytes 786440 | tf_op jit(solution)/shard_map/ppermute | solution.py:180
  30.5 2.2 %copy-start.1 = (bf16[256,512]{1,0:T(8,128)(2,1)}, bf16[256,512]{1,0:T(8,128)(2,1)S(1)}, u32[]{:S(2)}) copy-start(bf16[256,512]{1,0:T(8,128)(2,1)S(1)} %get-tuple-element.54.sum_b) | copy-start | bytes 786436
  30.5 6.4 %collective-permute-start.18 = (bf16[128,512]{1,0:T(8,128)(2,1)S(1)}, bf16[128,512]{1,0:T(8,128)(2,1)S(1)}, u32[]{:S(2)}, u32[]{:S(2)}) collective-permute-start(bf16[128,512]{1,0:T(8,128)(2,1)S(1)} %get-tuple-element.44), channel_id=1, source_target_pairs={{0,16},{8,24},{16,0},{24,8},{1,17},{9,25},{17,1},{25,9},{2,18},{10... | collective-permute-start | bytes 393224 | tf_op jit(solution)/shard_map/ppermute | solution.py:180
  31.9 10.4 %collective-permute-start.9 = (bf16[256,512]{1,0:T(8,128)(2,1)S(1)}, bf16[256,512]{1,0:T(8,128)(2,1)}, u32[]{:S(2)}, u32[]{:S(2)}) collective-permute-start(bf16[256,512]{1,0:T(8,128)(2,1)S(1)} %add.110.sum_a), channel_id=1, source_target_pairs={{0,16},{8,24},{16,0},{24,8},{1,17},{9,25},{17,1},{25,9},{2,18},{10... | collective-permute-start | bytes 786440 | tf_op jit(solution)/shard_map/ppermute | solution.py:180
  32.7 6.6 %collective-permute-start.19 = (bf16[128,1024]{1,0:T(8,128)(2,1)S(1)}, bf16[128,1024]{1,0:T(8,128)(2,1)}, u32[]{:S(2)}, u32[]{:S(2)}) collective-permute-start(bf16[128,1024]{1,0:T(8,128)(2,1)S(1)} %get-tuple-element.45.refs_16_), channel_id=1, source_target_pairs={{0,8},{8,0},{16,24},{24,16},{1,9},{9,1},{17,25},{25,17},{2,10},{10... | collective-permute-start | bytes 786440 | tf_op jit(solution)/shard_map/ppermute | solution.py:180
  32.7 6.6 %collective-permute-start.20 = (bf16[128,1024]{1,0:T(8,128)(2,1)S(1)}, bf16[128,1024]{1,0:T(8,128)(2,1)}, u32[]{:S(2)}, u32[]{:S(2)}) collective-permute-start(bf16[128,1024]{1,0:T(8,128)(2,1)S(1)} %collective-permute-done.4.refs_17_), channel_id=1, source_target_pairs={{0,8},{8,0},{16,24},{24,16},{1,9},{9,1},{17,25},{25,17},{2,10},{10... | collective-permute-start | bytes 786440 | tf_op jit(solution)/shard_map/ppermute | solution.py:180
  36.9 5.4 %collective-permute-start.21 = (bf16[128,512]{1,0:T(8,128)(2,1)S(1)}, bf16[128,512]{1,0:T(8,128)(2,1)}, u32[]{:S(2)}, u32[]{:S(2)}) collective-permute-start(bf16[128,512]{1,0:T(8,128)(2,1)S(1)} %collective-permute-done.18.mine), channel_id=1, source_target_pairs={{0,1},{1,0},{2,3},{3,2},{4,5},{5,4},{6,7},{7,6},{8,9},{9,8},{10,11... | collective-permute-start | bytes 393224 | tf_op jit(solution)/shard_map/ppermute | solution.py:249
  38.5 3.8 %copy-start.2 = (bf16[256,512]{1,0:T(8,128)(2,1)S(1)}, bf16[256,512]{1,0:T(8,128)(2,1)}, u32[]{:S(2)}) copy-start(bf16[256,512]{1,0:T(8,128)(2,1)} %copy-done.1) | copy-start | bytes 786436
  43.4 1.6 %collective-permute-start.23 = (bf16[256,512]{1,0:T(8,128)(2,1)S(1)}, bf16[256,512]{1,0:T(8,128)(2,1)S(1)}, u32[]{:S(2)}, u32[]{:S(2)}) collective-permute-start(bf16[256,512]{1,0:T(8,128)(2,1)S(1)} %get-tuple-element.58.near), channel_id=1, source_target_pairs={{0,8},{8,0},{16,24},{24,16},{1,9},{9,1},{17,25},{25,17},{2,10},{10... | collective-permute-start | bytes 786440 | tf_op jit(solution)/shard_map/ppermute | solution.py:180
  43.5 2.5 %collective-permute-start.22 = (bf16[256,512]{1,0:T(8,128)(2,1)S(1)}, bf16[256,512]{1,0:T(8,128)(2,1)S(1)}, u32[]{:S(2)}, u32[]{:S(2)}) collective-permute-start(bf16[256,512]{1,0:T(8,128)(2,1)S(1)} %get-tuple-element.57.near), channel_id=1, source_target_pairs={{0,8},{8,0},{16,24},{24,16},{1,9},{9,1},{17,25},{25,17},{2,10},{10... | collective-permute-start | bytes 786440 | tf_op jit(solution)/shard_map/ppermute | solution.py:180

commit v4 on v3

--- a/solution.py
+++ b/solution.py
@@ -80,25 +80,30 @@
         share[rows, :] = direct * inv
 
 
-def partial_kernel(zr, zc, near, far, row_part, col_part):
-    wa = near.shape[1]
-    zp = jnp.concatenate([near[...], far[...]], axis=0)
-    row_part[...] = dot_t(zr[:, :wa], zp)
-    col_part[...] = dot_t(zc[:, :wa], zp)
-
-
-def final_kernel(zr, zc, near, far, row_part, col_part, inverse, share, out_ref, stage, sems):
+def products(left, pa, pb):
+    wa = pa.shape[1]
+    return dot_t(left[:, :wa], pa[...]) + dot_t(left[:, wa:], pb[...])
+
+
+def partial_kernel(zr, zc, pa, pb, row_part, col_part):
+    row_part[...] = products(zr[...], pa, pb)
+    col_part[...] = products(zc[...], pa, pb)
+
+
+def final_kernel(zr, zc, pa, pb, row_part, col_part, inverse, share, out_ref, stage, sems):
     height, samples = zr.shape
-    wa = samples - near.shape[1]
-    zp = jnp.concatenate([near[...], far[...]], axis=0)
-    acol = power6(col_part[...] + dot_t(zc[:, wa:], zp), samples).astype(jnp.bfloat16)
+
+    def both(part, left):
+        product = jnp.concatenate([part, products(left, pa, pb)], axis=1)
+        return power6(product, samples).astype(jnp.bfloat16)
+
+    acol = both(col_part[...], zc[...])
     count = sems.shape[0]
     block = height // count
     copies = []
     for b in range(count):
         rows = slice(b * block, (b + 1) * block)
-        product = row_part[rows, :] + dot_t(zr[rows, wa:], zp)
-        arow = power6(product, samples).astype(jnp.bfloat16)
+        arow = both(row_part[rows, :], zr[rows, :])
         stage[rows, :] = dot_t(arow, acol) * inverse[rows, :] + share[rows, :]
         copy = pltpu.make_async_copy(
             stage.at[rows, :], out_ref.at[rows, :], sems.at[b]
@@ -184,6 +189,10 @@
     offsets = [0]
     for s in range(1, n // 2 + 1):
         offsets += [-s, s] if s < n // 2 else [s]
+    height = n * local
+    scale = degrees.astype(jnp.float32) * (1.0 / 1024.0)
+    kc = lax.dynamic_index_in_dim(scale.reshape(n_rows, n, local), c, 1, False).reshape(1, -1)
+    kr = lax.dynamic_slice_in_dim(scale, r * height, height, 0).reshape(-1, 1)
     fa, ba, fb, bb = za, za, zb, zb
     list_a, list_b = [za], [zb]
     top = n_rows // 2
@@ -191,7 +200,7 @@
     for s in range(1, n // 2 + 1):
         last = s == n // 2
         if s == n // 2 - 1:
-            fa, across = lax.optimization_barrier((fa, across))
+            fb, across, kr, kc = lax.optimization_barrier((fb, across, kr, kc))
         fa = lax.ppermute(fa, "cols", forward)
         list_a.append(fa)
         if not last:
@@ -206,6 +215,8 @@
     spots = (place + jnp.array(offsets, jnp.int32)) % n
     columns = jnp.where(spots < n // 2, 2 * spots, 2 * (n - 1 - spots) + 1)
     ids = ((r * n + columns)[:, None] * local + jnp.arange(local, dtype=jnp.int32)).reshape(-1)
+    gathered = lax.optimization_barrier((*list_a, *list_b))
+    list_a, list_b = gathered[:n], gathered[n:]
     half = pivots.shape[0] // 2
     side = r % 2
     split = pivots.reshape(2, half)
@@ -254,10 +265,6 @@
         masks += [q ^ mask for q in masks]
         mask //= 2
 
-    scale = degrees.astype(jnp.float32) * (1.0 / 1024.0)
-    kc = lax.dynamic_index_in_dim(scale.reshape(n_rows, n, local), c, 1, False).reshape(1, -1)
-    height = n * local
-    kr = lax.dynamic_slice_in_dim(scale, r * height, height, 0).reshape(-1, 1)
     where = jnp.concatenate([columns, jnp.array(masks, jnp.int32) ^ r])
     width = n_rows * local
     f32 = jnp.float32
@@ -288,16 +295,16 @@
         cost_estimate=CHEAP,
         name="merge",
     )(parity, sum_a, got_a, sum_b, got_b, mate_b)
-    pa, pb = (total_a, flip(total_a, 1)), (total_b, flip(total_b, 1))
+    far_a, far_b = flip(total_a, 1), flip(total_b, 1)
     row_part, col_part = pl.pallas_call(
         partial_kernel,
-        out_shape=[shape((height, 2 * half), f32), shape((width, 2 * half), f32)],
+        out_shape=[shape((height, half), f32), shape((width, half), f32)],
         in_specs=[VMEM] * 4,
         out_specs=[VMEM] * 2,
         compiler_params=params(8),
         cost_estimate=CHEAP,
         name="partial",
-    )(zr, zc, *pa)
+    )(zr, zc, total_a, total_b)
     return pl.pallas_call(
         final_kernel,
         out_shape=shape((height, width), f32),
@@ -307,7 +314,7 @@
         compiler_params=params(16),
         cost_estimate=CHEAP,
         name="final",
-    )(zr, zc, *pb, row_part, col_part, inverse, share)
+    )(zr, zc, far_a, far_b, row_part, col_part, inverse, share)
 
 
 def solution(mesh):

time: 49.3 us -> 48.4 us (0.982)
  starting transfers between devices: 22.1 us -> 23.1 us
  waiting for transfers between devices: 12.5 us -> 11.6 us
  local copies, waits for them, and re-layouts: 2.77 us -> 1.99 us
    ppermute x4, starting transfers between devices: 2.68 us -> 7.05 us  [per_device(): fa = lax.ppermute(fa, 'cols', forward)]
    ppermute x4, starting transfers between devices: 5.43 us -> 2.46 us  [per_device(): bb = lax.ppermute(bb, 'cols', backward)]
    ppermute x3, starting transfers between devices: 5.7 us -> 3.1 us  [per_device(): ba = lax.ppermute(ba, 'cols', backward)]
    ppermute x3, starting transfers between devices: 1.49 us -> 2.92 us  [per_device(): fb = lax.ppermute(fb, 'cols', forward)]
    ppermute x9, waiting for transfers between devices: 4.7 us -> 3.91 us  [per_device(): lax.ppermute(v, 'rows', [(i, i ^ mask) for i in range(n_rows)])]
    reshape x1, local copies, waits for them, and re-layouts: 0.77 us -> 0.01 us  [per_device(): lax.dynamic_index_in_dim(scale.reshape(n_rows, n, local), c, 1, False)]
    ppermute x9, starting transfers between devices: 5.51 us -> 6.23 us  [per_device(): lax.ppermute(v, 'rows', [(i, i ^ mask) for i in range(n_rows)])]
    unnamed x10 -> x8, local copies, waits for them, and re-layouts: 1.07 us -> 1.06 us
  transfers between devices with their start and end apart: 24 -> 24, of which waited for: 9 -> 13; matrix products, arithmetic and copies ran while one was open for 7% -> 6% of each run, Pallas kernels for 11% -> 10%
where the time goes in v4:
time: 48.4 us; the launch traced here: 48.2 us
  starting transfers between devices  23.1 us (48%)
  waiting for transfers between devices  11.6 us (24%)
  Pallas kernels  9.55 us (20%)
  local copies, waits for them, and re-layouts  1.99 us (4%)
  other arithmetic  1.78 us (4%)
    ppermute x4, starting transfers between devices, per_device(): fa = lax.ppermute(fa, 'cols', forward)  7.05 us
    ppermute x9, starting transfers between devices, per_device(): lax.ppermute(v, 'rows', [(i, i ^ mask) for i in range(n_rows)])  6.23 us
    ppermute x9, waiting for transfers between devices, per_device(): lax.ppermute(v, 'rows', [(i, i ^ mask) for i in range(n_rows)])  3.91 us
    ppermute x3, starting transfers between devices, per_device(): ba = lax.ppermute(ba, 'cols', backward)  3.1 us
    pallas_call x1, Pallas kernels, per_device(): pl.pallas_call(functools.partial(direct_kernel, n, n_rows), out_shape=[sh...  3.02 us
    ppermute x3, starting transfers between devices, per_device(): fb = lax.ppermute(fb, 'cols', forward)  2.92 us
    pallas_call x1, Pallas kernels, per_device(): pl.pallas_call(final_kernel, out_shape=shape((height, width), f32), in_sp...  2.75 us
    ppermute x4, waiting for transfers between devices, per_device(): bb = lax.ppermute(bb, 'cols', backward)  2.49 us
  transfers between devices with their start and end apart: 24, of which 13 were waited for; matrix products, arithmetic and copies ran while one was open for 6% of the time, Pallas kernels for 10%

profile of v4, /device:TPU:0, one launch (start us, length us, event | category | flops | bytes accessed | tf_op | source)
XLA Modules:
  0.0 48.2 jit_solution(7180564784506232317)
XLA Ops:
  0.0 1.0 %copy-done = f32[128,1024]{1,0:T(8,128)S(1)} copy-done((f32[128,1024]{1,0:T(8,128)S(1)}, f32[128,1024]{1,0:T(8,128)}, u32[]{:S(2)}) %copy-start) | copy-done | bytes 524312
  1.0 0.2 standardize.1
  1.3 3.1 %collective-permute-start = (bf16[128,512]{1,0:T(8,128)(2,1)S(1)}, bf16[128,512]{1,0:T(8,128)(2,1)S(1)}, u32[]{:S(2)}, u32[]{:S(2)}) collective-permute-start(bf16[128,512]{1,0:T(8,128)(2,1)S(1)} %get-tuple-element.56.refs_0_), channel_id=1, source_target_pairs={{0,2},{2,4},{4,6},{6,7},{7,5},{5,3},{3,1},{1,0},{8,10},{10,12},{12... | collective-permute-start | bytes 393224 | tf_op jit(solution)/shard_map/ppermute | solution.py:204
  4.4 0.0 collective-permute-start.1
  4.4 2.0 %collective-permute-start.7 = (bf16[128,512]{1,0:T(8,128)(2,1)S(1)}, bf16[128,512]{1,0:T(8,128)(2,1)S(1)}, u32[]{:S(2)}, u32[]{:S(2)}) collective-permute-start(bf16[128,512]{1,0:T(8,128)(2,1)S(1)} %get-tuple-element.68.refs_0_.refs_8_), channel_id=1, source_target_pairs={{0,2},{2,4},{4,6},{6,7},{7,5},{5,3},{3,1},{1,0},{8,10},{10,12},{12... | collective-permute-start | bytes 393224 | tf_op jit(solution)/shard_map/ppermute | solution.py:209
  6.4 0.0 collective-permute-start.8
  6.4 1.9 %collective-permute-start.11 = (bf16[128,1024]{1,0:T(8,128)(2,1)S(1)}, bf16[128,1024]{1,0:T(8,128)(2,1)S(1)}, u32[]{:S(2)}, u32[]{:S(2)}) collective-permute-start(bf16[128,1024]{1,0:T(8,128)(2,1)S(1)} %get-tuple-element.81.refs_16_), channel_id=1, source_target_pairs={{0,16},{8,24},{16,0},{24,8},{1,17},{9,25},{17,1},{25,9},{2,18},{10... | collective-permute-start | bytes 786440 | tf_op jit(solution)/shard_map/ppermute | solution.py:185
  8.3 0.7 %fusion.1 = (f32[4,8,128]{2,1,0:T(8,128)S(1)}, f32[4096]{0:T(1024)S(1)}) fusion(s32[4096]{0:T(1024)} %param.7), kind=kLoop, calls=%fused_computation.15 | loop fusion | flops 8192 | bytes 49152 | tf_op jit(solution)/shard_map/reshape | solution.py:194
  9.1 0.7 %add_multiply_fusion = (s32[8]{0:T(128)S(1)}, s32[8]{0:T(128)S(1)}) fusion(s32[]{:T(128)S(6)} %mul.22, s32[8]{0:T(128)} %constant.86.clone, s32[]{:T(128)S(6)} %select_n.50), kind=kLoop, calls=%fused_computation.13 | loop fusion | flops 160 | bytes 104 | tf_op jit(solution)/shard_map/mul | solution.py:217
  9.7 0.0 collective-permute-done.refs_1_
  9.7 1.6 %collective-permute-start.2 = (bf16[128,512]{1,0:T(8,128)(2,1)S(1)}, bf16[128,512]{1,0:T(8,128)(2,1)S(1)}, u32[]{:S(2)}, u32[]{:S(2)}) collective-permute-start(bf16[128,512]{1,0:T(8,128)(2,1)S(1)} %collective-permute-done.refs_1_), channel_id=1, source_target_pairs={{0,2},{2,4},{4,6},{6,7},{7,5},{5,3},{3,1},{1,0},{8,10},{10,12},{12... | collective-permute-start | bytes 393224 | tf_op jit(solution)/shard_map/ppermute | solution.py:204
  11.4 0.8 %collective-permute-done.8.refs_2_.refs_10_ = bf16[128,512]{1,0:T(8,128)(2,1)S(1)} collective-permute-done((bf16[128,512]{1,0:T(8,128)(2,1)S(1)}, bf16[128,512]{1,0:T(8,128)(2,1)S(1)}, u32[]{:S(2)}, u32[]{:S(2)}) %collective-permute-start.8) | collective-permute-done | bytes 131104 | tf_op jit(solution)/shard_map/ppermute | solution.py:211
  12.1 0.3 collective-permute-start.10
  12.4 0.1 add_bitcast_fusion
  12.5 0.7 %reshape.33 = s32[2,256]{1,0:T(2,128)S(1)} reshape(s32[512]{0:T(512)} %param.6) | data formatting | bytes 4096 | tf_op jit(solution)/shard_map/reshape | solution.py:222
  13.2 0.0 collective-permute-done.1.refs_2_
  13.2 1.7 %collective-permute-start.3 = (bf16[128,512]{1,0:T(8,128)(2,1)S(1)}, bf16[128,512]{1,0:T(8,128)(2,1)S(1)}, u32[]{:S(2)}, u32[]{:S(2)}) collective-permute-start(bf16[128,512]{1,0:T(8,128)(2,1)S(1)} %collective-permute-done.1.refs_2_), channel_id=1, source_target_pairs={{2,0},{4,2},{6,4},{7,6},{5,7},{3,5},{1,3},{0,1},{10,8},{12,10},{14... | collective-permute-start | bytes 393224 | tf_op jit(solution)/shard_map/ppermute | solution.py:207
  14.9 0.0 collective-permute-done.7.refs_1_.refs_9_
  14.9 0.3 collective-permute-start.9
  15.3 0.0 collective-permute-done.2.refs_3_
  15.3 1.7 %collective-permute-start.4 = (bf16[128,512]{1,0:T(8,128)(2,1)S(1)}, bf16[128,512]{1,0:T(8,128)(2,1)S(1)}, u32[]{:S(2)}, u32[]{:S(2)}) collective-permute-start(bf16[128,512]{1,0:T(8,128)(2,1)S(1)} %collective-permute-done.2.refs_3_), channel_id=1, source_target_pairs={{0,2},{2,4},{4,6},{6,7},{7,5},{5,3},{3,1},{1,0},{8,10},{10,12},{12... | collective-permute-start | bytes 393224 | tf_op jit(solution)/shard_map/ppermute | solution.py:204
  17.0 0.8 %collective-permute-done.10.refs_4_.refs_12_ = bf16[128,512]{1,0:T(8,128)(2,1)S(1)} collective-permute-done((bf16[128,512]{1,0:T(8,128)(2,1)S(1)}, bf16[128,512]{1,0:T(8,128)(2,1)S(1)}, u32[]{:S(2)}, u32[]{:S(2)}) %collective-permute-start.10) | collective-permute-done | bytes 131104 | tf_op jit(solution)/shard_map/ppermute | solution.py:211
  17.9 0.9 %collective-permute-start.13 = (bf16[128,512]{1,0:T(8,128)(2,1)S(1)}, bf16[128,512]{1,0:T(8,128)(2,1)S(1)}, u32[]{:S(2)}, u32[]{:S(2)}) collective-permute-start(bf16[128,512]{1,0:T(8,128)(2,1)S(1)} %collective-permute-done.10.refs_4_.refs_12_), channel_id=1, source_target_pairs={{2,0},{4,2},{6,4},{7,6},{5,7},{3,5},{1,3},{0,1},{10,8},{12,10},{14... | collective-permute-start | bytes 393224 | tf_op jit(solution)/shard_map/ppermute | solution.py:211
  18.8 1.2 %collective-permute-done.9.refs_3_.refs_11_ = bf16[128,512]{1,0:T(8,128)(2,1)S(1)} collective-permute-done((bf16[128,512]{1,0:T(8,128)(2,1)S(1)}, bf16[128,512]{1,0:T(8,128)(2,1)S(1)}, u32[]{:S(2)}, u32[]{:S(2)}) %collective-permute-start.9) | collective-permute-done | bytes 131104 | tf_op jit(solution)/shard_map/ppermute | solution.py:209
  20.0 0.0 collective-permute-done.11.refs_17_
  20.0 0.6 %collective-permute-start.12 = (bf16[128,512]{1,0:T(8,128)(2,1)S(1)}, bf16[128,512]{1,0:T(8,128)(2,1)S(1)}, u32[]{:S(2)}, u32[]{:S(2)}) collective-permute-start(bf16[128,512]{1,0:T(8,128)(2,1)S(1)} %collective-permute-done.9.refs_3_.refs_11_), channel_id=1, source_target_pairs={{0,2},{2,4},{4,6},{6,7},{7,5},{5,3},{3,1},{1,0},{8,10},{10,12},{12... | collective-permute-start | bytes 393224 | tf_op jit(solution)/shard_map/ppermute | solution.py:209
  20.6 0.1 collective-permute-done.3.refs_4_
  20.7 1.3 %collective-permute-start.5 = (bf16[128,512]{1,0:T(8,128)(2,1)S(1)}, bf16[128,512]{1,0:T(8,128)(2,1)S(1)}, u32[]{:S(2)}, u32[]{:S(2)}) collective-permute-start(bf16[128,512]{1,0:T(8,128)(2,1)S(1)} %collective-permute-done.3.refs_4_), channel_id=1, source_target_pairs={{2,0},{4,2},{6,4},{7,6},{5,7},{3,5},{1,3},{0,1},{10,8},{12,10},{14... | collective-permute-start | bytes 393224 | tf_op jit(solution)/shard_map/ppermute | solution.py:207
  22.0 0.8 %collective-permute-done.4.refs_5_ = bf16[128,512]{1,0:T(8,128)(2,1)S(1)} collective-permute-done((bf16[128,512]{1,0:T(8,128)(2,1)S(1)}, bf16[128,512]{1,0:T(8,128)(2,1)S(1)}, u32[]{:S(2)}, u32[]{:S(2)}) %collective-permute-start.4) | collective-permute-done | bytes 131104 | tf_op jit(solution)/shard_map/ppermute | solution.py:204
  22.8 0.6 %collective-permute-start.6 = (bf16[128,512]{1,0:T(8,128)(2,1)S(1)}, bf16[128,512]{1,0:T(8,128)(2,1)S(1)}, u32[]{:S(2)}, u32[]{:S(2)}) collective-permute-start(bf16[128,512]{1,0:T(8,128)(2,1)S(1)} %collective-permute-done.4.refs_5_), channel_id=1, source_target_pairs={{0,2},{2,4},{4,6},{6,7},{7,5},{5,3},{3,1},{1,0},{8,10},{10,12},{12... | collective-permute-start | bytes 393224 | tf_op jit(solution)/shard_map/ppermute | solution.py:204
  23.4 0.1 collective-permute-done.13.refs_6_.refs_14_
  23.5 1.3 %collective-permute-start.14 = (bf16[128,512]{1,0:T(8,128)(2,1)S(1)}, bf16[128,512]{1,0:T(8,128)(2,1)S(1)}, u32[]{:S(2)}, u32[]{:S(2)}) collective-permute-start(bf16[128,512]{1,0:T(8,128)(2,1)S(1)} %collective-permute-done.13.refs_6_.refs_14_), channel_id=1, source_target_pairs={{2,0},{4,2},{6,4},{7,6},{5,7},{3,5},{1,3},{0,1},{10,8},{12,10},{14... | collective-permute-start | bytes 393224 | tf_op jit(solution)/shard_map/ppermute | solution.py:211
  24.8 0.2 compare_convert_fusion.hot_ref
  25.1 1.0 %collective-permute-done.5.refs_6_ = bf16[128,512]{1,0:T(8,128)(2,1)S(1)} collective-permute-done((bf16[128,512]{1,0:T(8,128)(2,1)S(1)}, bf16[128,512]{1,0:T(8,128)(2,1)S(1)}, u32[]{:S(2)}, u32[]{:S(2)}) %collective-permute-start.5) | collective-permute-done | bytes 131104 | tf_op jit(solution)/shard_map/ppermute | solution.py:207
  26.1 1.6 %collective-permute-done.6.refs_7_ = bf16[128,512]{1,0:T(8,128)(2,1)S(1)} collective-permute-done((bf16[128,512]{1,0:T(8,128)(2,1)S(1)}, bf16[128,512]{1,0:T(8,128)(2,1)S(1)}, u32[]{:S(2)}, u32[]{:S(2)}) %collective-permute-start.6) | collective-permute-done | bytes 131104 | tf_op jit(solution)/shard_map/ppermute | solution.py:204
  27.8 0.7 %collective-permute-done.14.refs_7_.refs_15_ = bf16[128,512]{1,0:T(8,128)(2,1)S(1)} collective-permute-done((bf16[128,512]{1,0:T(8,128)(2,1)S(1)}, bf16[128,512]{1,0:T(8,128)(2,1)S(1)}, u32[]{:S(2)}, u32[]{:S(2)}) %collective-permute-start.14) | collective-permute-done | bytes 131104 | tf_op jit(solution)/shard_map/ppermute | solution.py:211
  28.5 0.7 %select.13 = (bf16[256,512]{1,0:T(8,128)(2,1)S(1)}, bf16[256,512]{1,0:T(8,128)(2,1)S(1)}) custom-call(bf16[512,1024]{1,0:T(8,128)(2,1)S(1)} %compare_convert_fusion.hot_ref, bf16[128,512]{1,0:T(8,128)(2,1)S(1)} %get-tuple-element.68.refs_0_.refs_8_, bf16[128,512]{1,0:T(8,128)(2,1)S(1)} %collective-permute-done.7.refs_1_.refs_9_, ...), custom_call_target="tpu_custom_call" | custom-call | flops 1 | bytes 1 | tf_op jit(solution)/shard_map/select/pallas_call | solution.py:233
  29.2 0.0 copy-start.3
  29.2 0.1 collective-permute-start.17
  29.3 0.7 %select.12 = (bf16[256,512]{1,0:T(8,128)(2,1)S(1)}, bf16[256,512]{1,0:T(8,128)(2,1)S(1)}) custom-call(bf16[512,1024]{1,0:T(8,128)(2,1)S(1)} %compare_convert_fusion.hot_ref, bf16[128,512]{1,0:T(8,128)(2,1)S(1)} %get-tuple-element.56.refs_0_, bf16[128,512]{1,0:T(8,128)(2,1)S(1)} %collective-permute-done.refs_1_, ...), custom_call_target="tpu_custom_call" | custom-call | flops 1 | bytes 1 | tf_op jit(solution)/shard_map/select/pallas_call | solution.py:233
  30.0 0.6 %collective-permute-start.15 = (bf16[256,512]{1,0:T(8,128)(2,1)S(1)}, bf16[256,512]{1,0:T(8,128)(2,1)S(1)}, u32[]{:S(2)}, u32[]{:S(2)}) collective-permute-start(bf16[256,512]{1,0:T(8,128)(2,1)S(1)} %get-tuple-element.65), channel_id=1, source_target_pairs={{0,8},{8,0},{16,24},{24,16},{1,9},{9,1},{17,25},{25,17},{2,10},{10... | collective-permute-start | bytes 786440 | tf_op jit(solution)/shard_map/ppermute | solution.py:185
  30.6 0.3 collective-permute-done.17.right
  30.9 0.0 copy-start.1
  30.9 1.7 %collective-permute-start.18 = (bf16[128,512]{1,0:T(8,128)(2,1)S(1)}, bf16[128,512]{1,0:T(8,128)(2,1)S(1)}, u32[]{:S(2)}, u32[]{:S(2)}) collective-permute-start(bf16[128,512]{1,0:T(8,128)(2,1)S(1)} %get-tuple-element.78), channel_id=1, source_target_pairs={{0,16},{8,24},{16,0},{24,8},{1,17},{9,25},{17,1},{25,9},{2,18},{10... | collective-permute-start | bytes 393224 | tf_op jit(solution)/shard_map/ppermute | solution.py:185
  32.6 0.0 collective-permute-done.15.right
  32.7 0.9 %collective-permute-start.16 = (bf16[256,512]{1,0:T(8,128)(2,1)S(1)}, bf16[256,512]{1,0:T(8,128)(2,1)}, u32[]{:S(2)}, u32[]{:S(2)}) collective-permute-start(bf16[256,512]{1,0:T(8,128)(2,1)S(1)} %add.110.sum_a), channel_id=1, source_target_pairs={{0,16},{8,24},{16,0},{24,8},{1,17},{9,25},{17,1},{25,9},{2,18},{10... | collective-permute-start | bytes 786440 | tf_op jit(solution)/shard_map/ppermute | solution.py:185
  33.5 0.1 collective-permute-start.19
  33.6 0.4 collective-permute-start.20
  34.0 3.3 %collective-permute-done.18.mine = bf16[128,512]{1,0:T(8,128)(2,1)S(1)} collective-permute-done((bf16[128,512]{1,0:T(8,128)(2,1)S(1)}, bf16[128,512]{1,0:T(8,128)(2,1)S(1)}, u32[]{:S(2)}, u32[]{:S(2)}) %collective-permute-start.18) | collective-permute-done | bytes 131104 | tf_op jit(solution)/shard_map/ppermute | solution.py:185
  37.3 1.3 %collective-permute-start.21 = (bf16[128,512]{1,0:T(8,128)(2,1)S(1)}, bf16[128,512]{1,0:T(8,128)(2,1)}, u32[]{:S(2)}, u32[]{:S(2)}) collective-permute-start(bf16[128,512]{1,0:T(8,128)(2,1)S(1)} %collective-permute-done.18.mine), channel_id=1, source_target_pairs={{0,1},{1,0},{2,3},{3,2},{4,5},{5,4},{6,7},{7,6},{8,9},{9,8},{10,11... | collective-permute-start | bytes 393224 | tf_op jit(solution)/shard_map/ppermute | solution.py:260
  38.6 0.1 pad_add_fusion.1.cols_ref
  38.7 0.2 copy.6.kr_ref
  38.9 0.0 copy-start.2
  38.9 0.0 collective-permute-done.20.refs_19_
  38.9 3.0 %direct.1 = (bf16[1024,1024]{1,0:T(8,128)(2,1)S(1)}, bf16[512,1024]{1,0:T(8,128)(2,1)S(1)}, f32[1024,512]{1,0:T(8,128)S(1)}, f32[1024,512]{1,0:T(8,128)S(1)}) custom-call(s32[12]{0:T(128)S(1)} %pad_add_fusion.1.cols_ref, f32[1024,1]{1,0:T(8,128)S(1)} %copy.6.kr_ref, f32[1,512]{1,0:T(1,128)S(1)} %dynamic-slice_bitcast_fusion.kc_ref, ...), custom_call_target="tpu_custom_call" | custom-call | flops 1 | bytes 1 | tf_op jit(solution)/shard_map/direct/pallas_call | solution.py:272
  42.0 0.4 collective-permute-done.21.mate
  42.4 0.0 collective-permute-done.16.got_a
  42.4 1.0 %merge.1 = (bf16[256,512]{1,0:T(8,128)(2,1)S(1)}, bf16[256,512]{1,0:T(8,128)(2,1)S(1)}) custom-call(s32[1]{0:T(128)} %bitcast.6.side_ref, bf16[256,512]{1,0:T(8,128)(2,1)S(1)} %add.110.sum_a, bf16[256,512]{1,0:T(8,128)(2,1)} %collective-permute-done.16.got_a, bf16[256,512]{1,0:T(8,128)(2,1)S(1)} %copy-done.2, ...), custom_call_target="tpu_custom_call" | custom-call | flops 1 | bytes 1 | tf_op jit(solution)/shard_map/merge/pallas_call | solution.py:289
  43.4 0.1 collective-permute-start.22
  43.5 0.5 %collective-permute-start.23 = (bf16[256,512]{1,0:T(8,128)(2,1)S(1)}, bf16[256,512]{1,0:T(8,128)(2,1)S(1)}, u32[]{:S(2)}, u32[]{:S(2)}) collective-permute-start(bf16[256,512]{1,0:T(8,128)(2,1)S(1)} %get-tuple-element.94.pb), channel_id=1, source_target_pairs={{0,8},{8,0},{16,24},{24,16},{1,9},{9,1},{17,25},{25,17},{2,10},{10... | collective-permute-start | bytes 786440 | tf_op jit(solution)/shard_map/ppermute | solution.py:185
  44.0 1.0 %partial.1 = (f32[1024,256]{1,0:T(8,128)S(1)}, f32[512,256]{1,0:T(8,128)S(1)}) custom-call(bf16[1024,1024]{1,0:T(8,128)(2,1)S(1)} %get-tuple-element.87.zr, bf16[512,1024]{1,0:T(8,128)(2,1)S(1)} %get-tuple-element.88.zc, bf16[256,512]{1,0:T(8,128)(2,1)S(1)} %get-tuple-element.93.pa, bf16[256,512]{1,0:T(8,128)(2,1)S(1)} %get-tuple-element.94.pb), custom_call_target="tpu_custom_call" | custom-call | flops 1 | bytes 1 | tf_op jit(solution)/shard_map/partial/pallas_call | solution.py:299
  45.0 0.0 collective-permute-done.22.pa
  45.0 0.4 collective-permute-done.23.pb
  45.4 2.8 %final.1 = f32[1024,512]{1,0:T(8,128)} custom-call(bf16[1024,1024]{1,0:T(8,128)(2,1)S(1)} %get-tuple-element.87.zr, bf16[512,1024]{1,0:T(8,128)(2,1)S(1)} %get-tuple-element.88.zc, bf16[256,512]{1,0:T(8,128)(2,1)S(1)} %collective-permute-done.22.pa, bf16[256,512]{1,0:T(8,128)(2,1)S(1)} %collective-permute-done.23.pb, ...), custom_call_target="tpu_custom_call" | custom-call | flops 1 | bytes 1 | tf_op jit(solution)/shard_map/final/pallas_call | solution.py:308
  (13 shorter events, 0.1 us)
Async XLA Ops:
  0.0 1.0 %copy-start = (f32[128,1024]{1,0:T(8,128)S(1)}, f32[128,1024]{1,0:T(8,128)}, u32[]{:S(2)}) copy-start(f32[128,1024]{1,0:T(8,128)} %x_ref.1) | copy-start | bytes 1572868
  1.3 8.4 %collective-permute-start = (bf16[128,512]{1,0:T(8,128)(2,1)S(1)}, bf16[128,512]{1,0:T(8,128)(2,1)S(1)}, u32[]{:S(2)}, u32[]{:S(2)}) collective-permute-start(bf16[128,512]{1,0:T(8,128)(2,1)S(1)} %get-tuple-element.56.refs_0_), channel_id=1, source_target_pairs={{0,2},{2,4},{4,6},{6,7},{7,5},{5,3},{3,1},{1,0},{8,10},{10,12},{12... | collective-permute-start | bytes 393224 | tf_op jit(solution)/shard_map/ppermute | solution.py:204
  4.4 8.8 %collective-permute-start.1 = (bf16[128,512]{1,0:T(8,128)(2,1)S(1)}, bf16[128,512]{1,0:T(8,128)(2,1)S(1)}, u32[]{:S(2)}, u32[]{:S(2)}) collective-permute-start(bf16[128,512]{1,0:T(8,128)(2,1)S(1)} %get-tuple-element.56.refs_0_), channel_id=1, source_target_pairs={{2,0},{4,2},{6,4},{7,6},{5,7},{3,5},{1,3},{0,1},{10,8},{12,10},{14... | collective-permute-start | bytes 393224 | tf_op jit(solution)/shard_map/ppermute | solution.py:207
  4.4 10.6 %collective-permute-start.7 = (bf16[128,512]{1,0:T(8,128)(2,1)S(1)}, bf16[128,512]{1,0:T(8,128)(2,1)S(1)}, u32[]{:S(2)}, u32[]{:S(2)}) collective-permute-start(bf16[128,512]{1,0:T(8,128)(2,1)S(1)} %get-tuple-element.68.refs_0_.refs_8_), channel_id=1, source_target_pairs={{0,2},{2,4},{4,6},{6,7},{7,5},{5,3},{3,1},{1,0},{8,10},{10,12},{12... | collective-permute-start | bytes 393224 | tf_op jit(solution)/shard_map/ppermute | solution.py:209
  6.4 5.8 %collective-permute-start.8 = (bf16[128,512]{1,0:T(8,128)(2,1)S(1)}, bf16[128,512]{1,0:T(8,128)(2,1)S(1)}, u32[]{:S(2)}, u32[]{:S(2)}) collective-permute-start(bf16[128,512]{1,0:T(8,128)(2,1)S(1)} %get-tuple-element.68.refs_0_.refs_8_), channel_id=1, source_target_pairs={{2,0},{4,2},{6,4},{7,6},{5,7},{3,5},{1,3},{0,1},{10,8},{12,10},{14... | collective-permute-start | bytes 393224 | tf_op jit(solution)/shard_map/ppermute | solution.py:211
  6.4 13.6 %collective-permute-start.11 = (bf16[128,1024]{1,0:T(8,128)(2,1)S(1)}, bf16[128,1024]{1,0:T(8,128)(2,1)S(1)}, u32[]{:S(2)}, u32[]{:S(2)}) collective-permute-start(bf16[128,1024]{1,0:T(8,128)(2,1)S(1)} %get-tuple-element.81.refs_16_), channel_id=1, source_target_pairs={{0,16},{8,24},{16,0},{24,8},{1,17},{9,25},{17,1},{25,9},{2,18},{10... | collective-permute-start | bytes 786440 | tf_op jit(solution)/shard_map/ppermute | solution.py:185
  9.7 5.6 %collective-permute-start.2 = (bf16[128,512]{1,0:T(8,128)(2,1)S(1)}, bf16[128,512]{1,0:T(8,128)(2,1)S(1)}, u32[]{:S(2)}, u32[]{:S(2)}) collective-permute-start(bf16[128,512]{1,0:T(8,128)(2,1)S(1)} %collective-permute-done.refs_1_), channel_id=1, source_target_pairs={{0,2},{2,4},{4,6},{6,7},{7,5},{5,3},{3,1},{1,0},{8,10},{10,12},{12... | collective-permute-start | bytes 393224 | tf_op jit(solution)/shard_map/ppermute | solution.py:204
  12.1 5.7 %collective-permute-start.10 = (bf16[128,512]{1,0:T(8,128)(2,1)S(1)}, bf16[128,512]{1,0:T(8,128)(2,1)S(1)}, u32[]{:S(2)}, u32[]{:S(2)}) collective-permute-start(bf16[128,512]{1,0:T(8,128)(2,1)S(1)} %collective-permute-done.8.refs_2_.refs_10_), channel_id=1, source_target_pairs={{2,0},{4,2},{6,4},{7,6},{5,7},{3,5},{1,3},{0,1},{10,8},{12,10},{14... | collective-permute-start | bytes 393224 | tf_op jit(solution)/shard_map/ppermute | solution.py:211
  13.2 7.5 %collective-permute-start.3 = (bf16[128,512]{1,0:T(8,128)(2,1)S(1)}, bf16[128,512]{1,0:T(8,128)(2,1)S(1)}, u32[]{:S(2)}, u32[]{:S(2)}) collective-permute-start(bf16[128,512]{1,0:T(8,128)(2,1)S(1)} %collective-permute-done.1.refs_2_), channel_id=1, source_target_pairs={{2,0},{4,2},{6,4},{7,6},{5,7},{3,5},{1,3},{0,1},{10,8},{12,10},{14... | collective-permute-start | bytes 393224 | tf_op jit(solution)/shard_map/ppermute | solution.py:207
  14.9 5.1 %collective-permute-start.9 = (bf16[128,512]{1,0:T(8,128)(2,1)S(1)}, bf16[128,512]{1,0:T(8,128)(2,1)S(1)}, u32[]{:S(2)}, u32[]{:S(2)}) collective-permute-start(bf16[128,512]{1,0:T(8,128)(2,1)S(1)} %collective-permute-done.7.refs_1_.refs_9_), channel_id=1, source_target_pairs={{0,2},{2,4},{4,6},{6,7},{7,5},{5,3},{3,1},{1,0},{8,10},{10,12},{12... | collective-permute-start | bytes 393224 | tf_op jit(solution)/shard_map/ppermute | solution.py:209
  15.3 7.5 %collective-permute-start.4 = (bf16[128,512]{1,0:T(8,128)(2,1)S(1)}, bf16[128,512]{1,0:T(8,128)(2,1)S(1)}, u32[]{:S(2)}, u32[]{:S(2)}) collective-permute-start(bf16[128,512]{1,0:T(8,128)(2,1)S(1)} %collective-permute-done.2.refs_3_), channel_id=1, source_target_pairs={{0,2},{2,4},{4,6},{6,7},{7,5},{5,3},{3,1},{1,0},{8,10},{10,12},{12... | collective-permute-start | bytes 393224 | tf_op jit(solution)/shard_map/ppermute | solution.py:204
  17.9 5.7 %collective-permute-start.13 = (bf16[128,512]{1,0:T(8,128)(2,1)S(1)}, bf16[128,512]{1,0:T(8,128)(2,1)S(1)}, u32[]{:S(2)}, u32[]{:S(2)}) collective-permute-start(bf16[128,512]{1,0:T(8,128)(2,1)S(1)} %collective-permute-done.10.refs_4_.refs_12_), channel_id=1, source_target_pairs={{2,0},{4,2},{6,4},{7,6},{5,7},{3,5},{1,3},{0,1},{10,8},{12,10},{14... | collective-permute-start | bytes 393224 | tf_op jit(solution)/shard_map/ppermute | solution.py:211
  20.0 6.1 %collective-permute-start.12 = (bf16[128,512]{1,0:T(8,128)(2,1)S(1)}, bf16[128,512]{1,0:T(8,128)(2,1)S(1)}, u32[]{:S(2)}, u32[]{:S(2)}) collective-permute-start(bf16[128,512]{1,0:T(8,128)(2,1)S(1)} %collective-permute-done.9.refs_3_.refs_11_), channel_id=1, source_target_pairs={{0,2},{2,4},{4,6},{6,7},{7,5},{5,3},{3,1},{1,0},{8,10},{10,12},{12... | collective-permute-start | bytes 393224 | tf_op jit(solution)/shard_map/ppermute | solution.py:209
  20.7 5.4 %collective-permute-start.5 = (bf16[128,512]{1,0:T(8,128)(2,1)S(1)}, bf16[128,512]{1,0:T(8,128)(2,1)S(1)}, u32[]{:S(2)}, u32[]{:S(2)}) collective-permute-start(bf16[128,512]{1,0:T(8,128)(2,1)S(1)} %collective-permute-done.3.refs_4_), channel_id=1, source_target_pairs={{2,0},{4,2},{6,4},{7,6},{5,7},{3,5},{1,3},{0,1},{10,8},{12,10},{14... | collective-permute-start | bytes 393224 | tf_op jit(solution)/shard_map/ppermute | solution.py:207
  22.8 5.0 %collective-permute-start.6 = (bf16[128,512]{1,0:T(8,128)(2,1)S(1)}, bf16[128,512]{1,0:T(8,128)(2,1)S(1)}, u32[]{:S(2)}, u32[]{:S(2)}) collective-permute-start(bf16[128,512]{1,0:T(8,128)(2,1)S(1)} %collective-permute-done.4.refs_5_), channel_id=1, source_target_pairs={{0,2},{2,4},{4,6},{6,7},{7,5},{5,3},{3,1},{1,0},{8,10},{10,12},{12... | collective-permute-start | bytes 393224 | tf_op jit(solution)/shard_map/ppermute | solution.py:204
  23.5 5.0 %collective-permute-start.14 = (bf16[128,512]{1,0:T(8,128)(2,1)S(1)}, bf16[128,512]{1,0:T(8,128)(2,1)S(1)}, u32[]{:S(2)}, u32[]{:S(2)}) collective-permute-start(bf16[128,512]{1,0:T(8,128)(2,1)S(1)} %collective-permute-done.13.refs_6_.refs_14_), channel_id=1, source_target_pairs={{2,0},{4,2},{6,4},{7,6},{5,7},{3,5},{1,3},{0,1},{10,8},{12,10},{14... | collective-permute-start | bytes 393224 | tf_op jit(solution)/shard_map/ppermute | solution.py:211
  29.2 9.4 %copy-start.3 = (s32[4]{0:T(128)S(1)}, s32[4]{0:T(128)}, u32[]{:S(2)}) copy-start(s32[4]{0:T(128)} %constant.87.clone) | copy-start | bytes 52
  29.2 1.6 %collective-permute-start.17 = (bf16[256,512]{1,0:T(8,128)(2,1)S(1)}, bf16[256,512]{1,0:T(8,128)(2,1)S(1)}, u32[]{:S(2)}, u32[]{:S(2)}) collective-permute-start(bf16[256,512]{1,0:T(8,128)(2,1)S(1)} %get-tuple-element.77), channel_id=1, source_target_pairs={{0,8},{8,0},{16,24},{24,16},{1,9},{9,1},{17,25},{25,17},{2,10},{10... | collective-permute-start | bytes 786440 | tf_op jit(solution)/shard_map/ppermute | solution.py:185
  30.0 2.6 %collective-permute-start.15 = (bf16[256,512]{1,0:T(8,128)(2,1)S(1)}, bf16[256,512]{1,0:T(8,128)(2,1)S(1)}, u32[]{:S(2)}, u32[]{:S(2)}) collective-permute-start(bf16[256,512]{1,0:T(8,128)(2,1)S(1)} %get-tuple-element.65), channel_id=1, source_target_pairs={{0,8},{8,0},{16,24},{24,16},{1,9},{9,1},{17,25},{25,17},{2,10},{10... | collective-permute-start | bytes 786440 | tf_op jit(solution)/shard_map/ppermute | solution.py:185
  30.9 2.7 %copy-start.1 = (bf16[256,512]{1,0:T(8,128)(2,1)}, bf16[256,512]{1,0:T(8,128)(2,1)S(1)}, u32[]{:S(2)}) copy-start(bf16[256,512]{1,0:T(8,128)(2,1)S(1)} %get-tuple-element.90.sum_b) | copy-start | bytes 786436
  30.9 6.4 %collective-permute-start.18 = (bf16[128,512]{1,0:T(8,128)(2,1)S(1)}, bf16[128,512]{1,0:T(8,128)(2,1)S(1)}, u32[]{:S(2)}, u32[]{:S(2)}) collective-permute-start(bf16[128,512]{1,0:T(8,128)(2,1)S(1)} %get-tuple-element.78), channel_id=1, source_target_pairs={{0,16},{8,24},{16,0},{24,8},{1,17},{9,25},{17,1},{25,9},{2,18},{10... | collective-permute-start | bytes 393224 | tf_op jit(solution)/shard_map/ppermute | solution.py:185
  32.7 9.7 %collective-permute-start.16 = (bf16[256,512]{1,0:T(8,128)(2,1)S(1)}, bf16[256,512]{1,0:T(8,128)(2,1)}, u32[]{:S(2)}, u32[]{:S(2)}) collective-permute-start(bf16[256,512]{1,0:T(8,128)(2,1)S(1)} %add.110.sum_a), channel_id=1, source_target_pairs={{0,16},{8,24},{16,0},{24,8},{1,17},{9,25},{17,1},{25,9},{2,18},{10... | collective-permute-start | bytes 786440 | tf_op jit(solution)/shard_map/ppermute | solution.py:185
  33.5 5.4 %collective-permute-start.19 = (bf16[128,1024]{1,0:T(8,128)(2,1)S(1)}, bf16[128,1024]{1,0:T(8,128)(2,1)}, u32[]{:S(2)}, u32[]{:S(2)}) collective-permute-start(bf16[128,1024]{1,0:T(8,128)(2,1)S(1)} %get-tuple-element.81.refs_16_), channel_id=1, source_target_pairs={{0,8},{8,0},{16,24},{24,16},{1,9},{9,1},{17,25},{25,17},{2,10},{10... | collective-permute-start | bytes 786440 | tf_op jit(solution)/shard_map/ppermute | solution.py:185
  33.6 5.3 %collective-permute-start.20 = (bf16[128,1024]{1,0:T(8,128)(2,1)S(1)}, bf16[128,1024]{1,0:T(8,128)(2,1)}, u32[]{:S(2)}, u32[]{:S(2)}) collective-permute-start(bf16[128,1024]{1,0:T(8,128)(2,1)S(1)} %collective-permute-done.11.refs_17_), channel_id=1, source_target_pairs={{0,8},{8,0},{16,24},{24,16},{1,9},{9,1},{17,25},{25,17},{2,10},{10... | collective-permute-start | bytes 786440 | tf_op jit(solution)/shard_map/ppermute | solution.py:185
  37.3 5.1 %collective-permute-start.21 = (bf16[128,512]{1,0:T(8,128)(2,1)S(1)}, bf16[128,512]{1,0:T(8,128)(2,1)}, u32[]{:S(2)}, u32[]{:S(2)}) collective-permute-start(bf16[128,512]{1,0:T(8,128)(2,1)S(1)} %collective-permute-done.18.mine), channel_id=1, source_target_pairs={{0,1},{1,0},{2,3},{3,2},{4,5},{5,4},{6,7},{7,6},{8,9},{9,8},{10,11... | collective-permute-start | bytes 393224 | tf_op jit(solution)/shard_map/ppermute | solution.py:260
  38.9 3.5 %copy-start.2 = (bf16[256,512]{1,0:T(8,128)(2,1)S(1)}, bf16[256,512]{1,0:T(8,128)(2,1)}, u32[]{:S(2)}) copy-start(bf16[256,512]{1,0:T(8,128)(2,1)} %copy-done.1) | copy-start | bytes 786436
  43.4 1.6 %collective-permute-start.22 = (bf16[256,512]{1,0:T(8,128)(2,1)S(1)}, bf16[256,512]{1,0:T(8,128)(2,1)S(1)}, u32[]{:S(2)}, u32[]{:S(2)}) collective-permute-start(bf16[256,512]{1,0:T(8,128)(2,1)S(1)} %get-tuple-element.93.pa), channel_id=1, source_target_pairs={{0,8},{8,0},{16,24},{24,16},{1,9},{9,1},{17,25},{25,17},{2,10},{10... | collective-permute-start | bytes 786440 | tf_op jit(solution)/shard_map/ppermute | solution.py:185
  43.5 1.9 %collective-permute-start.23 = (bf16[256,512]{1,0:T(8,128)(2,1)S(1)}, bf16[256,512]{1,0:T(8,128)(2,1)S(1)}, u32[]{:S(2)}, u32[]{:S(2)}) collective-permute-start(bf16[256,512]{1,0:T(8,128)(2,1)S(1)} %get-tuple-element.94.pb), channel_id=1, source_target_pairs={{0,8},{8,0},{16,24},{24,16},{1,9},{9,1},{17,25},{25,17},{2,10},{10... | collective-permute-start | bytes 786440 | tf_op jit(solution)/shard_map/ppermute | solution.py:185

commit v5 on v4

--- a/solution.py
+++ b/solution.py
@@ -80,21 +80,20 @@
         share[rows, :] = direct * inv
 
 
-def products(left, pa, pb):
-    wa = pa.shape[1]
-    return dot_t(left[:, :wa], pa[...]) + dot_t(left[:, wa:], pb[...])
-
-
-def partial_kernel(zr, zc, pa, pb, row_part, col_part):
-    row_part[...] = products(zr[...], pa, pb)
-    col_part[...] = products(zc[...], pa, pb)
-
-
-def final_kernel(zr, zc, pa, pb, row_part, col_part, inverse, share, out_ref, stage, sems):
+def products(left, rows):
+    return dot_t(left, rows[...])
+
+
+def partial_kernel(zr, zc, near, row_part, col_part):
+    row_part[...] = products(zr[...], near)
+    col_part[...] = products(zc[...], near)
+
+
+def final_kernel(zr, zc, far, row_part, col_part, inverse, share, out_ref, stage, sems):
     height, samples = zr.shape
 
     def both(part, left):
-        product = jnp.concatenate([part, products(left, pa, pb)], axis=1)
+        product = jnp.concatenate([part, products(left, far)], axis=1)
         return power6(product, samples).astype(jnp.bfloat16)
 
     acol = both(col_part[...], zc[...])
@@ -144,16 +143,17 @@
         part[...] = total[rows:, :]
 
 
-def merge_kernel(side_ref, sum_a, got_a, sum_b, mine, mate, out_a, out_b):
-    out_a[...] = sum_a[...] + got_a[...]
+def merge_kernel(side_ref, sum_a, got_a, sum_b, mine, mate, out):
+    wa = sum_a.shape[1]
+    out[:, :wa] = sum_a[...] + got_a[...]
     rows = mine.shape[0]
     for side in range(2):
         first, second = (mine, mate) if side == 0 else (mate, mine)
 
         @pl.when(side_ref[0] == side)
         def _():
-            out_b[:rows, :] = sum_b[:rows, :] + first[...]
-            out_b[rows:, :] = sum_b[rows:, :] + second[...]
+            out[:rows, wa:] = sum_b[:rows, :] + first[...]
+            out[rows:, wa:] = sum_b[rows:, :] + second[...]
 
 
 def per_device(expression, pivots, degrees):
@@ -286,35 +286,35 @@
     got_a, got_b, zr, zc, inverse, share, mate_b = lax.optimization_barrier(
         (got_a, got_b, zr, zc, inverse, share, mate_b)
     )
-    total_a, total_b = pl.pallas_call(
+    total = pl.pallas_call(
         merge_kernel,
-        out_shape=[OUT(sum_a.shape, bf16), OUT(sum_b.shape, bf16)],
+        out_shape=OUT((half, samples), bf16),
         in_specs=[SMEM] + [VMEM] * 5,
-        out_specs=[VMEM] * 2,
+        out_specs=VMEM,
         compiler_params=params(4),
         cost_estimate=CHEAP,
         name="merge",
     )(parity, sum_a, got_a, sum_b, got_b, mate_b)
-    far_a, far_b = flip(total_a, 1), flip(total_b, 1)
+    far = flip(total, 1)
     row_part, col_part = pl.pallas_call(
         partial_kernel,
         out_shape=[shape((height, half), f32), shape((width, half), f32)],
-        in_specs=[VMEM] * 4,
+        in_specs=[VMEM] * 3,
         out_specs=[VMEM] * 2,
         compiler_params=params(8),
         cost_estimate=CHEAP,
         name="partial",
-    )(zr, zc, total_a, total_b)
+    )(zr, zc, total)
     return pl.pallas_call(
         final_kernel,
         out_shape=shape((height, width), f32),
-        in_specs=[VMEM] * 8,
+        in_specs=[VMEM] * 7,
         out_specs=ANY,
         scratch_shapes=[pltpu.VMEM((height, width), f32), pltpu.SemaphoreType.DMA((n // 2,))],
         compiler_params=params(16),
         cost_estimate=CHEAP,
         name="final",
-    )(zr, zc, far_a, far_b, row_part, col_part, inverse, share)
+    )(zr, zc, far, row_part, col_part, inverse, share)
 
 
 def solution(mesh):

time: 48.4 us -> 48.5 us (level)
  starting transfers between devices: 23.1 us -> 22.6 us
  waiting for transfers between devices: 11.6 us -> 12.1 us
    ppermute x9 -> x8, starting transfers between devices: 6.23 us -> 5.74 us  [per_device(): lax.ppermute(v, 'rows', [(i, i ^ mask) for i in range(n_rows)])]
    ppermute x9 -> x8, waiting for transfers between devices: 3.91 us -> 4.39 us  [per_device(): lax.ppermute(v, 'rows', [(i, i ^ mask) for i in range(n_rows)])]
  transfers between devices with their start and end apart: 24 -> 23, of which waited for: 13 -> 13; matrix products, arithmetic and copies ran while one was open for 6% -> 6% of each run, Pallas kernels for 10% -> 10%
where the time goes in v5:
time: 48.5 us; the launch traced here: 48.2 us
  starting transfers between devices  22.6 us (47%)
  waiting for transfers between devices  12.1 us (25%)
  Pallas kernels  9.62 us (20%)
  local copies, waits for them, and re-layouts  1.99 us (4%)
  other arithmetic  1.78 us (4%)
    ppermute x4, starting transfers between devices, per_device(): fa = lax.ppermute(fa, 'cols', forward)  7.05 us
    ppermute x8, starting transfers between devices, per_device(): lax.ppermute(v, 'rows', [(i, i ^ mask) for i in range(n_rows)])  5.74 us
    ppermute x8, waiting for transfers between devices, per_device(): lax.ppermute(v, 'rows', [(i, i ^ mask) for i in range(n_rows)])  4.39 us
    ppermute x3, starting transfers between devices, per_device(): ba = lax.ppermute(ba, 'cols', backward)  3.1 us
    pallas_call x1, Pallas kernels, per_device(): pl.pallas_call(functools.partial(direct_kernel, n, n_rows), out_shape=[sh...  3.02 us
    ppermute x3, starting transfers between devices, per_device(): fb = lax.ppermute(fb, 'cols', forward)  2.92 us
    pallas_call x1, Pallas kernels, per_device(): pl.pallas_call(final_kernel, out_shape=shape((height, width), f32), in_sp...  2.81 us
    ppermute x4, waiting for transfers between devices, per_device(): bb = lax.ppermute(bb, 'cols', backward)  2.49 us
  transfers between devices with their start and end apart: 23, of which 13 were waited for; matrix products, arithmetic and copies ran while one was open for 6% of the time, Pallas kernels for 10%

profile of v5, /device:TPU:0, one launch (start us, length us, event | category | flops | bytes accessed | tf_op | source)
XLA Modules:
  0.0 48.2 jit_solution(4617793298842304943)
XLA Ops:
  0.0 1.0 %copy-done = f32[128,1024]{1,0:T(8,128)S(1)} copy-done((f32[128,1024]{1,0:T(8,128)S(1)}, f32[128,1024]{1,0:T(8,128)}, u32[]{:S(2)}) %copy-start) | copy-done | bytes 524312
  1.0 0.2 standardize.1
  1.3 3.1 %collective-permute-start = (bf16[128,512]{1,0:T(8,128)(2,1)S(1)}, bf16[128,512]{1,0:T(8,128)(2,1)S(1)}, u32[]{:S(2)}, u32[]{:S(2)}) collective-permute-start(bf16[128,512]{1,0:T(8,128)(2,1)S(1)} %get-tuple-element.54.refs_0_), channel_id=1, source_target_pairs={{0,2},{2,4},{4,6},{6,7},{7,5},{5,3},{3,1},{1,0},{8,10},{10,12},{12... | collective-permute-start | bytes 393224 | tf_op jit(solution)/shard_map/ppermute | solution.py:204
  4.4 0.0 collective-permute-start.1
  4.4 2.0 %collective-permute-start.7 = (bf16[128,512]{1,0:T(8,128)(2,1)S(1)}, bf16[128,512]{1,0:T(8,128)(2,1)S(1)}, u32[]{:S(2)}, u32[]{:S(2)}) collective-permute-start(bf16[128,512]{1,0:T(8,128)(2,1)S(1)} %get-tuple-element.66.refs_0_.refs_8_), channel_id=1, source_target_pairs={{0,2},{2,4},{4,6},{6,7},{7,5},{5,3},{3,1},{1,0},{8,10},{10,12},{12... | collective-permute-start | bytes 393224 | tf_op jit(solution)/shard_map/ppermute | solution.py:209
  6.4 0.0 collective-permute-start.8
  6.4 1.9 %collective-permute-start.11 = (bf16[128,1024]{1,0:T(8,128)(2,1)S(1)}, bf16[128,1024]{1,0:T(8,128)(2,1)S(1)}, u32[]{:S(2)}, u32[]{:S(2)}) collective-permute-start(bf16[128,1024]{1,0:T(8,128)(2,1)S(1)} %get-tuple-element.79.refs_16_), channel_id=1, source_target_pairs={{0,16},{8,24},{16,0},{24,8},{1,17},{9,25},{17,1},{25,9},{2,18},{10... | collective-permute-start | bytes 786440 | tf_op jit(solution)/shard_map/ppermute | solution.py:185
  8.3 0.7 %fusion.1 = (f32[4,8,128]{2,1,0:T(8,128)S(1)}, f32[4096]{0:T(1024)S(1)}) fusion(s32[4096]{0:T(1024)} %param.7), kind=kLoop, calls=%fused_computation.15 | loop fusion | flops 8192 | bytes 49152 | tf_op jit(solution)/shard_map/reshape | solution.py:194
  9.1 0.7 %add_multiply_fusion = (s32[8]{0:T(128)S(1)}, s32[8]{0:T(128)S(1)}) fusion(s32[]{:T(128)S(6)} %mul.22, s32[8]{0:T(128)} %constant.86.clone, s32[]{:T(128)S(6)} %select_n.50), kind=kLoop, calls=%fused_computation.13 | loop fusion | flops 160 | bytes 104 | tf_op jit(solution)/shard_map/mul | solution.py:217
  9.7 0.0 collective-permute-done.refs_1_
  9.7 1.6 %collective-permute-start.2 = (bf16[128,512]{1,0:T(8,128)(2,1)S(1)}, bf16[128,512]{1,0:T(8,128)(2,1)S(1)}, u32[]{:S(2)}, u32[]{:S(2)}) collective-permute-start(bf16[128,512]{1,0:T(8,128)(2,1)S(1)} %collective-permute-done.refs_1_), channel_id=1, source_target_pairs={{0,2},{2,4},{4,6},{6,7},{7,5},{5,3},{3,1},{1,0},{8,10},{10,12},{12... | collective-permute-start | bytes 393224 | tf_op jit(solution)/shard_map/ppermute | solution.py:204
  11.4 0.8 %collective-permute-done.8.refs_2_.refs_10_ = bf16[128,512]{1,0:T(8,128)(2,1)S(1)} collective-permute-done((bf16[128,512]{1,0:T(8,128)(2,1)S(1)}, bf16[128,512]{1,0:T(8,128)(2,1)S(1)}, u32[]{:S(2)}, u32[]{:S(2)}) %collective-permute-start.8) | collective-permute-done | bytes 131104 | tf_op jit(solution)/shard_map/ppermute | solution.py:211
  12.1 0.3 collective-permute-start.10
  12.4 0.1 add_bitcast_fusion
  12.5 0.7 %reshape.33 = s32[2,256]{1,0:T(2,128)S(1)} reshape(s32[512]{0:T(512)} %param.6) | data formatting | bytes 4096 | tf_op jit(solution)/shard_map/reshape | solution.py:222
  13.2 0.0 collective-permute-done.1.refs_2_
  13.2 1.7 %collective-permute-start.3 = (bf16[128,512]{1,0:T(8,128)(2,1)S(1)}, bf16[128,512]{1,0:T(8,128)(2,1)S(1)}, u32[]{:S(2)}, u32[]{:S(2)}) collective-permute-start(bf16[128,512]{1,0:T(8,128)(2,1)S(1)} %collective-permute-done.1.refs_2_), channel_id=1, source_target_pairs={{2,0},{4,2},{6,4},{7,6},{5,7},{3,5},{1,3},{0,1},{10,8},{12,10},{14... | collective-permute-start | bytes 393224 | tf_op jit(solution)/shard_map/ppermute | solution.py:207
  14.9 0.0 collective-permute-done.7.refs_1_.refs_9_
  14.9 0.3 collective-permute-start.9
  15.3 0.0 collective-permute-done.2.refs_3_
  15.3 1.7 %collective-permute-start.4 = (bf16[128,512]{1,0:T(8,128)(2,1)S(1)}, bf16[128,512]{1,0:T(8,128)(2,1)S(1)}, u32[]{:S(2)}, u32[]{:S(2)}) collective-permute-start(bf16[128,512]{1,0:T(8,128)(2,1)S(1)} %collective-permute-done.2.refs_3_), channel_id=1, source_target_pairs={{0,2},{2,4},{4,6},{6,7},{7,5},{5,3},{3,1},{1,0},{8,10},{10,12},{12... | collective-permute-start | bytes 393224 | tf_op jit(solution)/shard_map/ppermute | solution.py:204
  17.0 0.8 %collective-permute-done.10.refs_4_.refs_12_ = bf16[128,512]{1,0:T(8,128)(2,1)S(1)} collective-permute-done((bf16[128,512]{1,0:T(8,128)(2,1)S(1)}, bf16[128,512]{1,0:T(8,128)(2,1)S(1)}, u32[]{:S(2)}, u32[]{:S(2)}) %collective-permute-start.10) | collective-permute-done | bytes 131104 | tf_op jit(solution)/shard_map/ppermute | solution.py:211
  17.9 0.9 %collective-permute-start.13 = (bf16[128,512]{1,0:T(8,128)(2,1)S(1)}, bf16[128,512]{1,0:T(8,128)(2,1)S(1)}, u32[]{:S(2)}, u32[]{:S(2)}) collective-permute-start(bf16[128,512]{1,0:T(8,128)(2,1)S(1)} %collective-permute-done.10.refs_4_.refs_12_), channel_id=1, source_target_pairs={{2,0},{4,2},{6,4},{7,6},{5,7},{3,5},{1,3},{0,1},{10,8},{12,10},{14... | collective-permute-start | bytes 393224 | tf_op jit(solution)/shard_map/ppermute | solution.py:211
  18.8 1.2 %collective-permute-done.9.refs_3_.refs_11_ = bf16[128,512]{1,0:T(8,128)(2,1)S(1)} collective-permute-done((bf16[128,512]{1,0:T(8,128)(2,1)S(1)}, bf16[128,512]{1,0:T(8,128)(2,1)S(1)}, u32[]{:S(2)}, u32[]{:S(2)}) %collective-permute-start.9) | collective-permute-done | bytes 131104 | tf_op jit(solution)/shard_map/ppermute | solution.py:209
  20.0 0.0 collective-permute-done.11.refs_17_
  20.0 0.6 %collective-permute-start.12 = (bf16[128,512]{1,0:T(8,128)(2,1)S(1)}, bf16[128,512]{1,0:T(8,128)(2,1)S(1)}, u32[]{:S(2)}, u32[]{:S(2)}) collective-permute-start(bf16[128,512]{1,0:T(8,128)(2,1)S(1)} %collective-permute-done.9.refs_3_.refs_11_), channel_id=1, source_target_pairs={{0,2},{2,4},{4,6},{6,7},{7,5},{5,3},{3,1},{1,0},{8,10},{10,12},{12... | collective-permute-start | bytes 393224 | tf_op jit(solution)/shard_map/ppermute | solution.py:209
  20.6 0.1 collective-permute-done.3.refs_4_
  20.7 1.3 %collective-permute-start.5 = (bf16[128,512]{1,0:T(8,128)(2,1)S(1)}, bf16[128,512]{1,0:T(8,128)(2,1)S(1)}, u32[]{:S(2)}, u32[]{:S(2)}) collective-permute-start(bf16[128,512]{1,0:T(8,128)(2,1)S(1)} %collective-permute-done.3.refs_4_), channel_id=1, source_target_pairs={{2,0},{4,2},{6,4},{7,6},{5,7},{3,5},{1,3},{0,1},{10,8},{12,10},{14... | collective-permute-start | bytes 393224 | tf_op jit(solution)/shard_map/ppermute | solution.py:207
  22.0 0.8 %collective-permute-done.4.refs_5_ = bf16[128,512]{1,0:T(8,128)(2,1)S(1)} collective-permute-done((bf16[128,512]{1,0:T(8,128)(2,1)S(1)}, bf16[128,512]{1,0:T(8,128)(2,1)S(1)}, u32[]{:S(2)}, u32[]{:S(2)}) %collective-permute-start.4) | collective-permute-done | bytes 131104 | tf_op jit(solution)/shard_map/ppermute | solution.py:204
  22.8 0.6 %collective-permute-start.6 = (bf16[128,512]{1,0:T(8,128)(2,1)S(1)}, bf16[128,512]{1,0:T(8,128)(2,1)S(1)}, u32[]{:S(2)}, u32[]{:S(2)}) collective-permute-start(bf16[128,512]{1,0:T(8,128)(2,1)S(1)} %collective-permute-done.4.refs_5_), channel_id=1, source_target_pairs={{0,2},{2,4},{4,6},{6,7},{7,5},{5,3},{3,1},{1,0},{8,10},{10,12},{12... | collective-permute-start | bytes 393224 | tf_op jit(solution)/shard_map/ppermute | solution.py:204
  23.4 0.1 collective-permute-done.13.refs_6_.refs_14_
  23.5 1.3 %collective-permute-start.14 = (bf16[128,512]{1,0:T(8,128)(2,1)S(1)}, bf16[128,512]{1,0:T(8,128)(2,1)S(1)}, u32[]{:S(2)}, u32[]{:S(2)}) collective-permute-start(bf16[128,512]{1,0:T(8,128)(2,1)S(1)} %collective-permute-done.13.refs_6_.refs_14_), channel_id=1, source_target_pairs={{2,0},{4,2},{6,4},{7,6},{5,7},{3,5},{1,3},{0,1},{10,8},{12,10},{14... | collective-permute-start | bytes 393224 | tf_op jit(solution)/shard_map/ppermute | solution.py:211
  24.8 0.2 compare_convert_fusion.hot_ref
  25.1 1.0 %collective-permute-done.5.refs_6_ = bf16[128,512]{1,0:T(8,128)(2,1)S(1)} collective-permute-done((bf16[128,512]{1,0:T(8,128)(2,1)S(1)}, bf16[128,512]{1,0:T(8,128)(2,1)S(1)}, u32[]{:S(2)}, u32[]{:S(2)}) %collective-permute-start.5) | collective-permute-done | bytes 131104 | tf_op jit(solution)/shard_map/ppermute | solution.py:207
  26.1 0.0 collective-permute-done.12.refs_5_.refs_13_
  26.1 1.6 %collective-permute-done.6.refs_7_ = bf16[128,512]{1,0:T(8,128)(2,1)S(1)} collective-permute-done((bf16[128,512]{1,0:T(8,128)(2,1)S(1)}, bf16[128,512]{1,0:T(8,128)(2,1)S(1)}, u32[]{:S(2)}, u32[]{:S(2)}) %collective-permute-start.6) | collective-permute-done | bytes 131104 | tf_op jit(solution)/shard_map/ppermute | solution.py:204
  27.8 0.7 %collective-permute-done.14.refs_7_.refs_15_ = bf16[128,512]{1,0:T(8,128)(2,1)S(1)} collective-permute-done((bf16[128,512]{1,0:T(8,128)(2,1)S(1)}, bf16[128,512]{1,0:T(8,128)(2,1)S(1)}, u32[]{:S(2)}, u32[]{:S(2)}) %collective-permute-start.14) | collective-permute-done | bytes 131104 | tf_op jit(solution)/shard_map/ppermute | solution.py:211
  28.5 0.7 %select.13 = (bf16[256,512]{1,0:T(8,128)(2,1)S(1)}, bf16[256,512]{1,0:T(8,128)(2,1)S(1)}) custom-call(bf16[512,1024]{1,0:T(8,128)(2,1)S(1)} %compare_convert_fusion.hot_ref, bf16[128,512]{1,0:T(8,128)(2,1)S(1)} %get-tuple-element.66.refs_0_.refs_8_, bf16[128,512]{1,0:T(8,128)(2,1)S(1)} %collective-permute-done.7.refs_1_.refs_9_, ...), custom_call_target="tpu_custom_call" | custom-call | flops 1 | bytes 1 | tf_op jit(solution)/shard_map/select/pallas_call | solution.py:233
  29.2 0.0 copy-start.3
  29.2 0.1 collective-permute-start.17
  29.3 0.7 %select.12 = (bf16[256,512]{1,0:T(8,128)(2,1)S(1)}, bf16[256,512]{1,0:T(8,128)(2,1)S(1)}) custom-call(bf16[512,1024]{1,0:T(8,128)(2,1)S(1)} %compare_convert_fusion.hot_ref, bf16[128,512]{1,0:T(8,128)(2,1)S(1)} %get-tuple-element.54.refs_0_, bf16[128,512]{1,0:T(8,128)(2,1)S(1)} %collective-permute-done.refs_1_, ...), custom_call_target="tpu_custom_call" | custom-call | flops 1 | bytes 1 | tf_op jit(solution)/shard_map/select/pallas_call | solution.py:233
  30.0 0.6 %collective-permute-start.15 = (bf16[256,512]{1,0:T(8,128)(2,1)S(1)}, bf16[256,512]{1,0:T(8,128)(2,1)S(1)}, u32[]{:S(2)}, u32[]{:S(2)}) collective-permute-start(bf16[256,512]{1,0:T(8,128)(2,1)S(1)} %get-tuple-element.63), channel_id=1, source_target_pairs={{0,8},{8,0},{16,24},{24,16},{1,9},{9,1},{17,25},{25,17},{2,10},{10... | collective-permute-start | bytes 786440 | tf_op jit(solution)/shard_map/ppermute | solution.py:185
  30.6 0.3 collective-permute-done.17.right
  30.9 0.0 copy-start.1
  30.9 1.7 %collective-permute-start.18 = (bf16[128,512]{1,0:T(8,128)(2,1)S(1)}, bf16[128,512]{1,0:T(8,128)(2,1)S(1)}, u32[]{:S(2)}, u32[]{:S(2)}) collective-permute-start(bf16[128,512]{1,0:T(8,128)(2,1)S(1)} %get-tuple-element.76), channel_id=1, source_target_pairs={{0,16},{8,24},{16,0},{24,8},{1,17},{9,25},{17,1},{25,9},{2,18},{10... | collective-permute-start | bytes 393224 | tf_op jit(solution)/shard_map/ppermute | solution.py:185
  32.6 0.0 collective-permute-done.15.right
  32.7 0.9 %collective-permute-start.16 = (bf16[256,512]{1,0:T(8,128)(2,1)S(1)}, bf16[256,512]{1,0:T(8,128)(2,1)}, u32[]{:S(2)}, u32[]{:S(2)}) collective-permute-start(bf16[256,512]{1,0:T(8,128)(2,1)S(1)} %add.110.sum_a), channel_id=1, source_target_pairs={{0,16},{8,24},{16,0},{24,8},{1,17},{9,25},{17,1},{25,9},{2,18},{10... | collective-permute-start | bytes 786440 | tf_op jit(solution)/shard_map/ppermute | solution.py:185
  33.5 0.1 collective-permute-start.19
  33.6 0.4 collective-permute-start.20
  34.0 3.3 %collective-permute-done.18.mine = bf16[128,512]{1,0:T(8,128)(2,1)S(1)} collective-permute-done((bf16[128,512]{1,0:T(8,128)(2,1)S(1)}, bf16[128,512]{1,0:T(8,128)(2,1)S(1)}, u32[]{:S(2)}, u32[]{:S(2)}) %collective-permute-start.18) | collective-permute-done | bytes 131104 | tf_op jit(solution)/shard_map/ppermute | solution.py:185
  37.3 1.3 %collective-permute-start.21 = (bf16[128,512]{1,0:T(8,128)(2,1)S(1)}, bf16[128,512]{1,0:T(8,128)(2,1)}, u32[]{:S(2)}, u32[]{:S(2)}) collective-permute-start(bf16[128,512]{1,0:T(8,128)(2,1)S(1)} %collective-permute-done.18.mine), channel_id=1, source_target_pairs={{0,1},{1,0},{2,3},{3,2},{4,5},{5,4},{6,7},{7,6},{8,9},{9,8},{10,11... | collective-permute-start | bytes 393224 | tf_op jit(solution)/shard_map/ppermute | solution.py:260
  38.6 0.1 pad_add_fusion.1.cols_ref
  38.7 0.2 copy.6.kr_ref
  38.9 0.0 copy-start.2
  38.9 0.0 collective-permute-done.19.refs_18_
  38.9 0.0 collective-permute-done.20.refs_19_
  38.9 3.0 %direct.1 = (bf16[1024,1024]{1,0:T(8,128)(2,1)S(1)}, bf16[512,1024]{1,0:T(8,128)(2,1)S(1)}, f32[1024,512]{1,0:T(8,128)S(1)}, f32[1024,512]{1,0:T(8,128)S(1)}) custom-call(s32[12]{0:T(128)S(1)} %pad_add_fusion.1.cols_ref, f32[1024,1]{1,0:T(8,128)S(1)} %copy.6.kr_ref, f32[1,512]{1,0:T(1,128)S(1)} %dynamic-slice_bitcast_fusion.kc_ref, ...), custom_call_target="tpu_custom_call" | custom-call | flops 1 | bytes 1 | tf_op jit(solution)/shard_map/direct/pallas_call | solution.py:272
  42.0 0.4 collective-permute-done.21.mate
  42.4 0.0 collective-permute-done.16.got_a
  42.4 1.0 %merge.1.near = bf16[256,1024]{1,0:T(8,128)(2,1)S(1)} custom-call(s32[1]{0:T(128)} %bitcast.6.side_ref, bf16[256,512]{1,0:T(8,128)(2,1)S(1)} %add.110.sum_a, bf16[256,512]{1,0:T(8,128)(2,1)} %collective-permute-done.16.got_a, bf16[256,512]{1,0:T(8,128)(2,1)S(1)} %copy-done.2, bf16[128,512]{1,0:T(8,128)(2,1)S(1)} %collective-permute-done.18.mine, ...), custom_call_target="tpu_custom_call" | custom-call | flops 1 | bytes 1 | tf_op jit(solution)/shard_map/merge/pallas_call | solution.py:289
  43.4 0.1 collective-permute-start.22
  43.5 1.0 %partial.1 = (f32[1024,256]{1,0:T(8,128)S(1)}, f32[512,256]{1,0:T(8,128)S(1)}) custom-call(bf16[1024,1024]{1,0:T(8,128)(2,1)S(1)} %get-tuple-element.85.zr, bf16[512,1024]{1,0:T(8,128)(2,1)S(1)} %get-tuple-element.86.zc, bf16[256,1024]{1,0:T(8,128)(2,1)S(1)} %merge.1.near), custom_call_target="tpu_custom_call" | custom-call | flops 1 | bytes 1 | tf_op jit(solution)/shard_map/partial/pallas_call | solution.py:299
  44.5 0.9 %collective-permute-done.22.far = bf16[256,1024]{1,0:T(8,128)(2,1)S(1)} collective-permute-done((bf16[256,1024]{1,0:T(8,128)(2,1)S(1)}, bf16[256,1024]{1,0:T(8,128)(2,1)S(1)}, u32[]{:S(2)}, u32[]{:S(2)}) %collective-permute-start.22) | collective-permute-done | bytes 524320 | tf_op jit(solution)/shard_map/ppermute | solution.py:185
  45.4 2.8 %final.1 = f32[1024,512]{1,0:T(8,128)} custom-call(bf16[1024,1024]{1,0:T(8,128)(2,1)S(1)} %get-tuple-element.85.zr, bf16[512,1024]{1,0:T(8,128)(2,1)S(1)} %get-tuple-element.86.zc, bf16[256,1024]{1,0:T(8,128)(2,1)S(1)} %collective-permute-done.22.far, f32[1024,256]{1,0:T(8,128)S(1)} %get-tuple-element.91.row_part, ...), custom_call_target="tpu_custom_call" | custom-call | flops 1 | bytes 1 | tf_op jit(solution)/shard_map/final/pallas_call | solution.py:308
  (11 shorter events, 0.1 us)
Async XLA Ops:
  0.0 1.0 %copy-start = (f32[128,1024]{1,0:T(8,128)S(1)}, f32[128,1024]{1,0:T(8,128)}, u32[]{:S(2)}) copy-start(f32[128,1024]{1,0:T(8,128)} %x_ref.1) | copy-start | bytes 1572868
  1.3 8.4 %collective-permute-start = (bf16[128,512]{1,0:T(8,128)(2,1)S(1)}, bf16[128,512]{1,0:T(8,128)(2,1)S(1)}, u32[]{:S(2)}, u32[]{:S(2)}) collective-permute-start(bf16[128,512]{1,0:T(8,128)(2,1)S(1)} %get-tuple-element.54.refs_0_), channel_id=1, source_target_pairs={{0,2},{2,4},{4,6},{6,7},{7,5},{5,3},{3,1},{1,0},{8,10},{10,12},{12... | collective-permute-start | bytes 393224 | tf_op jit(solution)/shard_map/ppermute | solution.py:204
  4.4 8.8 %collective-permute-start.1 = (bf16[128,512]{1,0:T(8,128)(2,1)S(1)}, bf16[128,512]{1,0:T(8,128)(2,1)S(1)}, u32[]{:S(2)}, u32[]{:S(2)}) collective-permute-start(bf16[128,512]{1,0:T(8,128)(2,1)S(1)} %get-tuple-element.54.refs_0_), channel_id=1, source_target_pairs={{2,0},{4,2},{6,4},{7,6},{5,7},{3,5},{1,3},{0,1},{10,8},{12,10},{14... | collective-permute-start | bytes 393224 | tf_op jit(solution)/shard_map/ppermute | solution.py:207
  4.4 10.6 %collective-permute-start.7 = (bf16[128,512]{1,0:T(8,128)(2,1)S(1)}, bf16[128,512]{1,0:T(8,128)(2,1)S(1)}, u32[]{:S(2)}, u32[]{:S(2)}) collective-permute-start(bf16[128,512]{1,0:T(8,128)(2,1)S(1)} %get-tuple-element.66.refs_0_.refs_8_), channel_id=1, source_target_pairs={{0,2},{2,4},{4,6},{6,7},{7,5},{5,3},{3,1},{1,0},{8,10},{10,12},{12... | collective-permute-start | bytes 393224 | tf_op jit(solution)/shard_map/ppermute | solution.py:209
  6.4 5.8 %collective-permute-start.8 = (bf16[128,512]{1,0:T(8,128)(2,1)S(1)}, bf16[128,512]{1,0:T(8,128)(2,1)S(1)}, u32[]{:S(2)}, u32[]{:S(2)}) collective-permute-start(bf16[128,512]{1,0:T(8,128)(2,1)S(1)} %get-tuple-element.66.refs_0_.refs_8_), channel_id=1, source_target_pairs={{2,0},{4,2},{6,4},{7,6},{5,7},{3,5},{1,3},{0,1},{10,8},{12,10},{14... | collective-permute-start | bytes 393224 | tf_op jit(solution)/shard_map/ppermute | solution.py:211
  6.4 13.6 %collective-permute-start.11 = (bf16[128,1024]{1,0:T(8,128)(2,1)S(1)}, bf16[128,1024]{1,0:T(8,128)(2,1)S(1)}, u32[]{:S(2)}, u32[]{:S(2)}) collective-permute-start(bf16[128,1024]{1,0:T(8,128)(2,1)S(1)} %get-tuple-element.79.refs_16_), channel_id=1, source_target_pairs={{0,16},{8,24},{16,0},{24,8},{1,17},{9,25},{17,1},{25,9},{2,18},{10... | collective-permute-start | bytes 786440 | tf_op jit(solution)/shard_map/ppermute | solution.py:185
  9.7 5.6 %collective-permute-start.2 = (bf16[128,512]{1,0:T(8,128)(2,1)S(1)}, bf16[128,512]{1,0:T(8,128)(2,1)S(1)}, u32[]{:S(2)}, u32[]{:S(2)}) collective-permute-start(bf16[128,512]{1,0:T(8,128)(2,1)S(1)} %collective-permute-done.refs_1_), channel_id=1, source_target_pairs={{0,2},{2,4},{4,6},{6,7},{7,5},{5,3},{3,1},{1,0},{8,10},{10,12},{12... | collective-permute-start | bytes 393224 | tf_op jit(solution)/shard_map/ppermute | solution.py:204
  12.1 5.7 %collective-permute-start.10 = (bf16[128,512]{1,0:T(8,128)(2,1)S(1)}, bf16[128,512]{1,0:T(8,128)(2,1)S(1)}, u32[]{:S(2)}, u32[]{:S(2)}) collective-permute-start(bf16[128,512]{1,0:T(8,128)(2,1)S(1)} %collective-permute-done.8.refs_2_.refs_10_), channel_id=1, source_target_pairs={{2,0},{4,2},{6,4},{7,6},{5,7},{3,5},{1,3},{0,1},{10,8},{12,10},{14... | collective-permute-start | bytes 393224 | tf_op jit(solution)/shard_map/ppermute | solution.py:211
  13.2 7.5 %collective-permute-start.3 = (bf16[128,512]{1,0:T(8,128)(2,1)S(1)}, bf16[128,512]{1,0:T(8,128)(2,1)S(1)}, u32[]{:S(2)}, u32[]{:S(2)}) collective-permute-start(bf16[128,512]{1,0:T(8,128)(2,1)S(1)} %collective-permute-done.1.refs_2_), channel_id=1, source_target_pairs={{2,0},{4,2},{6,4},{7,6},{5,7},{3,5},{1,3},{0,1},{10,8},{12,10},{14... | collective-permute-start | bytes 393224 | tf_op jit(solution)/shard_map/ppermute | solution.py:207
  14.9 5.1 %collective-permute-start.9 = (bf16[128,512]{1,0:T(8,128)(2,1)S(1)}, bf16[128,512]{1,0:T(8,128)(2,1)S(1)}, u32[]{:S(2)}, u32[]{:S(2)}) collective-permute-start(bf16[128,512]{1,0:T(8,128)(2,1)S(1)} %collective-permute-done.7.refs_1_.refs_9_), channel_id=1, source_target_pairs={{0,2},{2,4},{4,6},{6,7},{7,5},{5,3},{3,1},{1,0},{8,10},{10,12},{12... | collective-permute-start | bytes 393224 | tf_op jit(solution)/shard_map/ppermute | solution.py:209
  15.3 7.5 %collective-permute-start.4 = (bf16[128,512]{1,0:T(8,128)(2,1)S(1)}, bf16[128,512]{1,0:T(8,128)(2,1)S(1)}, u32[]{:S(2)}, u32[]{:S(2)}) collective-permute-start(bf16[128,512]{1,0:T(8,128)(2,1)S(1)} %collective-permute-done.2.refs_3_), channel_id=1, source_target_pairs={{0,2},{2,4},{4,6},{6,7},{7,5},{5,3},{3,1},{1,0},{8,10},{10,12},{12... | collective-permute-start | bytes 393224 | tf_op jit(solution)/shard_map/ppermute | solution.py:204
  17.9 5.7 %collective-permute-start.13 = (bf16[128,512]{1,0:T(8,128)(2,1)S(1)}, bf16[128,512]{1,0:T(8,128)(2,1)S(1)}, u32[]{:S(2)}, u32[]{:S(2)}) collective-permute-start(bf16[128,512]{1,0:T(8,128)(2,1)S(1)} %collective-permute-done.10.refs_4_.refs_12_), channel_id=1, source_target_pairs={{2,0},{4,2},{6,4},{7,6},{5,7},{3,5},{1,3},{0,1},{10,8},{12,10},{14... | collective-permute-start | bytes 393224 | tf_op jit(solution)/shard_map/ppermute | solution.py:211
  20.0 6.1 %collective-permute-start.12 = (bf16[128,512]{1,0:T(8,128)(2,1)S(1)}, bf16[128,512]{1,0:T(8,128)(2,1)S(1)}, u32[]{:S(2)}, u32[]{:S(2)}) collective-permute-start(bf16[128,512]{1,0:T(8,128)(2,1)S(1)} %collective-permute-done.9.refs_3_.refs_11_), channel_id=1, source_target_pairs={{0,2},{2,4},{4,6},{6,7},{7,5},{5,3},{3,1},{1,0},{8,10},{10,12},{12... | collective-permute-start | bytes 393224 | tf_op jit(solution)/shard_map/ppermute | solution.py:209
  20.7 5.4 %collective-permute-start.5 = (bf16[128,512]{1,0:T(8,128)(2,1)S(1)}, bf16[128,512]{1,0:T(8,128)(2,1)S(1)}, u32[]{:S(2)}, u32[]{:S(2)}) collective-permute-start(bf16[128,512]{1,0:T(8,128)(2,1)S(1)} %collective-permute-done.3.refs_4_), channel_id=1, source_target_pairs={{2,0},{4,2},{6,4},{7,6},{5,7},{3,5},{1,3},{0,1},{10,8},{12,10},{14... | collective-permute-start | bytes 393224 | tf_op jit(solution)/shard_map/ppermute | solution.py:207
  22.8 5.0 %collective-permute-start.6 = (bf16[128,512]{1,0:T(8,128)(2,1)S(1)}, bf16[128,512]{1,0:T(8,128)(2,1)S(1)}, u32[]{:S(2)}, u32[]{:S(2)}) collective-permute-start(bf16[128,512]{1,0:T(8,128)(2,1)S(1)} %collective-permute-done.4.refs_5_), channel_id=1, source_target_pairs={{0,2},{2,4},{4,6},{6,7},{7,5},{5,3},{3,1},{1,0},{8,10},{10,12},{12... | collective-permute-start | bytes 393224 | tf_op jit(solution)/shard_map/ppermute | solution.py:204
  23.5 5.0 %collective-permute-start.14 = (bf16[128,512]{1,0:T(8,128)(2,1)S(1)}, bf16[128,512]{1,0:T(8,128)(2,1)S(1)}, u32[]{:S(2)}, u32[]{:S(2)}) collective-permute-start(bf16[128,512]{1,0:T(8,128)(2,1)S(1)} %collective-permute-done.13.refs_6_.refs_14_), channel_id=1, source_target_pairs={{2,0},{4,2},{6,4},{7,6},{5,7},{3,5},{1,3},{0,1},{10,8},{12,10},{14... | collective-permute-start | bytes 393224 | tf_op jit(solution)/shard_map/ppermute | solution.py:211
  29.2 9.4 %copy-start.3 = (s32[4]{0:T(128)S(1)}, s32[4]{0:T(128)}, u32[]{:S(2)}) copy-start(s32[4]{0:T(128)} %constant.87.clone) | copy-start | bytes 52
  29.2 1.6 %collective-permute-start.17 = (bf16[256,512]{1,0:T(8,128)(2,1)S(1)}, bf16[256,512]{1,0:T(8,128)(2,1)S(1)}, u32[]{:S(2)}, u32[]{:S(2)}) collective-permute-start(bf16[256,512]{1,0:T(8,128)(2,1)S(1)} %get-tuple-element.75), channel_id=1, source_target_pairs={{0,8},{8,0},{16,24},{24,16},{1,9},{9,1},{17,25},{25,17},{2,10},{10... | collective-permute-start | bytes 786440 | tf_op jit(solution)/shard_map/ppermute | solution.py:185
  30.0 2.6 %collective-permute-start.15 = (bf16[256,512]{1,0:T(8,128)(2,1)S(1)}, bf16[256,512]{1,0:T(8,128)(2,1)S(1)}, u32[]{:S(2)}, u32[]{:S(2)}) collective-permute-start(bf16[256,512]{1,0:T(8,128)(2,1)S(1)} %get-tuple-element.63), channel_id=1, source_target_pairs={{0,8},{8,0},{16,24},{24,16},{1,9},{9,1},{17,25},{25,17},{2,10},{10... | collective-permute-start | bytes 786440 | tf_op jit(solution)/shard_map/ppermute | solution.py:185
  30.9 2.7 %copy-start.1 = (bf16[256,512]{1,0:T(8,128)(2,1)}, bf16[256,512]{1,0:T(8,128)(2,1)S(1)}, u32[]{:S(2)}) copy-start(bf16[256,512]{1,0:T(8,128)(2,1)S(1)} %get-tuple-element.88.sum_b) | copy-start | bytes 786436
  30.9 6.4 %collective-permute-start.18 = (bf16[128,512]{1,0:T(8,128)(2,1)S(1)}, bf16[128,512]{1,0:T(8,128)(2,1)S(1)}, u32[]{:S(2)}, u32[]{:S(2)}) collective-permute-start(bf16[128,512]{1,0:T(8,128)(2,1)S(1)} %get-tuple-element.76), channel_id=1, source_target_pairs={{0,16},{8,24},{16,0},{24,8},{1,17},{9,25},{17,1},{25,9},{2,18},{10... | collective-permute-start | bytes 393224 | tf_op jit(solution)/shard_map/ppermute | solution.py:185
  32.7 9.7 %collective-permute-start.16 = (bf16[256,512]{1,0:T(8,128)(2,1)S(1)}, bf16[256,512]{1,0:T(8,128)(2,1)}, u32[]{:S(2)}, u32[]{:S(2)}) collective-permute-start(bf16[256,512]{1,0:T(8,128)(2,1)S(1)} %add.110.sum_a), channel_id=1, source_target_pairs={{0,16},{8,24},{16,0},{24,8},{1,17},{9,25},{17,1},{25,9},{2,18},{10... | collective-permute-start | bytes 786440 | tf_op jit(solution)/shard_map/ppermute | solution.py:185
  33.5 5.4 %collective-permute-start.19 = (bf16[128,1024]{1,0:T(8,128)(2,1)S(1)}, bf16[128,1024]{1,0:T(8,128)(2,1)}, u32[]{:S(2)}, u32[]{:S(2)}) collective-permute-start(bf16[128,1024]{1,0:T(8,128)(2,1)S(1)} %get-tuple-element.79.refs_16_), channel_id=1, source_target_pairs={{0,8},{8,0},{16,24},{24,16},{1,9},{9,1},{17,25},{25,17},{2,10},{10... | collective-permute-start | bytes 786440 | tf_op jit(solution)/shard_map/ppermute | solution.py:185
  33.6 5.3 %collective-permute-start.20 = (bf16[128,1024]{1,0:T(8,128)(2,1)S(1)}, bf16[128,1024]{1,0:T(8,128)(2,1)}, u32[]{:S(2)}, u32[]{:S(2)}) collective-permute-start(bf16[128,1024]{1,0:T(8,128)(2,1)S(1)} %collective-permute-done.11.refs_17_), channel_id=1, source_target_pairs={{0,8},{8,0},{16,24},{24,16},{1,9},{9,1},{17,25},{25,17},{2,10},{10... | collective-permute-start | bytes 786440 | tf_op jit(solution)/shard_map/ppermute | solution.py:185
  37.3 5.1 %collective-permute-start.21 = (bf16[128,512]{1,0:T(8,128)(2,1)S(1)}, bf16[128,512]{1,0:T(8,128)(2,1)}, u32[]{:S(2)}, u32[]{:S(2)}) collective-permute-start(bf16[128,512]{1,0:T(8,128)(2,1)S(1)} %collective-permute-done.18.mine), channel_id=1, source_target_pairs={{0,1},{1,0},{2,3},{3,2},{4,5},{5,4},{6,7},{7,6},{8,9},{9,8},{10,11... | collective-permute-start | bytes 393224 | tf_op jit(solution)/shard_map/ppermute | solution.py:260
  38.9 3.5 %copy-start.2 = (bf16[256,512]{1,0:T(8,128)(2,1)S(1)}, bf16[256,512]{1,0:T(8,128)(2,1)}, u32[]{:S(2)}) copy-start(bf16[256,512]{1,0:T(8,128)(2,1)} %copy-done.1) | copy-start | bytes 786436
  43.4 2.0 %collective-permute-start.22 = (bf16[256,1024]{1,0:T(8,128)(2,1)S(1)}, bf16[256,1024]{1,0:T(8,128)(2,1)S(1)}, u32[]{:S(2)}, u32[]{:S(2)}) collective-permute-start(bf16[256,1024]{1,0:T(8,128)(2,1)S(1)} %merge.1.near), channel_id=1, source_target_pairs={{0,8},{8,0},{16,24},{24,16},{1,9},{9,1},{17,25},{25,17},{2,10},{10... | collective-permute-start | bytes 1572872 | tf_op jit(solution)/shard_map/ppermute | solution.py:185

commit v6 on v5

--- a/solution.py
+++ b/solution.py
@@ -255,7 +255,7 @@
     )(parity, mine, theirs)
     got_b = flip(part, top)
     sum_a = add(*pivot_sums(list_a))
-    sum_a, z, across = lax.optimization_barrier((sum_a, z, across))
+    part, z, across = lax.optimization_barrier((part, z, across))
     got_a = flip(sum_a, top)
     mate_b = lax.ppermute(got_b, "cols", beside)
     pieces, masks = [z, across], [0, top]

time: 48.5 us -> 48.5 us (level)
  no operation moved by 1% of the time
where the time goes in v6:
time: 48.5 us; the launch traced here: 48.2 us
  starting transfers between devices  22.6 us (47%)
  waiting for transfers between devices  12.1 us (25%)
  Pallas kernels  9.62 us (20%)
  local copies, waits for them, and re-layouts  1.99 us (4%)
  other arithmetic  1.78 us (4%)
    ppermute x4, starting transfers between devices, per_device(): fa = lax.ppermute(fa, 'cols', forward)  7.05 us
    ppermute x8, starting transfers between devices, per_device(): lax.ppermute(v, 'rows', [(i, i ^ mask) for i in range(n_rows)])  5.74 us
    ppermute x8, waiting for transfers between devices, per_device(): lax.ppermute(v, 'rows', [(i, i ^ mask) for i in range(n_rows)])  4.39 us
    ppermute x3, starting transfers between devices, per_device(): ba = lax.ppermute(ba, 'cols', backward)  3.1 us
    pallas_call x1, Pallas kernels, per_device(): pl.pallas_call(functools.partial(direct_kernel, n, n_rows), out_shape=[sh...  3.02 us
    ppermute x3, starting transfers between devices, per_device(): fb = lax.ppermute(fb, 'cols', forward)  2.92 us
    pallas_call x1, Pallas kernels, per_device(): pl.pallas_call(final_kernel, out_shape=shape((height, width), f32), in_sp...  2.81 us
    ppermute x4, waiting for transfers between devices, per_device(): bb = lax.ppermute(bb, 'cols', backward)  2.49 us
  transfers between devices with their start and end apart: 23, of which 13 were waited for; matrix products, arithmetic and copies ran while one was open for 6% of the time, Pallas kernels for 10%

profile of v6, /device:TPU:0, one launch (start us, length us, event | category | flops | bytes accessed | tf_op | source)
XLA Modules:
  0.0 48.2 jit_solution(4617793298842304943)
XLA Ops:
  0.0 1.0 %copy-done = f32[128,1024]{1,0:T(8,128)S(1)} copy-done((f32[128,1024]{1,0:T(8,128)S(1)}, f32[128,1024]{1,0:T(8,128)}, u32[]{:S(2)}) %copy-start) | copy-done | bytes 524312
  1.0 0.2 standardize.1
  1.3 3.1 %collective-permute-start = (bf16[128,512]{1,0:T(8,128)(2,1)S(1)}, bf16[128,512]{1,0:T(8,128)(2,1)S(1)}, u32[]{:S(2)}, u32[]{:S(2)}) collective-permute-start(bf16[128,512]{1,0:T(8,128)(2,1)S(1)} %get-tuple-element.53.refs_0_), channel_id=1, source_target_pairs={{0,2},{2,4},{4,6},{6,7},{7,5},{5,3},{3,1},{1,0},{8,10},{10,12},{12... | collective-permute-start | bytes 393224 | tf_op jit(solution)/shard_map/ppermute | solution.py:204
  4.4 0.0 collective-permute-start.1
  4.4 2.0 %collective-permute-start.7 = (bf16[128,512]{1,0:T(8,128)(2,1)S(1)}, bf16[128,512]{1,0:T(8,128)(2,1)S(1)}, u32[]{:S(2)}, u32[]{:S(2)}) collective-permute-start(bf16[128,512]{1,0:T(8,128)(2,1)S(1)} %get-tuple-element.63.refs_0_.refs_8_), channel_id=1, source_target_pairs={{0,2},{2,4},{4,6},{6,7},{7,5},{5,3},{3,1},{1,0},{8,10},{10,12},{12... | collective-permute-start | bytes 393224 | tf_op jit(solution)/shard_map/ppermute | solution.py:209
  6.4 0.0 collective-permute-start.8
  6.4 1.9 %collective-permute-start.11 = (bf16[128,1024]{1,0:T(8,128)(2,1)S(1)}, bf16[128,1024]{1,0:T(8,128)(2,1)S(1)}, u32[]{:S(2)}, u32[]{:S(2)}) collective-permute-start(bf16[128,1024]{1,0:T(8,128)(2,1)S(1)} %get-tuple-element.77.refs_16_), channel_id=1, source_target_pairs={{0,16},{8,24},{16,0},{24,8},{1,17},{9,25},{17,1},{25,9},{2,18},{10... | collective-permute-start | bytes 786440 | tf_op jit(solution)/shard_map/ppermute | solution.py:185
  8.3 0.7 %fusion.1 = (f32[4,8,128]{2,1,0:T(8,128)S(1)}, f32[4096]{0:T(1024)S(1)}) fusion(s32[4096]{0:T(1024)} %param.7), kind=kLoop, calls=%fused_computation.15 | loop fusion | flops 8192 | bytes 49152 | tf_op jit(solution)/shard_map/reshape | solution.py:194
  9.1 0.7 %add_multiply_fusion = (s32[8]{0:T(128)S(1)}, s32[8]{0:T(128)S(1)}) fusion(s32[]{:T(128)S(6)} %mul.22, s32[8]{0:T(128)} %constant.86.clone, s32[]{:T(128)S(6)} %select_n.50), kind=kLoop, calls=%fused_computation.13 | loop fusion | flops 160 | bytes 104 | tf_op jit(solution)/shard_map/mul | solution.py:217
  9.7 0.0 collective-permute-done.refs_1_
  9.7 1.6 %collective-permute-start.2 = (bf16[128,512]{1,0:T(8,128)(2,1)S(1)}, bf16[128,512]{1,0:T(8,128)(2,1)S(1)}, u32[]{:S(2)}, u32[]{:S(2)}) collective-permute-start(bf16[128,512]{1,0:T(8,128)(2,1)S(1)} %collective-permute-done.refs_1_), channel_id=1, source_target_pairs={{0,2},{2,4},{4,6},{6,7},{7,5},{5,3},{3,1},{1,0},{8,10},{10,12},{12... | collective-permute-start | bytes 393224 | tf_op jit(solution)/shard_map/ppermute | solution.py:204
  11.4 0.8 %collective-permute-done.8.refs_2_.refs_10_ = bf16[128,512]{1,0:T(8,128)(2,1)S(1)} collective-permute-done((bf16[128,512]{1,0:T(8,128)(2,1)S(1)}, bf16[128,512]{1,0:T(8,128)(2,1)S(1)}, u32[]{:S(2)}, u32[]{:S(2)}) %collective-permute-start.8) | collective-permute-done | bytes 131104 | tf_op jit(solution)/shard_map/ppermute | solution.py:211
  12.1 0.3 collective-permute-start.10
  12.4 0.1 add_bitcast_fusion
  12.5 0.7 %reshape.33 = s32[2,256]{1,0:T(2,128)S(1)} reshape(s32[512]{0:T(512)} %param.6) | data formatting | bytes 4096 | tf_op jit(solution)/shard_map/reshape | solution.py:222
  13.2 0.0 collective-permute-done.1.refs_2_
  13.2 1.7 %collective-permute-start.3 = (bf16[128,512]{1,0:T(8,128)(2,1)S(1)}, bf16[128,512]{1,0:T(8,128)(2,1)S(1)}, u32[]{:S(2)}, u32[]{:S(2)}) collective-permute-start(bf16[128,512]{1,0:T(8,128)(2,1)S(1)} %collective-permute-done.1.refs_2_), channel_id=1, source_target_pairs={{2,0},{4,2},{6,4},{7,6},{5,7},{3,5},{1,3},{0,1},{10,8},{12,10},{14... | collective-permute-start | bytes 393224 | tf_op jit(solution)/shard_map/ppermute | solution.py:207
  14.9 0.0 collective-permute-done.7.refs_1_.refs_9_
  14.9 0.3 collective-permute-start.9
  15.3 0.0 collective-permute-done.2.refs_3_
  15.3 1.7 %collective-permute-start.4 = (bf16[128,512]{1,0:T(8,128)(2,1)S(1)}, bf16[128,512]{1,0:T(8,128)(2,1)S(1)}, u32[]{:S(2)}, u32[]{:S(2)}) collective-permute-start(bf16[128,512]{1,0:T(8,128)(2,1)S(1)} %collective-permute-done.2.refs_3_), channel_id=1, source_target_pairs={{0,2},{2,4},{4,6},{6,7},{7,5},{5,3},{3,1},{1,0},{8,10},{10,12},{12... | collective-permute-start | bytes 393224 | tf_op jit(solution)/shard_map/ppermute | solution.py:204
  17.0 0.8 %collective-permute-done.10.refs_4_.refs_12_ = bf16[128,512]{1,0:T(8,128)(2,1)S(1)} collective-permute-done((bf16[128,512]{1,0:T(8,128)(2,1)S(1)}, bf16[128,512]{1,0:T(8,128)(2,1)S(1)}, u32[]{:S(2)}, u32[]{:S(2)}) %collective-permute-start.10) | collective-permute-done | bytes 131104 | tf_op jit(solution)/shard_map/ppermute | solution.py:211
  17.9 0.9 %collective-permute-start.13 = (bf16[128,512]{1,0:T(8,128)(2,1)S(1)}, bf16[128,512]{1,0:T(8,128)(2,1)S(1)}, u32[]{:S(2)}, u32[]{:S(2)}) collective-permute-start(bf16[128,512]{1,0:T(8,128)(2,1)S(1)} %collective-permute-done.10.refs_4_.refs_12_), channel_id=1, source_target_pairs={{2,0},{4,2},{6,4},{7,6},{5,7},{3,5},{1,3},{0,1},{10,8},{12,10},{14... | collective-permute-start | bytes 393224 | tf_op jit(solution)/shard_map/ppermute | solution.py:211
  18.8 1.2 %collective-permute-done.9.refs_3_.refs_11_ = bf16[128,512]{1,0:T(8,128)(2,1)S(1)} collective-permute-done((bf16[128,512]{1,0:T(8,128)(2,1)S(1)}, bf16[128,512]{1,0:T(8,128)(2,1)S(1)}, u32[]{:S(2)}, u32[]{:S(2)}) %collective-permute-start.9) | collective-permute-done | bytes 131104 | tf_op jit(solution)/shard_map/ppermute | solution.py:209
  20.0 0.0 collective-permute-done.11.refs_17_
  20.0 0.6 %collective-permute-start.12 = (bf16[128,512]{1,0:T(8,128)(2,1)S(1)}, bf16[128,512]{1,0:T(8,128)(2,1)S(1)}, u32[]{:S(2)}, u32[]{:S(2)}) collective-permute-start(bf16[128,512]{1,0:T(8,128)(2,1)S(1)} %collective-permute-done.9.refs_3_.refs_11_), channel_id=1, source_target_pairs={{0,2},{2,4},{4,6},{6,7},{7,5},{5,3},{3,1},{1,0},{8,10},{10,12},{12... | collective-permute-start | bytes 393224 | tf_op jit(solution)/shard_map/ppermute | solution.py:209
  20.6 0.1 collective-permute-done.3.refs_4_
  20.7 1.3 %collective-permute-start.5 = (bf16[128,512]{1,0:T(8,128)(2,1)S(1)}, bf16[128,512]{1,0:T(8,128)(2,1)S(1)}, u32[]{:S(2)}, u32[]{:S(2)}) collective-permute-start(bf16[128,512]{1,0:T(8,128)(2,1)S(1)} %collective-permute-done.3.refs_4_), channel_id=1, source_target_pairs={{2,0},{4,2},{6,4},{7,6},{5,7},{3,5},{1,3},{0,1},{10,8},{12,10},{14... | collective-permute-start | bytes 393224 | tf_op jit(solution)/shard_map/ppermute | solution.py:207
  22.0 0.8 %collective-permute-done.4.refs_5_ = bf16[128,512]{1,0:T(8,128)(2,1)S(1)} collective-permute-done((bf16[128,512]{1,0:T(8,128)(2,1)S(1)}, bf16[128,512]{1,0:T(8,128)(2,1)S(1)}, u32[]{:S(2)}, u32[]{:S(2)}) %collective-permute-start.4) | collective-permute-done | bytes 131104 | tf_op jit(solution)/shard_map/ppermute | solution.py:204
  22.8 0.6 %collective-permute-start.6 = (bf16[128,512]{1,0:T(8,128)(2,1)S(1)}, bf16[128,512]{1,0:T(8,128)(2,1)S(1)}, u32[]{:S(2)}, u32[]{:S(2)}) collective-permute-start(bf16[128,512]{1,0:T(8,128)(2,1)S(1)} %collective-permute-done.4.refs_5_), channel_id=1, source_target_pairs={{0,2},{2,4},{4,6},{6,7},{7,5},{5,3},{3,1},{1,0},{8,10},{10,12},{12... | collective-permute-start | bytes 393224 | tf_op jit(solution)/shard_map/ppermute | solution.py:204
  23.4 0.1 collective-permute-done.13.refs_6_.refs_14_
  23.5 1.3 %collective-permute-start.14 = (bf16[128,512]{1,0:T(8,128)(2,1)S(1)}, bf16[128,512]{1,0:T(8,128)(2,1)S(1)}, u32[]{:S(2)}, u32[]{:S(2)}) collective-permute-start(bf16[128,512]{1,0:T(8,128)(2,1)S(1)} %collective-permute-done.13.refs_6_.refs_14_), channel_id=1, source_target_pairs={{2,0},{4,2},{6,4},{7,6},{5,7},{3,5},{1,3},{0,1},{10,8},{12,10},{14... | collective-permute-start | bytes 393224 | tf_op jit(solution)/shard_map/ppermute | solution.py:211
  24.8 0.2 compare_convert_fusion.hot_ref
  25.1 1.0 %collective-permute-done.5.refs_6_ = bf16[128,512]{1,0:T(8,128)(2,1)S(1)} collective-permute-done((bf16[128,512]{1,0:T(8,128)(2,1)S(1)}, bf16[128,512]{1,0:T(8,128)(2,1)S(1)}, u32[]{:S(2)}, u32[]{:S(2)}) %collective-permute-start.5) | collective-permute-done | bytes 131104 | tf_op jit(solution)/shard_map/ppermute | solution.py:207
  26.1 0.0 collective-permute-done.12.refs_5_.refs_13_
  26.1 1.6 %collective-permute-done.6.refs_7_ = bf16[128,512]{1,0:T(8,128)(2,1)S(1)} collective-permute-done((bf16[128,512]{1,0:T(8,128)(2,1)S(1)}, bf16[128,512]{1,0:T(8,128)(2,1)S(1)}, u32[]{:S(2)}, u32[]{:S(2)}) %collective-permute-start.6) | collective-permute-done | bytes 131104 | tf_op jit(solution)/shard_map/ppermute | solution.py:204
  27.8 0.7 %collective-permute-done.14.refs_7_.refs_15_ = bf16[128,512]{1,0:T(8,128)(2,1)S(1)} collective-permute-done((bf16[128,512]{1,0:T(8,128)(2,1)S(1)}, bf16[128,512]{1,0:T(8,128)(2,1)S(1)}, u32[]{:S(2)}, u32[]{:S(2)}) %collective-permute-start.14) | collective-permute-done | bytes 131104 | tf_op jit(solution)/shard_map/ppermute | solution.py:211
  28.5 0.7 %select.13 = (bf16[256,512]{1,0:T(8,128)(2,1)S(1)}, bf16[256,512]{1,0:T(8,128)(2,1)S(1)}) custom-call(bf16[512,1024]{1,0:T(8,128)(2,1)S(1)} %compare_convert_fusion.hot_ref, bf16[128,512]{1,0:T(8,128)(2,1)S(1)} %get-tuple-element.63.refs_0_.refs_8_, bf16[128,512]{1,0:T(8,128)(2,1)S(1)} %collective-permute-done.7.refs_1_.refs_9_, ...), custom_call_target="tpu_custom_call" | custom-call | flops 1 | bytes 1 | tf_op jit(solution)/shard_map/select/pallas_call | solution.py:233
  29.2 0.0 copy-start.3
  29.2 0.1 collective-permute-start.17
  29.3 0.7 %select.12 = (bf16[256,512]{1,0:T(8,128)(2,1)S(1)}, bf16[256,512]{1,0:T(8,128)(2,1)S(1)}) custom-call(bf16[512,1024]{1,0:T(8,128)(2,1)S(1)} %compare_convert_fusion.hot_ref, bf16[128,512]{1,0:T(8,128)(2,1)S(1)} %get-tuple-element.53.refs_0_, bf16[128,512]{1,0:T(8,128)(2,1)S(1)} %collective-permute-done.refs_1_, ...), custom_call_target="tpu_custom_call" | custom-call | flops 1 | bytes 1 | tf_op jit(solution)/shard_map/select/pallas_call | solution.py:233
  30.0 0.6 %collective-permute-start.15 = (bf16[256,512]{1,0:T(8,128)(2,1)S(1)}, bf16[256,512]{1,0:T(8,128)(2,1)S(1)}, u32[]{:S(2)}, u32[]{:S(2)}) collective-permute-start(bf16[256,512]{1,0:T(8,128)(2,1)S(1)} %get-tuple-element.62), channel_id=1, source_target_pairs={{0,8},{8,0},{16,24},{24,16},{1,9},{9,1},{17,25},{25,17},{2,10},{10... | collective-permute-start | bytes 786440 | tf_op jit(solution)/shard_map/ppermute | solution.py:185
  30.6 0.3 collective-permute-done.17.right
  30.9 0.0 copy-start.1
  30.9 1.7 %collective-permute-start.18 = (bf16[128,512]{1,0:T(8,128)(2,1)S(1)}, bf16[128,512]{1,0:T(8,128)(2,1)S(1)}, u32[]{:S(2)}, u32[]{:S(2)}) collective-permute-start(bf16[128,512]{1,0:T(8,128)(2,1)S(1)} %get-tuple-element.73), channel_id=1, source_target_pairs={{0,16},{8,24},{16,0},{24,8},{1,17},{9,25},{17,1},{25,9},{2,18},{10... | collective-permute-start | bytes 393224 | tf_op jit(solution)/shard_map/ppermute | solution.py:185
  32.6 0.0 collective-permute-done.15.right
  32.7 0.9 %collective-permute-start.16 = (bf16[256,512]{1,0:T(8,128)(2,1)S(1)}, bf16[256,512]{1,0:T(8,128)(2,1)}, u32[]{:S(2)}, u32[]{:S(2)}) collective-permute-start(bf16[256,512]{1,0:T(8,128)(2,1)S(1)} %add.110.sum_a), channel_id=1, source_target_pairs={{0,16},{8,24},{16,0},{24,8},{1,17},{9,25},{17,1},{25,9},{2,18},{10... | collective-permute-start | bytes 786440 | tf_op jit(solution)/shard_map/ppermute | solution.py:185
  33.5 0.1 collective-permute-start.19
  33.6 0.4 collective-permute-start.20
  34.0 3.3 %collective-permute-done.18.mine = bf16[128,512]{1,0:T(8,128)(2,1)S(1)} collective-permute-done((bf16[128,512]{1,0:T(8,128)(2,1)S(1)}, bf16[128,512]{1,0:T(8,128)(2,1)S(1)}, u32[]{:S(2)}, u32[]{:S(2)}) %collective-permute-start.18) | collective-permute-done | bytes 131104 | tf_op jit(solution)/shard_map/ppermute | solution.py:185
  37.3 1.3 %collective-permute-start.21 = (bf16[128,512]{1,0:T(8,128)(2,1)S(1)}, bf16[128,512]{1,0:T(8,128)(2,1)}, u32[]{:S(2)}, u32[]{:S(2)}) collective-permute-start(bf16[128,512]{1,0:T(8,128)(2,1)S(1)} %collective-permute-done.18.mine), channel_id=1, source_target_pairs={{0,1},{1,0},{2,3},{3,2},{4,5},{5,4},{6,7},{7,6},{8,9},{9,8},{10,11... | collective-permute-start | bytes 393224 | tf_op jit(solution)/shard_map/ppermute | solution.py:260
  38.6 0.1 pad_add_fusion.1.cols_ref
  38.7 0.2 copy.6.kr_ref
  38.9 0.0 copy-start.2
  38.9 0.0 collective-permute-done.19.refs_18_
  38.9 0.0 collective-permute-done.20.refs_19_
  38.9 3.0 %direct.1 = (bf16[1024,1024]{1,0:T(8,128)(2,1)S(1)}, bf16[512,1024]{1,0:T(8,128)(2,1)S(1)}, f32[1024,512]{1,0:T(8,128)S(1)}, f32[1024,512]{1,0:T(8,128)S(1)}) custom-call(s32[12]{0:T(128)S(1)} %pad_add_fusion.1.cols_ref, f32[1024,1]{1,0:T(8,128)S(1)} %copy.6.kr_ref, f32[1,512]{1,0:T(1,128)S(1)} %dynamic-slice_bitcast_fusion.kc_ref, ...), custom_call_target="tpu_custom_call" | custom-call | flops 1 | bytes 1 | tf_op jit(solution)/shard_map/direct/pallas_call | solution.py:272
  42.0 0.4 collective-permute-done.21.mate
  42.4 0.0 collective-permute-done.16.got_a
  42.4 1.0 %merge.1.near = bf16[256,1024]{1,0:T(8,128)(2,1)S(1)} custom-call(s32[1]{0:T(128)} %bitcast.6.side_ref, bf16[256,512]{1,0:T(8,128)(2,1)S(1)} %add.110.sum_a, bf16[256,512]{1,0:T(8,128)(2,1)} %collective-permute-done.16.got_a, bf16[256,512]{1,0:T(8,128)(2,1)S(1)} %copy-done.2, bf16[128,512]{1,0:T(8,128)(2,1)S(1)} %collective-permute-done.18.mine, ...), custom_call_target="tpu_custom_call" | custom-call | flops 1 | bytes 1 | tf_op jit(solution)/shard_map/merge/pallas_call | solution.py:289
  43.4 0.1 collective-permute-start.22
  43.5 1.0 %partial.1 = (f32[1024,256]{1,0:T(8,128)S(1)}, f32[512,256]{1,0:T(8,128)S(1)}) custom-call(bf16[1024,1024]{1,0:T(8,128)(2,1)S(1)} %get-tuple-element.83.zr, bf16[512,1024]{1,0:T(8,128)(2,1)S(1)} %get-tuple-element.84.zc, bf16[256,1024]{1,0:T(8,128)(2,1)S(1)} %merge.1.near), custom_call_target="tpu_custom_call" | custom-call | flops 1 | bytes 1 | tf_op jit(solution)/shard_map/partial/pallas_call | solution.py:299
  44.5 0.9 %collective-permute-done.22.far = bf16[256,1024]{1,0:T(8,128)(2,1)S(1)} collective-permute-done((bf16[256,1024]{1,0:T(8,128)(2,1)S(1)}, bf16[256,1024]{1,0:T(8,128)(2,1)S(1)}, u32[]{:S(2)}, u32[]{:S(2)}) %collective-permute-start.22) | collective-permute-done | bytes 524320 | tf_op jit(solution)/shard_map/ppermute | solution.py:185
  45.4 2.8 %final.1 = f32[1024,512]{1,0:T(8,128)} custom-call(bf16[1024,1024]{1,0:T(8,128)(2,1)S(1)} %get-tuple-element.83.zr, bf16[512,1024]{1,0:T(8,128)(2,1)S(1)} %get-tuple-element.84.zc, bf16[256,1024]{1,0:T(8,128)(2,1)S(1)} %collective-permute-done.22.far, f32[1024,256]{1,0:T(8,128)S(1)} %get-tuple-element.89.row_part, ...), custom_call_target="tpu_custom_call" | custom-call | flops 1 | bytes 1 | tf_op jit(solution)/shard_map/final/pallas_call | solution.py:308
  (11 shorter events, 0.1 us)
Async XLA Ops:
  0.0 1.0 %copy-start = (f32[128,1024]{1,0:T(8,128)S(1)}, f32[128,1024]{1,0:T(8,128)}, u32[]{:S(2)}) copy-start(f32[128,1024]{1,0:T(8,128)} %x_ref.1) | copy-start | bytes 1572868
  1.3 8.4 %collective-permute-start = (bf16[128,512]{1,0:T(8,128)(2,1)S(1)}, bf16[128,512]{1,0:T(8,128)(2,1)S(1)}, u32[]{:S(2)}, u32[]{:S(2)}) collective-permute-start(bf16[128,512]{1,0:T(8,128)(2,1)S(1)} %get-tuple-element.53.refs_0_), channel_id=1, source_target_pairs={{0,2},{2,4},{4,6},{6,7},{7,5},{5,3},{3,1},{1,0},{8,10},{10,12},{12... | collective-permute-start | bytes 393224 | tf_op jit(solution)/shard_map/ppermute | solution.py:204
  4.4 8.8 %collective-permute-start.1 = (bf16[128,512]{1,0:T(8,128)(2,1)S(1)}, bf16[128,512]{1,0:T(8,128)(2,1)S(1)}, u32[]{:S(2)}, u32[]{:S(2)}) collective-permute-start(bf16[128,512]{1,0:T(8,128)(2,1)S(1)} %get-tuple-element.53.refs_0_), channel_id=1, source_target_pairs={{2,0},{4,2},{6,4},{7,6},{5,7},{3,5},{1,3},{0,1},{10,8},{12,10},{14... | collective-permute-start | bytes 393224 | tf_op jit(solution)/shard_map/ppermute | solution.py:207
  4.4 10.6 %collective-permute-start.7 = (bf16[128,512]{1,0:T(8,128)(2,1)S(1)}, bf16[128,512]{1,0:T(8,128)(2,1)S(1)}, u32[]{:S(2)}, u32[]{:S(2)}) collective-permute-start(bf16[128,512]{1,0:T(8,128)(2,1)S(1)} %get-tuple-element.63.refs_0_.refs_8_), channel_id=1, source_target_pairs={{0,2},{2,4},{4,6},{6,7},{7,5},{5,3},{3,1},{1,0},{8,10},{10,12},{12... | collective-permute-start | bytes 393224 | tf_op jit(solution)/shard_map/ppermute | solution.py:209
  6.4 5.8 %collective-permute-start.8 = (bf16[128,512]{1,0:T(8,128)(2,1)S(1)}, bf16[128,512]{1,0:T(8,128)(2,1)S(1)}, u32[]{:S(2)}, u32[]{:S(2)}) collective-permute-start(bf16[128,512]{1,0:T(8,128)(2,1)S(1)} %get-tuple-element.63.refs_0_.refs_8_), channel_id=1, source_target_pairs={{2,0},{4,2},{6,4},{7,6},{5,7},{3,5},{1,3},{0,1},{10,8},{12,10},{14... | collective-permute-start | bytes 393224 | tf_op jit(solution)/shard_map/ppermute | solution.py:211
  6.4 13.6 %collective-permute-start.11 = (bf16[128,1024]{1,0:T(8,128)(2,1)S(1)}, bf16[128,1024]{1,0:T(8,128)(2,1)S(1)}, u32[]{:S(2)}, u32[]{:S(2)}) collective-permute-start(bf16[128,1024]{1,0:T(8,128)(2,1)S(1)} %get-tuple-element.77.refs_16_), channel_id=1, source_target_pairs={{0,16},{8,24},{16,0},{24,8},{1,17},{9,25},{17,1},{25,9},{2,18},{10... | collective-permute-start | bytes 786440 | tf_op jit(solution)/shard_map/ppermute | solution.py:185
  9.7 5.6 %collective-permute-start.2 = (bf16[128,512]{1,0:T(8,128)(2,1)S(1)}, bf16[128,512]{1,0:T(8,128)(2,1)S(1)}, u32[]{:S(2)}, u32[]{:S(2)}) collective-permute-start(bf16[128,512]{1,0:T(8,128)(2,1)S(1)} %collective-permute-done.refs_1_), channel_id=1, source_target_pairs={{0,2},{2,4},{4,6},{6,7},{7,5},{5,3},{3,1},{1,0},{8,10},{10,12},{12... | collective-permute-start | bytes 393224 | tf_op jit(solution)/shard_map/ppermute | solution.py:204
  12.1 5.7 %collective-permute-start.10 = (bf16[128,512]{1,0:T(8,128)(2,1)S(1)}, bf16[128,512]{1,0:T(8,128)(2,1)S(1)}, u32[]{:S(2)}, u32[]{:S(2)}) collective-permute-start(bf16[128,512]{1,0:T(8,128)(2,1)S(1)} %collective-permute-done.8.refs_2_.refs_10_), channel_id=1, source_target_pairs={{2,0},{4,2},{6,4},{7,6},{5,7},{3,5},{1,3},{0,1},{10,8},{12,10},{14... | collective-permute-start | bytes 393224 | tf_op jit(solution)/shard_map/ppermute | solution.py:211
  13.2 7.5 %collective-permute-start.3 = (bf16[128,512]{1,0:T(8,128)(2,1)S(1)}, bf16[128,512]{1,0:T(8,128)(2,1)S(1)}, u32[]{:S(2)}, u32[]{:S(2)}) collective-permute-start(bf16[128,512]{1,0:T(8,128)(2,1)S(1)} %collective-permute-done.1.refs_2_), channel_id=1, source_target_pairs={{2,0},{4,2},{6,4},{7,6},{5,7},{3,5},{1,3},{0,1},{10,8},{12,10},{14... | collective-permute-start | bytes 393224 | tf_op jit(solution)/shard_map/ppermute | solution.py:207
  14.9 5.1 %collective-permute-start.9 = (bf16[128,512]{1,0:T(8,128)(2,1)S(1)}, bf16[128,512]{1,0:T(8,128)(2,1)S(1)}, u32[]{:S(2)}, u32[]{:S(2)}) collective-permute-start(bf16[128,512]{1,0:T(8,128)(2,1)S(1)} %collective-permute-done.7.refs_1_.refs_9_), channel_id=1, source_target_pairs={{0,2},{2,4},{4,6},{6,7},{7,5},{5,3},{3,1},{1,0},{8,10},{10,12},{12... | collective-permute-start | bytes 393224 | tf_op jit(solution)/shard_map/ppermute | solution.py:209
  15.3 7.5 %collective-permute-start.4 = (bf16[128,512]{1,0:T(8,128)(2,1)S(1)}, bf16[128,512]{1,0:T(8,128)(2,1)S(1)}, u32[]{:S(2)}, u32[]{:S(2)}) collective-permute-start(bf16[128,512]{1,0:T(8,128)(2,1)S(1)} %collective-permute-done.2.refs_3_), channel_id=1, source_target_pairs={{0,2},{2,4},{4,6},{6,7},{7,5},{5,3},{3,1},{1,0},{8,10},{10,12},{12... | collective-permute-start | bytes 393224 | tf_op jit(solution)/shard_map/ppermute | solution.py:204
  17.9 5.7 %collective-permute-start.13 = (bf16[128,512]{1,0:T(8,128)(2,1)S(1)}, bf16[128,512]{1,0:T(8,128)(2,1)S(1)}, u32[]{:S(2)}, u32[]{:S(2)}) collective-permute-start(bf16[128,512]{1,0:T(8,128)(2,1)S(1)} %collective-permute-done.10.refs_4_.refs_12_), channel_id=1, source_target_pairs={{2,0},{4,2},{6,4},{7,6},{5,7},{3,5},{1,3},{0,1},{10,8},{12,10},{14... | collective-permute-start | bytes 393224 | tf_op jit(solution)/shard_map/ppermute | solution.py:211
  20.0 6.1 %collective-permute-start.12 = (bf16[128,512]{1,0:T(8,128)(2,1)S(1)}, bf16[128,512]{1,0:T(8,128)(2,1)S(1)}, u32[]{:S(2)}, u32[]{:S(2)}) collective-permute-start(bf16[128,512]{1,0:T(8,128)(2,1)S(1)} %collective-permute-done.9.refs_3_.refs_11_), channel_id=1, source_target_pairs={{0,2},{2,4},{4,6},{6,7},{7,5},{5,3},{3,1},{1,0},{8,10},{10,12},{12... | collective-permute-start | bytes 393224 | tf_op jit(solution)/shard_map/ppermute | solution.py:209
  20.7 5.4 %collective-permute-start.5 = (bf16[128,512]{1,0:T(8,128)(2,1)S(1)}, bf16[128,512]{1,0:T(8,128)(2,1)S(1)}, u32[]{:S(2)}, u32[]{:S(2)}) collective-permute-start(bf16[128,512]{1,0:T(8,128)(2,1)S(1)} %collective-permute-done.3.refs_4_), channel_id=1, source_target_pairs={{2,0},{4,2},{6,4},{7,6},{5,7},{3,5},{1,3},{0,1},{10,8},{12,10},{14... | collective-permute-start | bytes 393224 | tf_op jit(solution)/shard_map/ppermute | solution.py:207
  22.8 5.0 %collective-permute-start.6 = (bf16[128,512]{1,0:T(8,128)(2,1)S(1)}, bf16[128,512]{1,0:T(8,128)(2,1)S(1)}, u32[]{:S(2)}, u32[]{:S(2)}) collective-permute-start(bf16[128,512]{1,0:T(8,128)(2,1)S(1)} %collective-permute-done.4.refs_5_), channel_id=1, source_target_pairs={{0,2},{2,4},{4,6},{6,7},{7,5},{5,3},{3,1},{1,0},{8,10},{10,12},{12... | collective-permute-start | bytes 393224 | tf_op jit(solution)/shard_map/ppermute | solution.py:204
  23.5 5.0 %collective-permute-start.14 = (bf16[128,512]{1,0:T(8,128)(2,1)S(1)}, bf16[128,512]{1,0:T(8,128)(2,1)S(1)}, u32[]{:S(2)}, u32[]{:S(2)}) collective-permute-start(bf16[128,512]{1,0:T(8,128)(2,1)S(1)} %collective-permute-done.13.refs_6_.refs_14_), channel_id=1, source_target_pairs={{2,0},{4,2},{6,4},{7,6},{5,7},{3,5},{1,3},{0,1},{10,8},{12,10},{14... | collective-permute-start | bytes 393224 | tf_op jit(solution)/shard_map/ppermute | solution.py:211
  29.2 9.4 %copy-start.3 = (s32[4]{0:T(128)S(1)}, s32[4]{0:T(128)}, u32[]{:S(2)}) copy-start(s32[4]{0:T(128)} %constant.87.clone) | copy-start | bytes 52
  29.2 1.6 %collective-permute-start.17 = (bf16[256,512]{1,0:T(8,128)(2,1)S(1)}, bf16[256,512]{1,0:T(8,128)(2,1)S(1)}, u32[]{:S(2)}, u32[]{:S(2)}) collective-permute-start(bf16[256,512]{1,0:T(8,128)(2,1)S(1)} %get-tuple-element.72), channel_id=1, source_target_pairs={{0,8},{8,0},{16,24},{24,16},{1,9},{9,1},{17,25},{25,17},{2,10},{10... | collective-permute-start | bytes 786440 | tf_op jit(solution)/shard_map/ppermute | solution.py:185
  30.0 2.6 %collective-permute-start.15 = (bf16[256,512]{1,0:T(8,128)(2,1)S(1)}, bf16[256,512]{1,0:T(8,128)(2,1)S(1)}, u32[]{:S(2)}, u32[]{:S(2)}) collective-permute-start(bf16[256,512]{1,0:T(8,128)(2,1)S(1)} %get-tuple-element.62), channel_id=1, source_target_pairs={{0,8},{8,0},{16,24},{24,16},{1,9},{9,1},{17,25},{25,17},{2,10},{10... | collective-permute-start | bytes 786440 | tf_op jit(solution)/shard_map/ppermute | solution.py:185
  30.9 2.7 %copy-start.1 = (bf16[256,512]{1,0:T(8,128)(2,1)}, bf16[256,512]{1,0:T(8,128)(2,1)S(1)}, u32[]{:S(2)}) copy-start(bf16[256,512]{1,0:T(8,128)(2,1)S(1)} %get-tuple-element.86.sum_b) | copy-start | bytes 786436
  30.9 6.4 %collective-permute-start.18 = (bf16[128,512]{1,0:T(8,128)(2,1)S(1)}, bf16[128,512]{1,0:T(8,128)(2,1)S(1)}, u32[]{:S(2)}, u32[]{:S(2)}) collective-permute-start(bf16[128,512]{1,0:T(8,128)(2,1)S(1)} %get-tuple-element.73), channel_id=1, source_target_pairs={{0,16},{8,24},{16,0},{24,8},{1,17},{9,25},{17,1},{25,9},{2,18},{10... | collective-permute-start | bytes 393224 | tf_op jit(solution)/shard_map/ppermute | solution.py:185
  32.7 9.7 %collective-permute-start.16 = (bf16[256,512]{1,0:T(8,128)(2,1)S(1)}, bf16[256,512]{1,0:T(8,128)(2,1)}, u32[]{:S(2)}, u32[]{:S(2)}) collective-permute-start(bf16[256,512]{1,0:T(8,128)(2,1)S(1)} %add.110.sum_a), channel_id=1, source_target_pairs={{0,16},{8,24},{16,0},{24,8},{1,17},{9,25},{17,1},{25,9},{2,18},{10... | collective-permute-start | bytes 786440 | tf_op jit(solution)/shard_map/ppermute | solution.py:185
  33.5 5.4 %collective-permute-start.19 = (bf16[128,1024]{1,0:T(8,128)(2,1)S(1)}, bf16[128,1024]{1,0:T(8,128)(2,1)}, u32[]{:S(2)}, u32[]{:S(2)}) collective-permute-start(bf16[128,1024]{1,0:T(8,128)(2,1)S(1)} %get-tuple-element.77.refs_16_), channel_id=1, source_target_pairs={{0,8},{8,0},{16,24},{24,16},{1,9},{9,1},{17,25},{25,17},{2,10},{10... | collective-permute-start | bytes 786440 | tf_op jit(solution)/shard_map/ppermute | solution.py:185
  33.6 5.3 %collective-permute-start.20 = (bf16[128,1024]{1,0:T(8,128)(2,1)S(1)}, bf16[128,1024]{1,0:T(8,128)(2,1)}, u32[]{:S(2)}, u32[]{:S(2)}) collective-permute-start(bf16[128,1024]{1,0:T(8,128)(2,1)S(1)} %collective-permute-done.11.refs_17_), channel_id=1, source_target_pairs={{0,8},{8,0},{16,24},{24,16},{1,9},{9,1},{17,25},{25,17},{2,10},{10... | collective-permute-start | bytes 786440 | tf_op jit(solution)/shard_map/ppermute | solution.py:185
  37.3 5.1 %collective-permute-start.21 = (bf16[128,512]{1,0:T(8,128)(2,1)S(1)}, bf16[128,512]{1,0:T(8,128)(2,1)}, u32[]{:S(2)}, u32[]{:S(2)}) collective-permute-start(bf16[128,512]{1,0:T(8,128)(2,1)S(1)} %collective-permute-done.18.mine), channel_id=1, source_target_pairs={{0,1},{1,0},{2,3},{3,2},{4,5},{5,4},{6,7},{7,6},{8,9},{9,8},{10,11... | collective-permute-start | bytes 393224 | tf_op jit(solution)/shard_map/ppermute | solution.py:260
  38.9 3.5 %copy-start.2 = (bf16[256,512]{1,0:T(8,128)(2,1)S(1)}, bf16[256,512]{1,0:T(8,128)(2,1)}, u32[]{:S(2)}) copy-start(bf16[256,512]{1,0:T(8,128)(2,1)} %copy-done.1) | copy-start | bytes 786436
  43.4 2.0 %collective-permute-start.22 = (bf16[256,1024]{1,0:T(8,128)(2,1)S(1)}, bf16[256,1024]{1,0:T(8,128)(2,1)S(1)}, u32[]{:S(2)}, u32[]{:S(2)}) collective-permute-start(bf16[256,1024]{1,0:T(8,128)(2,1)S(1)} %merge.1.near), channel_id=1, source_target_pairs={{0,8},{8,0},{16,24},{24,16},{1,9},{9,1},{17,25},{25,17},{2,10},{10... | collective-permute-start | bytes 1572872 | tf_op jit(solution)/shard_map/ppermute | solution.py:185
